TPU v7x, 768 devices: a whole 4x8x12 slice. The times are simulated.
768 devices in a mesh: aa: 12 (over z_lo, core), ba: 64 (over z_hi, y, x).
Axes of the slice: x: 4, y: 8, z: 12 (z_hi: 2, z_lo: 6; z = z_hi * 6 + z_lo), core: 2. Of those that a mesh axis runs over, the one named last changes fastest.
Arguments:
- activations: bfloat16 [3072, 4224], P('aa', 'ba'), may hold values from -16 to 16
- out_grad: bfloat16 [3072, 4096], P('aa', 'ba'), may hold values from -0.107910156 to 0.107910156
- momentum: float32 [4224, 4096], P('aa', 'ba'), may hold values from -6 to 6
- weight: float32 [4224, 4096], P('aa', 'ba'), may hold values from -6 to 6
- norm_scale: float32 [], replicated, may hold values from 128.99231 to 257.98462
- step_size: float32 [], replicated, may hold values from 0.5 to 2
Outputs:
- new_weight: float32 [4224, 4096], P('aa', 'ba')
- new_momentum: float32 [4224, 4096], P('aa', 'ba')
All inputs are finite; a program needn't handle non-finite values.
Results may differ from a plain program's by a relative error of at most 0.00068.
Values may be sent and summed in bfloat16 or wider, within the bound.
No kernel may reach another device: no remote copies, remote signals or barrier semaphores. Data moves between devices by JAX's collectives and lax.ppermute only.
A program may use at most 32 MiB of HBM per device.

v0:
```python
import math

import jax
import jax.numpy as jnp
from jax import lax
from jax.sharding import Mesh
from jax.sharding import PartitionSpec as P

ROWS = 4224
COLS = 4096
BA = ("ba_0", "ba_1", "ba_2")


def cut_along(shard, dim, size):
    before, after = (shard.shape[:dim], shard.shape[dim + 1 :])
    return jnp.moveaxis(shard.reshape(*before, size, -1, *after), dim, 0)


def sum_at_owner(shard, axis, dim):
    pieces = cut_along(shard, dim, lax.axis_size(axis))
    arrived = lax.all_to_all(pieces, axis, split_axis=0, concat_axis=0, tiled=True)
    return arrived.sum(axis=0)


def laid_out(pieces, dim):
    dims = list(pieces.shape[1:])
    dims[dim] *= pieces.shape[0]
    return jnp.moveaxis(pieces, 0, dim).reshape(dims)


def all_blocks(shard, axes, order):
    pieces = shard[None]
    for k in order:
        pieces = lax.all_gather(pieces, axes[k], axis=0, tiled=True)
    held = [lax.axis_size(axes[k]) for k in reversed(order)]
    pieces = pieces.reshape(*held, *shard.shape)
    turned = sorted(range(len(order)), key=lambda place: order[len(order) - 1 - place])
    return pieces.transpose(*turned, *range(len(order), pieces.ndim)).reshape(-1, *shard.shape)


def gathered_by_axis(shard, axes, order, dim):
    return laid_out(all_blocks(shard, axes, order), dim)


def inner_rows(left, right):
    return lax.dot_general(
        left, right, (((0,), (0,)), ((), ())), preferred_element_type=jnp.float32
    )


def per_device(activations, out_grad, momentum, weight, norm_scale, step_size):
    partial_term = inner_rows(lax.all_gather(activations, BA, axis=1, tiled=True), out_grad)
    gradient = sum_at_owner(partial_term, "aa", 0)
    new_momentum = 0.95 * momentum + gradient
    scaled = (new_momentum / norm_scale).astype(jnp.bfloat16)
    row_panel = gathered_by_axis(scaled, BA, (0, 1, 2), 1)
    gram_part = inner_rows(row_panel, scaled)
    width = gram_part.shape[0]
    groups = lax.axis_size("aa")
    padding = (groups - width % groups) % groups
    padded = jnp.pad(gram_part, ((0, padding), (0, 0)))
    share = sum_at_owner(padded, "aa", 0).astype(jnp.bfloat16)
    gram_cols = lax.all_gather(share, "aa", axis=0, tiled=True)[:width]
    first_power = jnp.dot(row_panel, gram_cols, preferred_element_type=jnp.float32).astype(
        jnp.bfloat16
    )
    second_power = jnp.dot(
        gathered_by_axis(first_power, BA, (0, 1, 2), 1),
        gram_cols,
        preferred_element_type=jnp.float32,
    )
    direction = (
        3.4445 * scaled.astype(jnp.float32)
        - 4.775 * first_power.astype(jnp.float32)
        + 2.0315 * second_power
    )
    factor = 0.2 * math.sqrt(max(ROWS, COLS))
    new_weight = weight - step_size * factor * direction
    return (new_weight, new_momentum)


def solution(mesh):
    torus = Mesh(mesh.devices.reshape(mesh.shape["aa"], 2, 8, 4), ("aa", "ba_0", "ba_1", "ba_2"))
    in_specs = (P("aa", BA), P("aa", BA), P("aa", BA), P("aa", BA), P(), P())
    out_specs = (P("aa", BA), P("aa", BA))
    return jax.shard_map(
        per_device, mesh=torus, in_specs=in_specs, out_specs=out_specs, check_vma=False
    )
```

profile of v0, /device:TPU:1, one launch (start us, length us, event | category | flops | bytes accessed | tf_op | source)
XLA Modules:
  0.0 502.6 jit_solution(4992839117486105059)
XLA Ops:
  7.9 171.8 %all-gather.14.cloned.1.call-done = bf16[64,66,256]{2,1,0:T(8,128)(2,1)} async-done(((bf16[1,66,256]{2,1,0:T(8,128)(2,1)}), bf16[64,66,256]{2,1,0:T(8,128)(2,1)}) %all-gather.14.cloned.1.call-update) | async-done | bytes 2162704 | tf_op jit(solution)/shard_map/all_gather | solution.py:52
  179.7 2.7 reshape.39
  184.1 1.4 copy.16
  185.5 7.9 %all-to-all-start = ((f32[12,352,64]{1,2,0:T(8,128)}), f32[12,352,64]{1,2,0:T(8,128)S(1)}, u32[]{:S(2)}, u32[]{:S(2)}) async-start(f32[12,352,64]{1,2,0:T(8,128)} %copy.16), calls=%async_computation | async-start | bytes 2359296 | tf_op jit(solution)/shard_map/all_to_all | solution.py:21
  194.1 41.5 %all-to-all-done = f32[12,352,64]{1,2,0:T(8,128)S(1)} async-done(((f32[12,352,64]{1,2,0:T(8,128)}), f32[12,352,64]{1,2,0:T(8,128)S(1)}, u32[]{:S(2)}, u32[]{:S(2)}) %all-to-all-start) | async-done | bytes 1081376 | tf_op jit(solution)/shard_map/all_to_all | solution.py:21
  236.3 10.0 %all-gather.3 = bf16[2,352,64]{1,2,0:T(8,128)(2,1)S(1)} all-gather(bf16[1,352,64]{1,2,0:T(8,128)(2,1)S(1)} %bitcast.41), channel_id=2, replica_groups=mesh['aa'=12,'ba_0'=2,'ba_1'=8,'ba_2'=4] {'ba_0'}, dimensions={0}, use_global_device_ids=true | all-gather | bytes 135168 | tf_op jit(solution)/shard_map/all_gather | solution.py:34
  246.3 22.9 %all_gather.26 = bf16[16,352,64]{1,2,0:T(8,128)(2,1)} all-gather(bf16[2,352,64]{1,2,0:T(8,128)(2,1)S(1)} %all-gather.3), channel_id=1, replica_groups=mesh['aa'=12,'ba_0'=2,'ba_1'=8,'ba_2'=4] {'ba_1'}, dimensions={0}, use_global_device_ids=true | all-gather | bytes 811008 | tf_op jit(solution)/shard_map/all_gather | solution.py:34
  269.3 50.1 %all-gather.10.cloned.1.call-done = bf16[64,352,64]{1,2,0:T(8,128)(2,1)} async-done(((bf16[16,352,64]{1,2,0:T(8,128)(2,1)}), bf16[64,352,64]{1,2,0:T(8,128)(2,1)}) %all-gather.10.cloned.1.call-update) | async-done | bytes 2883600 | tf_op jit(solution)/shard_map/all_gather | solution.py:34
  319.4 2.3 copy.17
  321.7 1.1 fusion.6
  322.8 1.1 pad.4
  323.9 3.2 reshape.32
  327.1 1.8 copy.18
  328.9 50.8 %all_to_all.10 = f32[12,342,64]{1,2,0:T(8,128)} all-to-all(f32[12,342,64]{1,2,0:T(8,128)S(1)} %copy.18), channel_id=1, replica_groups=mesh['aa'=12,'ba_0'=2,'ba_1'=8,'ba_2'=4] {'aa'}, dimensions={0} | all-to-all | bytes 2101248 | tf_op jit(solution)/shard_map/all_to_all | solution.py:21
  379.7 1.3 reduce_sum.19
  381.0 23.2 %all-gather.4 = bf16[12,342,64]{1,2,0:T(8,128)(2,1)S(1)} all-gather(bf16[1,342,64]{1,2,0:T(8,128)(2,1)S(1)} %bitcast.43), channel_id=1, replica_groups=mesh['aa'=12,'ba_0'=2,'ba_1'=8,'ba_2'=4] {'aa'}, dimensions={0}, use_global_device_ids=true | all-gather | bytes 569088 | tf_op jit(solution)/shard_map/all_gather | solution.py:63
  404.2 1.2 copy.19
  405.4 2.4 reshape.43
  407.8 1.6 convolution_convert_fusion
  409.4 10.0 %all-gather.5 = bf16[2,352,64]{1,2,0:T(8,128)(2,1)S(1)} all-gather(bf16[1,352,64]{1,2,0:T(8,128)(2,1)S(1)} %bitcast.42), channel_id=3, replica_groups=mesh['aa'=12,'ba_0'=2,'ba_1'=8,'ba_2'=4] {'ba_0'}, dimensions={0}, use_global_device_ids=true | all-gather | bytes 135168 | tf_op jit(solution)/shard_map/all_gather | solution.py:34
  419.4 23.5 %all_gather.30 = bf16[16,352,64]{1,2,0:T(8,128)(2,1)} all-gather(bf16[2,352,64]{1,2,0:T(8,128)(2,1)S(1)} %all-gather.5), channel_id=1, replica_groups=mesh['aa'=12,'ba_0'=2,'ba_1'=8,'ba_2'=4] {'ba_1'}, dimensions={0}, use_global_device_ids=true | all-gather | bytes 811008 | tf_op jit(solution)/shard_map/all_gather | solution.py:34
  443.6 48.7 %all-gather.12.cloned.1.call-done = bf16[64,352,64]{1,2,0:T(8,128)(2,1)} async-done(((bf16[16,352,64]{1,2,0:T(8,128)(2,1)}), bf16[64,352,64]{1,2,0:T(8,128)(2,1)}) %all-gather.12.cloned.1.call-update) | async-done | bytes 2883600 | tf_op jit(solution)/shard_map/all_gather | solution.py:34
  492.4 2.4 copy.20
  494.8 1.3 fusion.2
  (18 shorter events, 3.2 us)
Async XLA Ops:
  7.2 175.2 %copy-start = (bf16[256,64]{0,1:T(8,128)(2,1)S(1)}, bf16[256,64]{0,1:T(8,128)(2,1)}, u32[]{:S(2)}) copy-start(bf16[256,64]{0,1:T(8,128)(2,1)} %param.7) | copy-start | bytes 98308
  7.2 172.5 %all-gather.14.cloned.1.call-start = ((), (), s32[]{:S(2)}) async-start(), calls=%async_computation.4 | async-start | bytes 2396160 | tf_op jit(solution)/shard_map/all_gather | solution.py:52
  185.5 50.1 %copy-start.2 = (f32[352,64]{0,1:T(8,128)S(1)}, f32[352,64]{0,1:T(8,128)}, u32[]{:S(2)}) copy-start(f32[352,64]{0,1:T(8,128)} %param.8) | copy-start | bytes 270340
  185.5 50.1 %all-to-all-start = ((f32[12,352,64]{1,2,0:T(8,128)}), f32[12,352,64]{1,2,0:T(8,128)S(1)}, u32[]{:S(2)}, u32[]{:S(2)}) async-start(f32[12,352,64]{1,2,0:T(8,128)} %copy.16), calls=%async_computation | async-start | bytes 2359296 | tf_op jit(solution)/shard_map/all_to_all | solution.py:21
  193.4 126.0 %all-gather.10.cloned.1.call-start = ((), (), s32[]{:S(2)}) async-start(), calls=%async_computation.2 | async-start | bytes 3932160 | tf_op jit(solution)/shard_map/all_gather | solution.py:34
  269.2 223.1 %all-gather.12.cloned.1.call-start = ((), (), s32[]{:S(2)}) async-start(), calls=%async_computation.3 | async-start | bytes 3932160 | tf_op jit(solution)/shard_map/all_gather | solution.py:34
  492.3 2.4 copy-start.1
  492.4 2.4 copy-start.3
Sparse Core Ops, SparseCore 0:
  13.4 166.3 all-gather.13
  269.3 50.0 all-gather.9
  443.1 49.1 all-gather.11
where the time goes:
time: 503 us
  waiting for transfers between devices  313 us (62%)
  blocking collectives  140 us (28%)
  local copies, waits for them, and re-layouts  19.4 us (4%)
  between operations  15.1 us (3%)
  starting transfers between devices  8 us (2%)
    all_gather x1, waiting for transfers between devices, per_device(): lax.all_gather(activations, BA, axis=1, tiled=True)  172 us
    all_gather x2, waiting for transfers between devices, all_blocks(): pieces = lax.all_gather(pieces, axes[k], axis=0, tiled=True)  98.8 us
    all_gather x4, blocking collectives, all_blocks(): pieces = lax.all_gather(pieces, axes[k], axis=0, tiled=True)  66.4 us
    all_to_all x1, blocking collectives, sum_at_owner(): lax.all_to_all(pieces, axis, split_axis=0, concat_axis=0, tiled=True)  50.8 us
    all_to_all x1, waiting for transfers between devices, sum_at_owner(): lax.all_to_all(pieces, axis, split_axis=0, concat_axis=0, tiled=True)  41.5 us
    all_gather x1, blocking collectives, per_device(): gram_cols = lax.all_gather(share, 'aa', axis=0, tiled=True)[:width]  23.2 us
  transfers between devices with their start and end apart: 4, of which 4 were waited for; matrix products, arithmetic and copies ran while one was open for 0% of the time, Pallas kernels for 0%

commit v1 on v0

v1 whole, which is shorter than its diff:
```python
import math

import jax
import jax.numpy as jnp
from jax import lax
from jax.sharding import Mesh
from jax.sharding import PartitionSpec as P

ROWS = 4224
COLS = 4096
ZL, CORES, ZH, Y, X = 6, 2, 2, 8, 4
COLUMN = ("zl", "core", "zh")
SWAP = [(0, 1), (1, 0)]


def place(zl, core, zh):
    return (zl * CORES + core) * ZH + zh


TO_WORK = [
    (place(3 * zh + zl // 2, zl % 2, core), place(zl, core, zh))
    for zl in range(ZL)
    for core in range(CORES)
    for zh in range(ZH)
]
TO_HOME = [(work, home) for home, work in TO_WORK]


def contract(left, right, dims):
    return lax.dot_general(left, right, (dims, ((), ())), preferred_element_type=jnp.float32)


def exchanged(pieces, axes):
    return lax.all_to_all(pieces, axes, split_axis=0, concat_axis=0, tiled=True)


def from_all(shard, axes, size):
    return exchanged(jnp.broadcast_to(shard[None], (size, *shard.shape)), axes)


def over_plane(tile):
    rows, width = tile.shape
    by_y = from_all(tile, "y", Y).reshape(Y * rows, width)
    return from_all(by_y, "x", X).reshape(X * Y * rows, width)


def per_device(activations, out_grad, momentum, weight, norm_scale, step_size):
    own_half = lax.axis_index("core") == lax.axis_index("zh")
    act, grad_out = activations.T, out_grad.T
    features, tokens = act.shape
    peer_out = lax.ppermute(grad_out, "zh", SWAP)
    kept = lax.ppermute(momentum.T, COLUMN, TO_WORK)

    act = over_plane(act).reshape(X, Y, features, tokens)
    act = act.transpose(1, 0, 2, 3).reshape(ZL, -1, tokens)
    mine = jnp.where(own_half, grad_out, peer_out)
    other = jnp.where(own_half, peer_out, grad_out)
    leaving = jnp.stack([contract(other, act[k], ((1,), (1,))) for k in range(ZL)])
    came = lax.ppermute(leaving, "core", SWAP)
    staying = jnp.stack([contract(mine, act[k], ((1,), (1,))) for k in range(ZL)])
    gradient = exchanged(staying + came, "zl").sum(axis=0)

    new_momentum = 0.95 * kept + gradient
    scaled = (new_momentum / norm_scale).astype(jnp.bfloat16)
    momentum_home = lax.ppermute(new_momentum, COLUMN, TO_HOME).T

    width = scaled.shape[0]
    pair = jnp.concatenate([scaled, lax.ppermute(scaled, "core", SWAP)])
    panel = over_plane(scaled)
    depth = panel.shape[0]
    share = -(-depth // (ZL * ZH * 16)) * 16
    part = contract(panel, pair, ((1,), (1,)))
    part = jnp.pad(part, ((0, ZL * ZH * share - depth), (0, 0)))
    part = part.reshape(ZL * ZH, share, 2 * width)
    gram = exchanged(part, ("zh", "zl")).sum(axis=0).astype(jnp.bfloat16)
    gram = from_all(gram, ("zh", "zl"), ZL * ZH).reshape(-1, 2 * width)[:depth]

    def times_gram(rows):
        both = contract(gram, rows, ((0,), (0,)))
        return both[:width] + lax.ppermute(both[width:], "core", SWAP)

    first_power = times_gram(panel).astype(jnp.bfloat16)
    second_power = times_gram(over_plane(first_power))
    direction = (
        3.4445 * scaled.astype(jnp.float32)
        - 4.775 * first_power.astype(jnp.float32)
        + 2.0315 * second_power
    )
    direction = lax.ppermute(direction, COLUMN, TO_HOME).T
    factor = 0.2 * math.sqrt(max(ROWS, COLS))
    return (weight - step_size * factor * direction, momentum_home)


def solution(mesh):
    torus = Mesh(
        mesh.devices.reshape(ZL, CORES, ZH, Y, X), ("zl", "core", "zh", "y", "x")
    )
    tiles = P(("zl", "core"), ("zh", "y", "x"))
    return jax.shard_map(
        per_device,
        mesh=torus,
        in_specs=(tiles, tiles, tiles, tiles, P(), P()),
        out_specs=(tiles, tiles),
        check_vma=False,
    )
```

time: 503 us -> 283 us (0.56)
  the two profiles are of different devices: /device:TPU:1 before, /device:TPU:192 now
where the time goes in v1:
time: 283 us; the launch traced here: 282 us
  blocking collectives  155 us (55%)
  waiting for transfers between devices  61.1 us (22%)
  starting transfers between devices  50.1 us (18%)
  local copies, waits for them, and re-layouts  7.55 us (3%)
  matrix products  4.08 us (1%)
    all_to_all x6, blocking collectives, exchanged(): return lax.all_to_all(pieces, axes, split_axis=0, concat_axis=0, tiled=True)  155 us
    all_to_all x3, waiting for transfers between devices, exchanged(): return lax.all_to_all(pieces, axes, split_axis=0, concat_axis=0, tiled=True)  33.9 us
    ppermute x1, waiting for transfers between devices, per_device(): momentum_home = lax.ppermute(new_momentum, COLUMN, TO_HOME).T  22 us
    all_to_all x3, starting transfers between devices, exchanged(): return lax.all_to_all(pieces, axes, split_axis=0, concat_axis=0, tiled=True)  17 us
    ppermute x1, starting transfers between devices, per_device(): peer_out = lax.ppermute(grad_out, 'zh', SWAP)  12.4 us
    ppermute x1, starting transfers between devices, per_device(): kept = lax.ppermute(momentum.T, COLUMN, TO_WORK)  6.17 us
  transfers between devices with their start and end apart: 11, of which 7 were waited for; matrix products, arithmetic and copies ran while one was open for 1% of the time, Pallas kernels for 0%

profile of v1, /device:TPU:192, one launch (start us, length us, event | category | flops | bytes accessed | tf_op | source)
XLA Modules:
  0.0 282.0 jit_solution(14411481541855030756)
XLA Ops:
  1.4 19.5 %all_to_all.45 = bf16[8,66,256]{2,1,0:T(8,128)(2,1)S(1)} all-to-all(bf16[8,66,256]{2,1,0:T(8,128)(2,1)S(1)} %broadcast_in_dim.20), channel_id=1, replica_groups=mesh['zl'=6,'core'=2,'zh'=2,'y'=8,'x'=4] {'y'}, dimensions={0} | all-to-all | bytes 540672 | tf_op jit(solution)/shard_map/all_to_all | solution.py:34
  22.0 4.4 %all-to-all-start.1 = ((bf16[4,528,256]{2,1,0:T(8,128)(2,1)}), bf16[4,528,256]{2,1,0:T(8,128)(2,1)S(1)}, u32[]{:S(2)}, u32[]{:S(2)}) async-start(bf16[4,528,256]{2,1,0:T(8,128)(2,1)} %broadcast_in_dim.22), calls=%async_computation.1 | async-start | bytes 2162688 | tf_op jit(solution)/shard_map/all_to_all | solution.py:34
  26.5 12.4 %collective-permute-start.1 = (bf16[64,256]{1,0:T(8,128)(2,1)S(1)}, bf16[64,256]{1,0:T(8,128)(2,1)S(1)}, u32[]{:S(2)}, u32[]{:S(2)}) collective-permute-start(bf16[64,256]{1,0:T(8,128)(2,1)S(1)} %bitcast.120), channel_id=1, source_target_pairs={{0,32},{32,0},{1,33},{33,1},{2,34},{34,2},{3,35},{35,3},{4,36},{36... | collective-permute-start | bytes 98312 | tf_op jit(solution)/shard_map/ppermute | solution.py:51
  38.9 1.9 collective-permute-done.1
  43.1 1.9 collective-permute-start.2
  47.9 9.0 %all-to-all-start.2 = ((f32[6,64,352]{2,1,0:T(8,128)}), f32[6,64,352]{2,1,0:T(8,128)S(1)}, u32[]{:S(2)}, u32[]{:S(2)}) async-start(f32[6,64,352]{2,1,0:T(8,128)} %add.17), calls=%async_computation.2 | async-start | bytes 1179648 | tf_op jit(solution)/shard_map/all_to_all | solution.py:34
  57.0 6.2 %collective-permute-start = (f32[64,352]{0,1:T(8,128)S(1)}, f32[64,352]{0,1:T(8,128)S(1)}, u32[]{:S(2)}, u32[]{:S(2)}) collective-permute-start(f32[64,352]{0,1:T(8,128)S(1)} %bitcast.118), channel_id=1, source_target_pairs={{0,0},{384,32},{32,64},{416,96},{64,128},{448,160},{96,192},{480,2... | collective-permute-start | bytes 270344 | tf_op jit(solution)/shard_map/ppermute | solution.py:52
  63.8 19.8 %all-to-all-done.2 = f32[6,64,352]{2,1,0:T(8,128)S(1)} async-done(((f32[6,64,352]{2,1,0:T(8,128)}), f32[6,64,352]{2,1,0:T(8,128)S(1)}, u32[]{:S(2)}, u32[]{:S(2)}) %all-to-all-start.2) | async-done | bytes 540704 | tf_op jit(solution)/shard_map/all_to_all | solution.py:34
  84.7 16.2 %all_to_all.46 = bf16[8,64,352]{2,1,0:T(8,128)(2,1)S(1)} all-to-all(bf16[8,64,352]{2,1,0:T(8,128)(2,1)S(1)} %broadcast_in_dim.23), channel_id=1, replica_groups=mesh['zl'=6,'core'=2,'zh'=2,'y'=8,'x'=4] {'y'}, dimensions={0} | all-to-all | bytes 720896 | tf_op jit(solution)/shard_map/all_to_all | solution.py:34
  101.1 1.2 broadcast_in_dim.50
  102.3 3.5 %all-to-all-start.4 = ((bf16[4,512,352]{1,2,0:T(8,128)(2,1)}), bf16[4,512,352]{1,2,0:T(8,128)(2,1)S(1)}, u32[]{:S(2)}, u32[]{:S(2)}) async-start(bf16[4,512,352]{1,2,0:T(8,128)(2,1)} %broadcast_in_dim.50), calls=%async_computation.4 | async-start | bytes 2883584 | tf_op jit(solution)/shard_map/all_to_all | solution.py:34
  105.8 1.9 collective-permute-start.3
  107.8 14.1 %all-to-all-done.4 = bf16[4,512,352]{1,2,0:T(8,128)(2,1)S(1)} async-done(((bf16[4,512,352]{1,2,0:T(8,128)(2,1)}), bf16[4,512,352]{1,2,0:T(8,128)(2,1)S(1)}, u32[]{:S(2)}, u32[]{:S(2)}) %all-to-all-start.4) | async-done | bytes 1441824 | tf_op jit(solution)/shard_map/all_to_all | solution.py:34
  122.8 53.1 %all_to_all.47 = f32[12,176,128]{2,1,0:T(8,128)S(1)} all-to-all(f32[12,176,128]{2,1,0:T(8,128)S(1)} %bitcast.110), channel_id=1, replica_groups=mesh['zl'=6,'core'=2,'zh'=2,'y'=8,'x'=4] {'zh','zl'}, dimensions={0} | all-to-all | bytes 2162688 | tf_op jit(solution)/shard_map/all_to_all | solution.py:34
  176.0 27.6 %all_to_all.48 = bf16[12,176,128]{2,1,0:T(8,128)(2,1)S(1)} all-to-all(bf16[12,176,128]{2,1,0:T(8,128)(2,1)S(1)} %broadcast_in_dim.51), channel_id=1, replica_groups=mesh['zl'=6,'core'=2,'zh'=2,'y'=8,'x'=4] {'zh','zl'}, dimensions={0} | all-to-all | bytes 1081344 | tf_op jit(solution)/shard_map/all_to_all | solution.py:34
  204.3 1.9 collective-permute-start.4
  206.2 1.4 collective-permute-done.4
  207.7 17.7 %all_to_all.49 = bf16[8,64,352]{2,1,0:T(8,128)(2,1)S(1)} all-to-all(bf16[8,64,352]{2,1,0:T(8,128)(2,1)S(1)} %broadcast_in_dim.52), channel_id=1, replica_groups=mesh['zl'=6,'core'=2,'zh'=2,'y'=8,'x'=4] {'y'}, dimensions={0} | all-to-all | bytes 720896 | tf_op jit(solution)/shard_map/all_to_all | solution.py:34
  225.8 20.9 %all_to_all.50 = bf16[4,512,352]{1,2,0:T(8,128)(2,1)S(1)} all-to-all(bf16[4,512,352]{1,2,0:T(8,128)(2,1)S(1)} %broadcast_in_dim.54), channel_id=1, replica_groups=mesh['zl'=6,'core'=2,'zh'=2,'y'=8,'x'=4] {'x'}, dimensions={0} | all-to-all | bytes 2883584 | tf_op jit(solution)/shard_map/all_to_all | solution.py:34
  247.6 1.9 collective-permute-start.5
  249.6 4.8 %collective-permute-start.7 = (f32[64,352]{0,1:T(8,128)S(1)}, f32[64,352]{0,1:T(8,128)S(1)}, u32[]{:S(2)}, u32[]{:S(2)}) collective-permute-start(f32[64,352]{0,1:T(8,128)S(1)} %copy-done), channel_id=1, source_target_pairs={{0,0},{32,384},{64,32},{96,416},{128,64},{160,448},{192,96},{224,4... | collective-permute-start | bytes 270344 | tf_op jit(solution)/shard_map/ppermute | solution.py:65
  254.4 2.1 collective-permute-start.6
  257.3 22.0 %collective-permute-done.7 = f32[64,352]{0,1:T(8,128)S(1)} collective-permute-done((f32[64,352]{0,1:T(8,128)S(1)}, f32[64,352]{0,1:T(8,128)S(1)}, u32[]{:S(2)}, u32[]{:S(2)}) %collective-permute-start.7) | collective-permute-done | bytes 90144 | tf_op jit(solution)/shard_map/ppermute | solution.py:65
  280.0 1.2 collective-permute-done.6
  (60 shorter events, 13.0 us)
Async XLA Ops:
  22.0 4.4 %copy-start.3 = (bf16[256,64]{0,1:T(8,128)(2,1)S(1)}, bf16[256,64]{0,1:T(8,128)(2,1)}, u32[]{:S(2)}) copy-start(bf16[256,64]{0,1:T(8,128)(2,1)} %param.7) | copy-start | bytes 98308
  22.0 18.8 %all-to-all-start.1 = ((bf16[4,528,256]{2,1,0:T(8,128)(2,1)}), bf16[4,528,256]{2,1,0:T(8,128)(2,1)S(1)}, u32[]{:S(2)}, u32[]{:S(2)}) async-start(bf16[4,528,256]{2,1,0:T(8,128)(2,1)} %broadcast_in_dim.22), calls=%async_computation.1 | async-start | bytes 2162688 | tf_op jit(solution)/shard_map/all_to_all | solution.py:34
  26.5 14.3 %collective-permute-start.1 = (bf16[64,256]{1,0:T(8,128)(2,1)S(1)}, bf16[64,256]{1,0:T(8,128)(2,1)S(1)}, u32[]{:S(2)}, u32[]{:S(2)}) collective-permute-start(bf16[64,256]{1,0:T(8,128)(2,1)S(1)} %bitcast.120), channel_id=1, source_target_pairs={{0,32},{32,0},{1,33},{33,1},{2,34},{34,2},{3,35},{35,3},{4,36},{36... | collective-permute-start | bytes 98312 | tf_op jit(solution)/shard_map/ppermute | solution.py:51
  43.1 3.9 %collective-permute-start.2 = (f32[6,64,352]{2,1,0:T(8,128)S(1)}, f32[6,64,352]{2,1,0:T(8,128)S(1)}, u32[]{:S(2)}, u32[]{:S(2)}) collective-permute-start(f32[6,64,352]{2,1,0:T(8,128)S(1)} %fusion), channel_id=1, source_target_pairs={{0,64},{64,0},{1,65},{65,1},{2,66},{66,2},{3,67},{67,3},{4,68},{68... | collective-permute-start | bytes 1622024 | tf_op jit(solution)/shard_map/ppermute | solution.py:59
  46.2 10.7 %copy-start.1 = (f32[352,64]{0,1:T(8,128)S(1)}, f32[352,64]{0,1:T(8,128)}, u32[]{:S(2)}) copy-start(f32[352,64]{0,1:T(8,128)} %param.8) | copy-start | bytes 270340
  47.9 35.8 %all-to-all-start.2 = ((f32[6,64,352]{2,1,0:T(8,128)}), f32[6,64,352]{2,1,0:T(8,128)S(1)}, u32[]{:S(2)}, u32[]{:S(2)}) async-start(f32[6,64,352]{2,1,0:T(8,128)} %add.17), calls=%async_computation.2 | async-start | bytes 1179648 | tf_op jit(solution)/shard_map/all_to_all | solution.py:34
  57.0 26.8 %collective-permute-start = (f32[64,352]{0,1:T(8,128)S(1)}, f32[64,352]{0,1:T(8,128)S(1)}, u32[]{:S(2)}, u32[]{:S(2)}) collective-permute-start(f32[64,352]{0,1:T(8,128)S(1)} %bitcast.118), channel_id=1, source_target_pairs={{0,0},{384,32},{32,64},{416,96},{64,128},{448,160},{96,192},{480,2... | collective-permute-start | bytes 270344 | tf_op jit(solution)/shard_map/ppermute | solution.py:52
  102.3 19.5 %all-to-all-start.4 = ((bf16[4,512,352]{1,2,0:T(8,128)(2,1)}), bf16[4,512,352]{1,2,0:T(8,128)(2,1)S(1)}, u32[]{:S(2)}, u32[]{:S(2)}) async-start(bf16[4,512,352]{1,2,0:T(8,128)(2,1)} %broadcast_in_dim.50), calls=%async_computation.4 | async-start | bytes 2883584 | tf_op jit(solution)/shard_map/all_to_all | solution.py:34
  105.8 16.2 %collective-permute-start.3 = (bf16[64,352]{0,1:T(8,128)(2,1)S(1)}, bf16[64,352]{0,1:T(8,128)(2,1)S(1)}, u32[]{:S(2)}, u32[]{:S(2)}) collective-permute-start(bf16[64,352]{0,1:T(8,128)(2,1)S(1)} %get-tuple-element.10), channel_id=1, source_target_pairs={{0,64},{64,0},{1,65},{65,1},{2,66},{66,2},{3,67},{67,3},{4,68},{68... | collective-permute-start | bytes 135176 | tf_op jit(solution)/shard_map/ppermute | solution.py:68
  204.3 3.3 %collective-permute-start.4 = (f32[64,352]{0,1:T(8,128)S(1)}, f32[64,352]{0,1:T(8,128)S(1)}, u32[]{:S(2)}, u32[]{:S(2)}) collective-permute-start(f32[64,352]{0,1:T(8,128)S(1)} %slice.58), channel_id=1, source_target_pairs={{0,64},{64,0},{1,65},{65,1},{2,66},{66,2},{3,67},{67,3},{4,68},{68... | collective-permute-start | bytes 270344 | tf_op jit(solution)/shard_map/ppermute | solution.py:80
  246.9 2.6 copy-start
  247.5 9.0 %copy-start.2 = (f32[352,64]{0,1:T(8,128)S(1)}, f32[352,64]{0,1:T(8,128)}, u32[]{:S(2)}) copy-start(f32[352,64]{0,1:T(8,128)} %param.9) | copy-start | bytes 270340
  247.6 6.7 %collective-permute-start.5 = (f32[64,352]{0,1:T(8,128)S(1)}, f32[64,352]{0,1:T(8,128)S(1)}, u32[]{:S(2)}, u32[]{:S(2)}) collective-permute-start(f32[64,352]{0,1:T(8,128)S(1)} %slice.60), channel_id=1, source_target_pairs={{0,64},{64,0},{1,65},{65,1},{2,66},{66,2},{3,67},{67,3},{4,68},{68... | collective-permute-start | bytes 270344 | tf_op jit(solution)/shard_map/ppermute | solution.py:80
  249.6 29.7 %collective-permute-start.7 = (f32[64,352]{0,1:T(8,128)S(1)}, f32[64,352]{0,1:T(8,128)S(1)}, u32[]{:S(2)}, u32[]{:S(2)}) collective-permute-start(f32[64,352]{0,1:T(8,128)S(1)} %copy-done), channel_id=1, source_target_pairs={{0,0},{32,384},{64,32},{96,416},{128,64},{160,448},{192,96},{224,4... | collective-permute-start | bytes 270344 | tf_op jit(solution)/shard_map/ppermute | solution.py:65
  254.4 26.8 %collective-permute-start.6 = (f32[64,352]{0,1:T(8,128)S(1)}, f32[64,352]{0,1:T(8,128)S(1)}, u32[]{:S(2)}, u32[]{:S(2)}) collective-permute-start(f32[64,352]{0,1:T(8,128)S(1)} %fusion.17), channel_id=1, source_target_pairs={{0,0},{32,384},{64,32},{96,416},{128,64},{160,448},{192,96},{224,4... | collective-permute-start | bytes 270344 | tf_op jit(solution)/shard_map/ppermute | solution.py:89

commit v2 on v1

v2 whole, which is shorter than its diff:
```python
import math

import jax
import jax.numpy as jnp
from jax import lax
from jax.sharding import Mesh
from jax.sharding import PartitionSpec as P

ROWS = 4224
COLS = 4096
Z1, Z0, CORES, ZH, Y, X = 3, 2, 2, 2, 8, 4
AXES = ("z1", "z0", "core", "zh", "y", "x")
COLUMN = ("z1", "z0", "core", "zh")
RING = ("zh", "z1", "z0")
NEAR = ("z1", "z0", "zh")
ZL, Z = Z1 * Z0, ZH * Z1 * Z0


def place(zl, core, zh):
    return (zl * CORES + core) * ZH + zh


TO_WORK = [
    (place(3 * zh + zl // 2, zl % 2, core), place(zl, core, zh))
    for zl in range(ZL)
    for core in range(CORES)
    for zh in range(ZH)
]
TO_HOME = [(work, home) for home, work in TO_WORK]


def ring(z):
    return z % Z % ZL * ZH + z % Z // ZL


EVEN_PAIRS = [(ring(z), ring(z ^ 1)) for z in range(Z)]
ODD_PAIRS = [(ring(z), ring((z - 1 ^ 1) + 1)) for z in range(Z)]


def contract(left, right, dims):
    return lax.dot_general(left, right, (dims, ((), ())), preferred_element_type=jnp.float32)


def exchanged(pieces, axes):
    return lax.all_to_all(pieces, axes, split_axis=0, concat_axis=0, tiled=True)


def from_all(shard, axes, size):
    return exchanged(jnp.broadcast_to(shard[None], (size, *shard.shape)), axes)


def over_plane(tile):
    rows, width = tile.shape
    by_y = from_all(tile, "y", Y).reshape(Y * rows, width)
    return from_all(by_y, "x", X).reshape(X * Y * rows, width)


def per_device(activations, out_grad, momentum, weight, norm_scale, step_size):
    core, high, odd = (lax.axis_index(name) for name in ("core", "zh", "z0"))
    act, grad_out = activations.T, out_grad.T
    features, tokens = act.shape
    peer_out = lax.ppermute(grad_out, "zh", [(0, 1), (1, 0)])
    kept = lax.ppermute(momentum.T, COLUMN, TO_WORK)

    act = over_plane(act).reshape(X, Y, features, tokens)
    act = act.transpose(1, 0, 2, 3).reshape(ZL, -1, tokens)
    low_half = jnp.where(high == 0, grad_out, peer_out)
    high_half = jnp.where(high == 0, peer_out, grad_out)
    part = jnp.stack(
        [contract(half, act[k], ((1,), (1,))) for half in (low_half, high_half) for k in range(ZL)]
    )
    width, height = part.shape[1:]
    part = exchanged(part.reshape(CORES, ZL, width, height), "core").sum(axis=0)
    part = part.reshape(Z1, Z0, width, height).transpose(1, 0, 2, 3)
    part = exchanged(part, "z0").sum(axis=0)
    gradient = exchanged(part, "z1").sum(axis=0)

    new_momentum = 0.95 * kept + gradient
    scaled = (new_momentum / norm_scale).astype(jnp.bfloat16)
    momentum_home = lax.ppermute(new_momentum, COLUMN, TO_HOME)

    pair = lax.all_gather(scaled, "core", axis=0, tiled=True)
    panel = over_plane(scaled)
    panel, momentum_home = lax.optimization_barrier((panel, momentum_home))
    depth = panel.shape[0]
    part = contract(panel, pair, ((1,), (1,)))
    piece = -(-depth // (2 * Z * 8)) * 8
    part = jnp.pad(part, ((0, 2 * Z * piece - depth), (0, 0)))
    part = part.reshape(2, Z0, Z // Z0 * piece, CORES * width)
    leaving = lax.dynamic_index_in_dim(part, 1 - odd, 1, False)
    staying = lax.dynamic_index_in_dim(part, odd, 1, False)
    came = jnp.stack(
        [lax.ppermute(leaving[0], NEAR, EVEN_PAIRS), lax.ppermute(leaving[1], NEAR, ODD_PAIRS)]
    )
    part = (staying + came).reshape(2, Z // Z0, piece, CORES * width).transpose(1, 0, 2, 3)
    gram = exchanged(part, ("zh", "z1")).sum(axis=0).astype(jnp.bfloat16)
    gram = from_all(gram, RING, Z).reshape(Z // Z0, Z0, 2, piece, CORES * width)
    gram = gram.transpose(2, 1, 0, 3, 4).reshape(-1, CORES * width)[:depth]

    def times_gram(rows):
        both = contract(gram, rows, ((0,), (0,))).reshape(CORES, width, height)
        both = lax.all_gather(both, "core", axis=0, tiled=False)
        return lax.dynamic_index_in_dim(both, core, 1, False).sum(axis=0)

    first_power = times_gram(panel).astype(jnp.bfloat16)
    second_power = times_gram(over_plane(first_power))
    direction = (
        3.4445 * scaled.astype(jnp.float32)
        - 4.775 * first_power.astype(jnp.float32)
        + 2.0315 * second_power
    )
    direction = lax.ppermute(direction, COLUMN, TO_HOME).T
    factor = 0.2 * math.sqrt(max(ROWS, COLS))
    return (weight - step_size * factor * direction, momentum_home.T)


def solution(mesh):
    torus = Mesh(mesh.devices.reshape(Z1, Z0, CORES, ZH, Y, X), AXES)
    tiles = P(("z1", "z0", "core"), ("zh", "y", "x"))
    return jax.shard_map(
        per_device,
        mesh=torus,
        in_specs=(tiles, tiles, tiles, tiles, P(), P()),
        out_specs=(tiles, tiles),
        check_vma=False,
    )
```

time: 283 us -> 268 us (0.947)
  the two profiles are of different devices: /device:TPU:192 before, /device:TPU:1 now
where the time goes in v2:
time: 268 us; the launch traced here: 264 us
  blocking collectives  109 us (41%)
  starting transfers between devices  70.2 us (26%)
  waiting for transfers between devices  65.7 us (25%)
  local copies, waits for them, and re-layouts  10.3 us (4%)
  matrix products  4.13 us (2%)
  other arithmetic  2.7 us (1%)
    all_to_all x6, blocking collectives, exchanged(): return lax.all_to_all(pieces, axes, split_axis=0, concat_axis=0, tiled=True)  99.2 us
    all_to_all x5, waiting for transfers between devices, exchanged(): return lax.all_to_all(pieces, axes, split_axis=0, concat_axis=0, tiled=True)  55.2 us
    all_to_all x5, starting transfers between devices, exchanged(): return lax.all_to_all(pieces, axes, split_axis=0, concat_axis=0, tiled=True)  32 us
    ppermute x1, starting transfers between devices, per_device(): peer_out = lax.ppermute(grad_out, 'zh', [(0, 1), (1, 0)])  14.8 us
    ppermute x1, starting transfers between devices, per_device(): momentum_home = lax.ppermute(new_momentum, COLUMN, TO_HOME)  12.4 us
    all_gather x2, blocking collectives, times_gram(): both = lax.all_gather(both, 'core', axis=0, tiled=False)  7.9 us
    broadcast_in_dim x10, local copies, waits for them, and re-layouts, from_all(): return exchanged(jnp.broadcast_to(shard[None], (size, *shard.shape)), axes)  5.69 us
  transfers between devices with their start and end apart: 11, of which 8 were waited for; matrix products, arithmetic and copies ran while one was open for 0% of the time, Pallas kernels for 0%

profile of v2, /device:TPU:1, one launch (start us, length us, event | category | flops | bytes accessed | tf_op | source)
XLA Modules:
  0.0 264.4 jit_solution(12914719947459004738)
XLA Ops:
  1.4 17.1 %all_to_all.55 = bf16[8,66,256]{2,1,0:T(8,128)(2,1)S(1)} all-to-all(bf16[8,66,256]{2,1,0:T(8,128)(2,1)S(1)} %broadcast_in_dim.20), channel_id=1, replica_groups=mesh['z1'=3,'z0'=2,'core'=2,'zh'=2,'y'=8,'x'=4] {'y'}, dimensions={0} | all-to-all | bytes 540672 | tf_op jit(solution)/shard_map/all_to_all | solution.py:45
  19.7 5.3 %all-to-all-start.1 = ((bf16[4,528,256]{2,1,0:T(8,128)(2,1)}), bf16[4,528,256]{2,1,0:T(8,128)(2,1)S(1)}, u32[]{:S(2)}, u32[]{:S(2)}) async-start(bf16[4,528,256]{2,1,0:T(8,128)(2,1)} %broadcast_in_dim.22), calls=%async_computation.1 | async-start | bytes 2162688 | tf_op jit(solution)/shard_map/all_to_all | solution.py:45
  25.0 14.8 %collective-permute-start.1 = (bf16[64,256]{1,0:T(8,128)(2,1)S(1)}, bf16[64,256]{1,0:T(8,128)(2,1)S(1)}, u32[]{:S(2)}, u32[]{:S(2)}) collective-permute-start(bf16[64,256]{1,0:T(8,128)(2,1)S(1)} %bitcast.151), channel_id=1, source_target_pairs={{0,32},{32,0},{1,33},{33,1},{2,34},{34,2},{3,35},{35,3},{4,36},{36... | collective-permute-start | bytes 98312 | tf_op jit(solution)/shard_map/ppermute | solution.py:62
  44.6 8.2 %all_to_all.56 = f32[2,6,64,352]{3,2,1,0:T(8,128)S(1)} all-to-all(f32[2,6,64,352]{3,2,1,0:T(8,128)S(1)} %bitcast.145), channel_id=1, replica_groups=mesh['z1'=3,'z0'=2,'core'=2,'zh'=2,'y'=8,'x'=4] {'core'}, dimensions={0} | all-to-all | bytes 2162688 | tf_op jit(solution)/shard_map/all_to_all | solution.py:45
  53.0 10.8 %all_to_all.57 = f32[2,3,64,352]{3,2,1,0:T(8,128)S(1)} all-to-all(f32[2,3,64,352]{3,2,1,0:T(8,128)S(1)} %copy.36), channel_id=1, replica_groups=mesh['z1'=3,'z0'=2,'core'=2,'zh'=2,'y'=8,'x'=4] {'z0'}, dimensions={0} | all-to-all | bytes 1081344 | tf_op jit(solution)/shard_map/all_to_all | solution.py:45
  64.6 6.9 %all-to-all-start.4 = ((f32[3,64,352]{2,1,0:T(8,128)}), f32[3,64,352]{2,1,0:T(8,128)S(1)}, u32[]{:S(2)}, u32[]{:S(2)}) async-start(f32[3,64,352]{2,1,0:T(8,128)} %reduce_sum.55), calls=%async_computation.4 | async-start | bytes 589824 | tf_op jit(solution)/shard_map/all_to_all | solution.py:45
  71.5 3.6 %collective-permute-start = (f32[64,352]{1,0:T(8,128)S(1)}, f32[64,352]{1,0:T(8,128)S(1)}, u32[]{:S(2)}, u32[]{:S(2)}) collective-permute-start(f32[64,352]{1,0:T(8,128)S(1)} %bitcast.152), channel_id=1, source_target_pairs={{0,0},{384,32},{32,64},{416,96},{64,128},{448,160},{96,192},{480,2... | collective-permute-start | bytes 270344 | tf_op jit(solution)/shard_map/ppermute | solution.py:63
  75.7 11.9 %all-to-all-done.4 = f32[3,64,352]{2,1,0:T(8,128)S(1)} async-done(((f32[3,64,352]{2,1,0:T(8,128)}), f32[3,64,352]{2,1,0:T(8,128)S(1)}, u32[]{:S(2)}, u32[]{:S(2)}) %all-to-all-start.4) | async-done | bytes 270368 | tf_op jit(solution)/shard_map/all_to_all | solution.py:45
  87.8 16.5 %all_to_all.58 = bf16[8,64,352]{2,1,0:T(8,128)(2,1)S(1)} all-to-all(bf16[8,64,352]{2,1,0:T(8,128)(2,1)S(1)} %broadcast_in_dim.23), channel_id=1, replica_groups=mesh['z1'=3,'z0'=2,'core'=2,'zh'=2,'y'=8,'x'=4] {'y'}, dimensions={0} | all-to-all | bytes 720896 | tf_op jit(solution)/shard_map/all_to_all | solution.py:45
  105.7 3.7 %all-to-all-start.6 = ((bf16[4,512,352]{1,2,0:T(8,128)(2,1)}), bf16[4,512,352]{1,2,0:T(8,128)(2,1)S(1)}, u32[]{:S(2)}, u32[]{:S(2)}) async-start(bf16[4,512,352]{1,2,0:T(8,128)(2,1)} %broadcast_in_dim.50), calls=%async_computation.6 | async-start | bytes 2883584 | tf_op jit(solution)/shard_map/all_to_all | solution.py:45
  109.4 12.4 %collective-permute-start.2 = (f32[64,352]{1,0:T(8,128)S(1)}, f32[64,352]{1,0:T(8,128)S(1)}, u32[]{:S(2)}, u32[]{:S(2)}) collective-permute-start(f32[64,352]{1,0:T(8,128)S(1)} %get-tuple-element.7), channel_id=1, source_target_pairs={{0,0},{32,384},{64,32},{96,416},{128,64},{160,448},{192,96},{224,4... | collective-permute-start | bytes 270344 | tf_op jit(solution)/shard_map/ppermute | solution.py:80
  123.7 2.7 %all-to-all-done.6 = bf16[4,512,352]{1,2,0:T(8,128)(2,1)S(1)} async-done(((bf16[4,512,352]{1,2,0:T(8,128)(2,1)}), bf16[4,512,352]{1,2,0:T(8,128)(2,1)S(1)}, u32[]{:S(2)}, u32[]{:S(2)}) %all-to-all-start.6) | async-done | bytes 1441824 | tf_op jit(solution)/shard_map/all_to_all | solution.py:45
  131.4 3.3 %collective-permute-done.3 = f32[528,128]{1,0:T(8,128)S(1)} collective-permute-done((f32[528,128]{1,0:T(8,128)S(1)}, f32[528,128]{1,0:T(8,128)S(1)}, u32[]{:S(2)}, u32[]{:S(2)}) %collective-permute-start.3) | collective-permute-done | bytes 270368 | tf_op jit(solution)/shard_map/ppermute | solution.py:93
  134.7 3.2 %collective-permute-done.4 = f32[528,128]{1,0:T(8,128)} collective-permute-done((f32[528,128]{1,0:T(8,128)S(1)}, f32[528,128]{1,0:T(8,128)}, u32[]{:S(2)}, u32[]{:S(2)}) %collective-permute-start.4) | collective-permute-done | bytes 270368 | tf_op jit(solution)/shard_map/ppermute | solution.py:93
  139.0 29.1 %all_to_all.59 = f32[6,2,88,128]{3,2,1,0:T(8,128)S(1)} all-to-all(f32[6,2,88,128]{3,2,1,0:T(8,128)S(1)} %copy.40), channel_id=1, replica_groups=mesh['z1'=3,'z0'=2,'core'=2,'zh'=2,'y'=8,'x'=4] {'zh','z1'}, dimensions={0} | all-to-all | bytes 1081344 | tf_op jit(solution)/shard_map/all_to_all | solution.py:45
  169.0 12.5 %all-to-all-start.8 = ((bf16[12,2,88,128]{3,2,1,0:T(8,128)(2,1)}), bf16[12,2,88,128]{3,2,1,0:T(8,128)(2,1)S(1)}, u32[]{:S(2)}, u32[]{:S(2)}) async-start(bf16[12,2,88,128]{3,2,1,0:T(8,128)(2,1)} %broadcast_in_dim.51), calls=%async_computation.8 | async-start | bytes 1081344 | tf_op jit(solution)/shard_map/all_to_all | solution.py:45
  181.5 21.9 %all-to-all-done.8 = bf16[12,2,88,128]{3,2,1,0:T(8,128)(2,1)S(1)} async-done(((bf16[12,2,88,128]{3,2,1,0:T(8,128)(2,1)}), bf16[12,2,88,128]{3,2,1,0:T(8,128)(2,1)S(1)}, u32[]{:S(2)}, u32[]{:S(2)}) %all-to-all-start.8) | async-done | bytes 540704 | tf_op jit(solution)/shard_map/all_to_all | solution.py:45
  204.1 4.7 %all_gather.10 = f32[2,2,64,352]{3,2,1,0:T(8,128)S(1)} all-gather(f32[1,2,64,352]{3,2,1,0:T(8,128)S(1)} %bitcast.147), channel_id=1, replica_groups=mesh['z1'=3,'z0'=2,'core'=2,'zh'=2,'y'=8,'x'=4] {'core'}, dimensions={0}, use_global_device_ids=true | all-gather | bytes 540672 | tf_op jit(solution)/shard_map/all_gather | solution.py:102
  208.9 17.5 %all_to_all.60 = bf16[8,64,352]{2,1,0:T(8,128)(2,1)S(1)} all-to-all(bf16[8,64,352]{2,1,0:T(8,128)(2,1)S(1)} %broadcast_in_dim.52), channel_id=1, replica_groups=mesh['z1'=3,'z0'=2,'core'=2,'zh'=2,'y'=8,'x'=4] {'y'}, dimensions={0} | all-to-all | bytes 720896 | tf_op jit(solution)/shard_map/all_to_all | solution.py:45
  227.8 3.5 %all-to-all-start.10 = ((bf16[4,512,352]{1,2,0:T(8,128)(2,1)}), bf16[4,512,352]{1,2,0:T(8,128)(2,1)S(1)}, u32[]{:S(2)}, u32[]{:S(2)}) async-start(bf16[4,512,352]{1,2,0:T(8,128)(2,1)} %broadcast_in_dim.54), calls=%async_computation.10 | async-start | bytes 2883584 | tf_op jit(solution)/shard_map/all_to_all | solution.py:45
  231.6 18.6 %all-to-all-done.10 = bf16[4,512,352]{1,2,0:T(8,128)(2,1)S(1)} async-done(((bf16[4,512,352]{1,2,0:T(8,128)(2,1)}), bf16[4,512,352]{1,2,0:T(8,128)(2,1)S(1)}, u32[]{:S(2)}, u32[]{:S(2)}) %all-to-all-start.10) | async-done | bytes 1441824 | tf_op jit(solution)/shard_map/all_to_all | solution.py:45
  253.1 3.2 %all-gather = f32[4,64,352]{2,1,0:T(8,128)S(1)} all-gather(f32[2,64,352]{2,1,0:T(8,128)S(1)} %fusion.16), channel_id=2, replica_groups=mesh['z1'=3,'z0'=2,'core'=2,'zh'=2,'y'=8,'x'=4] {'core'}, dimensions={0}, use_global_device_ids=true | all-gather | bytes 540672 | tf_op jit(solution)/shard_map/all_gather | solution.py:102
  256.3 3.5 %collective-permute-start.5 = (f32[64,352]{1,0:T(8,128)S(1)}, f32[64,352]{1,0:T(8,128)S(1)}, u32[]{:S(2)}, u32[]{:S(2)}) collective-permute-start(f32[64,352]{1,0:T(8,128)S(1)} %multiply_add_fusion), channel_id=1, source_target_pairs={{0,0},{32,384},{64,32},{96,416},{128,64},{160,448},{192,96},{224,4... | collective-permute-start | bytes 270344 | tf_op jit(solution)/shard_map/ppermute | solution.py:112
  260.5 2.6 collective-permute-done.5
  (68 shorter events, 24.1 us)
Async XLA Ops:
  19.7 5.3 %copy-start.3 = (bf16[256,64]{0,1:T(8,128)(2,1)S(1)}, bf16[256,64]{0,1:T(8,128)(2,1)}, u32[]{:S(2)}) copy-start(bf16[256,64]{0,1:T(8,128)(2,1)} %param.7) | copy-start | bytes 98308
  19.7 21.5 %all-to-all-start.1 = ((bf16[4,528,256]{2,1,0:T(8,128)(2,1)}), bf16[4,528,256]{2,1,0:T(8,128)(2,1)S(1)}, u32[]{:S(2)}, u32[]{:S(2)}) async-start(bf16[4,528,256]{2,1,0:T(8,128)(2,1)} %broadcast_in_dim.22), calls=%async_computation.1 | async-start | bytes 2162688 | tf_op jit(solution)/shard_map/all_to_all | solution.py:45
  25.0 16.1 %collective-permute-start.1 = (bf16[64,256]{1,0:T(8,128)(2,1)S(1)}, bf16[64,256]{1,0:T(8,128)(2,1)S(1)}, u32[]{:S(2)}, u32[]{:S(2)}) collective-permute-start(bf16[64,256]{1,0:T(8,128)(2,1)S(1)} %bitcast.151), channel_id=1, source_target_pairs={{0,32},{32,0},{1,33},{33,1},{2,34},{34,2},{3,35},{35,3},{4,36},{36... | collective-permute-start | bytes 98312 | tf_op jit(solution)/shard_map/ppermute | solution.py:62
  53.0 18.5 %copy-start.4 = (f32[352,64]{0,1:T(8,128)S(1)}, f32[352,64]{0,1:T(8,128)}, u32[]{:S(2)}) copy-start(f32[352,64]{0,1:T(8,128)} %param.8) | copy-start | bytes 270340
  64.6 23.1 %all-to-all-start.4 = ((f32[3,64,352]{2,1,0:T(8,128)}), f32[3,64,352]{2,1,0:T(8,128)S(1)}, u32[]{:S(2)}, u32[]{:S(2)}) async-start(f32[3,64,352]{2,1,0:T(8,128)} %reduce_sum.55), calls=%async_computation.4 | async-start | bytes 589824 | tf_op jit(solution)/shard_map/all_to_all | solution.py:45
  71.5 16.2 %collective-permute-start = (f32[64,352]{1,0:T(8,128)S(1)}, f32[64,352]{1,0:T(8,128)S(1)}, u32[]{:S(2)}, u32[]{:S(2)}) collective-permute-start(f32[64,352]{1,0:T(8,128)S(1)} %bitcast.152), channel_id=1, source_target_pairs={{0,0},{384,32},{32,64},{416,96},{64,128},{448,160},{96,192},{480,2... | collective-permute-start | bytes 270344 | tf_op jit(solution)/shard_map/ppermute | solution.py:63
  105.7 20.8 %all-to-all-start.6 = ((bf16[4,512,352]{1,2,0:T(8,128)(2,1)}), bf16[4,512,352]{1,2,0:T(8,128)(2,1)S(1)}, u32[]{:S(2)}, u32[]{:S(2)}) async-start(bf16[4,512,352]{1,2,0:T(8,128)(2,1)} %broadcast_in_dim.50), calls=%async_computation.6 | async-start | bytes 2883584 | tf_op jit(solution)/shard_map/all_to_all | solution.py:45
  109.4 17.3 %collective-permute-start.2 = (f32[64,352]{1,0:T(8,128)S(1)}, f32[64,352]{1,0:T(8,128)S(1)}, u32[]{:S(2)}, u32[]{:S(2)}) collective-permute-start(f32[64,352]{1,0:T(8,128)S(1)} %get-tuple-element.7), channel_id=1, source_target_pairs={{0,0},{32,384},{64,32},{96,416},{128,64},{160,448},{192,96},{224,4... | collective-permute-start | bytes 270344 | tf_op jit(solution)/shard_map/ppermute | solution.py:80
  126.7 0.7 copy-start
  127.5 7.2 %collective-permute-start.3 = (f32[528,128]{1,0:T(8,128)S(1)}, f32[528,128]{1,0:T(8,128)S(1)}, u32[]{:S(2)}, u32[]{:S(2)}) collective-permute-start(f32[528,128]{1,0:T(8,128)S(1)} %get-tuple-element.8), channel_id=1, source_target_pairs={{0,128},{128,0},{256,384},{384,256},{512,640},{640,512},{32,160},{... | collective-permute-start | bytes 811016 | tf_op jit(solution)/shard_map/ppermute | solution.py:93
  129.4 8.5 %collective-permute-start.4 = (f32[528,128]{1,0:T(8,128)S(1)}, f32[528,128]{1,0:T(8,128)}, u32[]{:S(2)}, u32[]{:S(2)}) collective-permute-start(f32[528,128]{1,0:T(8,128)S(1)} %get-tuple-element.9), channel_id=1, source_target_pairs={{0,672},{128,256},{256,128},{384,512},{512,384},{640,32},{32,640},... | collective-permute-start | bytes 811016 | tf_op jit(solution)/shard_map/ppermute | solution.py:93
  169.0 34.4 %all-to-all-start.8 = ((bf16[12,2,88,128]{3,2,1,0:T(8,128)(2,1)}), bf16[12,2,88,128]{3,2,1,0:T(8,128)(2,1)S(1)}, u32[]{:S(2)}, u32[]{:S(2)}) async-start(bf16[12,2,88,128]{3,2,1,0:T(8,128)(2,1)} %broadcast_in_dim.51), calls=%async_computation.8 | async-start | bytes 1081344 | tf_op jit(solution)/shard_map/all_to_all | solution.py:45
  227.8 22.5 %all-to-all-start.10 = ((bf16[4,512,352]{1,2,0:T(8,128)(2,1)}), bf16[4,512,352]{1,2,0:T(8,128)(2,1)S(1)}, u32[]{:S(2)}, u32[]{:S(2)}) async-start(bf16[4,512,352]{1,2,0:T(8,128)(2,1)} %broadcast_in_dim.54), calls=%async_computation.10 | async-start | bytes 2883584 | tf_op jit(solution)/shard_map/all_to_all | solution.py:45
  252.5 10.6 %copy-start.2 = (f32[352,64]{0,1:T(8,128)S(1)}, f32[352,64]{0,1:T(8,128)}, u32[]{:S(2)}) copy-start(f32[352,64]{0,1:T(8,128)} %param.9) | copy-start | bytes 270340
  253.1 10.7 %copy-start.1 = (f32[64,352]{1,0:T(8,128)S(1)}, f32[64,352]{1,0:T(8,128)}, u32[]{:S(2)}) copy-start(f32[64,352]{1,0:T(8,128)} %copy-done) | copy-start | bytes 270340
  256.3 6.8 %collective-permute-start.5 = (f32[64,352]{1,0:T(8,128)S(1)}, f32[64,352]{1,0:T(8,128)S(1)}, u32[]{:S(2)}, u32[]{:S(2)}) collective-permute-start(f32[64,352]{1,0:T(8,128)S(1)} %multiply_add_fusion), channel_id=1, source_target_pairs={{0,0},{32,384},{64,32},{96,416},{128,64},{160,448},{192,96},{224,4... | collective-permute-start | bytes 270344 | tf_op jit(solution)/shard_map/ppermute | solution.py:112

commit v3 on v2

--- a/solution.py
+++ b/solution.py
@@ -3,6 +3,7 @@
 import jax
 import jax.numpy as jnp
 from jax import lax
+from jax.experimental.layout import Layout, with_layout_constraint
 from jax.sharding import Mesh
 from jax.sharding import PartitionSpec as P
 
@@ -49,10 +50,17 @@
     return exchanged(jnp.broadcast_to(shard[None], (size, *shard.shape)), axes)
 
 
-def over_plane(tile):
+def row_major(array):
+    return with_layout_constraint(array, Layout(tuple(range(array.ndim))))
+
+
+def over_plane(tile, beside_y=(), beside_x=()):
     rows, width = tile.shape
     by_y = from_all(tile, "y", Y).reshape(Y * rows, width)
-    return from_all(by_y, "x", X).reshape(X * Y * rows, width)
+    by_y, *beside_y = lax.optimization_barrier((row_major(by_y), *beside_y))
+    panel = from_all(by_y, "x", X).reshape(X * Y * rows, width)
+    panel, *beside_x = lax.optimization_barrier((row_major(panel), *beside_x))
+    return panel, *beside_y, *beside_x
 
 
 def per_device(activations, out_grad, momentum, weight, norm_scale, step_size):
@@ -62,7 +70,8 @@
     peer_out = lax.ppermute(grad_out, "zh", [(0, 1), (1, 0)])
     kept = lax.ppermute(momentum.T, COLUMN, TO_WORK)
 
-    act = over_plane(act).reshape(X, Y, features, tokens)
+    act, peer_out, kept = over_plane(act, (peer_out,), (kept,))
+    act = act.reshape(X, Y, features, tokens)
     act = act.transpose(1, 0, 2, 3).reshape(ZL, -1, tokens)
     low_half = jnp.where(high == 0, grad_out, peer_out)
     high_half = jnp.where(high == 0, peer_out, grad_out)
@@ -80,8 +89,7 @@
     momentum_home = lax.ppermute(new_momentum, COLUMN, TO_HOME)
 
     pair = lax.all_gather(scaled, "core", axis=0, tiled=True)
-    panel = over_plane(scaled)
-    panel, momentum_home = lax.optimization_barrier((panel, momentum_home))
+    panel, momentum_home = over_plane(scaled, (), (momentum_home,))
     depth = panel.shape[0]
     part = contract(panel, pair, ((1,), (1,)))
     piece = -(-depth // (2 * Z * 8)) * 8
@@ -94,7 +102,7 @@
     )
     part = (staying + came).reshape(2, Z // Z0, piece, CORES * width).transpose(1, 0, 2, 3)
     gram = exchanged(part, ("zh", "z1")).sum(axis=0).astype(jnp.bfloat16)
-    gram = from_all(gram, RING, Z).reshape(Z // Z0, Z0, 2, piece, CORES * width)
+    gram = lax.all_gather(gram, RING, axis=0, tiled=False).reshape(Z // Z0, Z0, 2, piece, CORES * width)
     gram = gram.transpose(2, 1, 0, 3, 4).reshape(-1, CORES * width)[:depth]
 
     def times_gram(rows):
@@ -103,7 +111,7 @@
         return lax.dynamic_index_in_dim(both, core, 1, False).sum(axis=0)
 
     first_power = times_gram(panel).astype(jnp.bfloat16)
-    second_power = times_gram(over_plane(first_power))
+    second_power = times_gram(over_plane(first_power)[0])
     direction = (
         3.4445 * scaled.astype(jnp.float32)
         - 4.775 * first_power.astype(jnp.float32)

time: 268 us -> 257 us (0.959)
  waiting for transfers between devices: 65.7 us -> 41.7 us
  blocking collectives: 109 us -> 121 us
  starting transfers between devices: 70.2 us -> 74.8 us
    all_gather x0 -> x1, blocking collectives: none -> 32.9 us  [per_device(): lax.all_gather(gram, RING, axis=0, tiled=False)]
    all_to_all x5, waiting for transfers between devices: 55.2 us -> 25.3 us  [exchanged(): return lax.all_to_all(pieces, axes, split_axis=0, concat_axis=0, tiled=True)]
    all_to_all x6 -> x5, blocking collectives: 99.2 us -> 74.2 us  [exchanged(): return lax.all_to_all(pieces, axes, split_axis=0, concat_axis=0, tiled=True)]
    ppermute x1, waiting for transfers between devices: 0.01 us -> 9.45 us  [per_device(): kept = lax.ppermute(momentum.T, COLUMN, TO_WORK)]
    ppermute x1, starting transfers between devices: 1.92 us -> 7.55 us  [per_device(): lax.ppermute(leaving[1], NEAR, ODD_PAIRS)]
    all_gather x2, blocking collectives: 7.9 us -> 12.5 us  [times_gram(): both = lax.all_gather(both, 'core', axis=0, tiled=False)]
    all_to_all x5, starting transfers between devices: 32 us -> 28.6 us  [exchanged(): return lax.all_to_all(pieces, axes, split_axis=0, concat_axis=0, tiled=True)]
    ppermute x1, waiting for transfers between devices: 3.29 us -> 0.01 us  [per_device(): lax.ppermute(leaving[0], NEAR, EVEN_PAIRS)]
  transfers between devices with their start and end apart: 11 -> 11, of which waited for: 8 -> 7; matrix products, arithmetic and copies ran while one was open for 0% -> 0% of each run, Pallas kernels for 0% -> 0%
where the time goes in v3:
time: 257 us; the launch traced here: 256 us
  blocking collectives  121 us (47%)
  starting transfers between devices  74.8 us (29%)
  waiting for transfers between devices  41.7 us (16%)
  local copies, waits for them, and re-layouts  8.66 us (3%)
  matrix products  3.82 us (1%)
  other arithmetic  2.71 us (1%)
    all_to_all x5, blocking collectives, exchanged(): return lax.all_to_all(pieces, axes, split_axis=0, concat_axis=0, tiled=True)  74.2 us
    all_gather x1, blocking collectives, per_device(): lax.all_gather(gram, RING, axis=0, tiled=False)  32.9 us
    all_to_all x5, starting transfers between devices, exchanged(): return lax.all_to_all(pieces, axes, split_axis=0, concat_axis=0, tiled=True)  28.6 us
    all_to_all x5, waiting for transfers between devices, exchanged(): return lax.all_to_all(pieces, axes, split_axis=0, concat_axis=0, tiled=True)  25.3 us
    ppermute x1, starting transfers between devices, per_device(): peer_out = lax.ppermute(grad_out, 'zh', [(0, 1), (1, 0)])  14.8 us
    ppermute x1, starting transfers between devices, per_device(): momentum_home = lax.ppermute(new_momentum, COLUMN, TO_HOME)  13.2 us
    all_gather x2, blocking collectives, times_gram(): both = lax.all_gather(both, 'core', axis=0, tiled=False)  12.5 us
    ppermute x1, waiting for transfers between devices, per_device(): kept = lax.ppermute(momentum.T, COLUMN, TO_WORK)  9.45 us
  transfers between devices with their start and end apart: 11, of which 7 were waited for; matrix products, arithmetic and copies ran while one was open for 0% of the time, Pallas kernels for 0%

profile of v3, /device:TPU:1, one launch (start us, length us, event | category | flops | bytes accessed | tf_op | source)
XLA Modules:
  0.0 255.5 jit_solution(10703109950413124827)
XLA Ops:
  2.1 7.7 %all-to-all-start = ((bf16[8,66,256]{2,1,0:T(8,128)(2,1)}), bf16[8,66,256]{2,1,0:T(8,128)(2,1)S(1)}, u32[]{:S(2)}, u32[]{:S(2)}) async-start(bf16[8,66,256]{2,1,0:T(8,128)(2,1)} %broadcast_in_dim.12), calls=%async_computation | async-start | bytes 589824 | tf_op jit(solution)/shard_map/all_to_all | solution.py:46
  9.8 14.8 %collective-permute-start = (bf16[64,256]{1,0:T(8,128)(2,1)}, bf16[64,256]{1,0:T(8,128)(2,1)S(1)}, u32[]{:S(2)}, u32[]{:S(2)}) collective-permute-start(bf16[64,256]{1,0:T(8,128)(2,1)} %bitcast.144), channel_id=1, source_target_pairs={{0,32},{32,0},{1,33},{33,1},{2,34},{34,2},{3,35},{35,3},{4,36},{36... | collective-permute-start | bytes 98312 | tf_op jit(solution)/shard_map/ppermute | solution.py:70
  27.2 4.1 %all-to-all-start.1 = ((bf16[4,528,256]{2,1,0:T(8,128)(2,1)}), bf16[4,528,256]{2,1,0:T(8,128)(2,1)S(1)}, u32[]{:S(2)}, u32[]{:S(2)}) async-start(bf16[4,528,256]{2,1,0:T(8,128)(2,1)} %broadcast_in_dim.13), calls=%async_computation.1 | async-start | bytes 2162688 | tf_op jit(solution)/shard_map/all_to_all | solution.py:46
  31.3 5.1 %collective-permute-start.1 = (f32[64,352]{1,0:T(8,128)S(1)}, f32[64,352]{1,0:T(8,128)S(1)}, u32[]{:S(2)}, u32[]{:S(2)}) collective-permute-start(f32[64,352]{1,0:T(8,128)S(1)} %bitcast.145), channel_id=1, source_target_pairs={{0,0},{384,32},{32,64},{416,96},{64,128},{448,160},{96,192},{480,2... | collective-permute-start | bytes 270344 | tf_op jit(solution)/shard_map/ppermute | solution.py:71
  36.5 9.5 %collective-permute-done.1 = f32[64,352]{1,0:T(8,128)S(1)} collective-permute-done((f32[64,352]{1,0:T(8,128)S(1)}, f32[64,352]{1,0:T(8,128)S(1)}, u32[]{:S(2)}, u32[]{:S(2)}) %collective-permute-start.1) | collective-permute-done | bytes 90144 | tf_op jit(solution)/shard_map/ppermute | solution.py:71
  49.1 6.1 %all_to_all.50 = f32[2,6,64,352]{3,2,1,0:T(8,128)S(1)} all-to-all(f32[2,6,64,352]{3,2,1,0:T(8,128)S(1)} %bitcast.138), channel_id=1, replica_groups=mesh['z1'=3,'z0'=2,'core'=2,'zh'=2,'y'=8,'x'=4] {'core'}, dimensions={0} | all-to-all | bytes 2162688 | tf_op jit(solution)/shard_map/all_to_all | solution.py:46
  55.4 10.7 %all_to_all.51 = f32[2,3,64,352]{3,2,1,0:T(8,128)S(1)} all-to-all(f32[2,3,64,352]{3,2,1,0:T(8,128)S(1)} %copy.35), channel_id=1, replica_groups=mesh['z1'=3,'z0'=2,'core'=2,'zh'=2,'y'=8,'x'=4] {'z0'}, dimensions={0} | all-to-all | bytes 1081344 | tf_op jit(solution)/shard_map/all_to_all | solution.py:46
  66.8 6.7 %all-to-all-start.4 = ((f32[3,64,352]{2,1,0:T(8,128)}), f32[3,64,352]{2,1,0:T(8,128)S(1)}, u32[]{:S(2)}, u32[]{:S(2)}) async-start(f32[3,64,352]{2,1,0:T(8,128)} %reduce_sum.55), calls=%async_computation.4 | async-start | bytes 589824 | tf_op jit(solution)/shard_map/all_to_all | solution.py:46
  74.2 12.3 %all-to-all-done.4 = f32[3,64,352]{2,1,0:T(8,128)S(1)} async-done(((f32[3,64,352]{2,1,0:T(8,128)}), f32[3,64,352]{2,1,0:T(8,128)S(1)}, u32[]{:S(2)}, u32[]{:S(2)}) %all-to-all-start.4) | async-done | bytes 270368 | tf_op jit(solution)/shard_map/all_to_all | solution.py:46
  86.7 19.9 %all_to_all.52 = bf16[8,64,352]{2,1,0:T(8,128)(2,1)S(1)} all-to-all(bf16[8,64,352]{2,1,0:T(8,128)(2,1)S(1)} %broadcast_in_dim.14), channel_id=1, replica_groups=mesh['z1'=3,'z0'=2,'core'=2,'zh'=2,'y'=8,'x'=4] {'y'}, dimensions={0} | all-to-all | bytes 720896 | tf_op jit(solution)/shard_map/all_to_all | solution.py:46
  108.0 3.5 %all-to-all-start.6 = ((bf16[4,512,352]{1,2,0:T(8,128)(2,1)}), bf16[4,512,352]{1,2,0:T(8,128)(2,1)S(1)}, u32[]{:S(2)}, u32[]{:S(2)}) async-start(bf16[4,512,352]{1,2,0:T(8,128)(2,1)} %broadcast_in_dim.15), calls=%async_computation.6 | async-start | bytes 2883584 | tf_op jit(solution)/shard_map/all_to_all | solution.py:46
  111.6 13.2 %collective-permute-start.2 = (f32[64,352]{1,0:T(8,128)S(1)}, f32[64,352]{1,0:T(8,128)S(1)}, u32[]{:S(2)}, u32[]{:S(2)}) collective-permute-start(f32[64,352]{1,0:T(8,128)S(1)} %get-tuple-element.15), channel_id=1, source_target_pairs={{0,0},{32,384},{64,32},{96,416},{128,64},{160,448},{192,96},{224,4... | collective-permute-start | bytes 270344 | tf_op jit(solution)/shard_map/ppermute | solution.py:89
  124.8 1.9 all_gather.13
  130.1 1.9 collective-permute-start.3
  132.1 7.5 %collective-permute-start.4 = (f32[528,128]{1,0:T(8,128)S(1)}, f32[528,128]{1,0:T(8,128)}, u32[]{:S(2)}, u32[]{:S(2)}) collective-permute-start(f32[528,128]{1,0:T(8,128)S(1)} %get-tuple-element.17), channel_id=1, source_target_pairs={{0,672},{128,256},{256,128},{384,512},{512,384},{640,32},{32,640},... | collective-permute-start | bytes 811016 | tf_op jit(solution)/shard_map/ppermute | solution.py:101
  139.7 3.9 %collective-permute-done.4 = f32[528,128]{1,0:T(8,128)} collective-permute-done((f32[528,128]{1,0:T(8,128)S(1)}, f32[528,128]{1,0:T(8,128)}, u32[]{:S(2)}, u32[]{:S(2)}) %collective-permute-start.4) | collective-permute-done | bytes 270368 | tf_op jit(solution)/shard_map/ppermute | solution.py:101
  145.4 6.5 %all-to-all-start.7 = ((f32[6,2,88,128]{3,2,1,0:T(8,128)}), f32[6,2,88,128]{3,2,1,0:T(8,128)S(1)}, u32[]{:S(2)}, u32[]{:S(2)}) async-start(f32[6,2,88,128]{3,2,1,0:T(8,128)} %copy.39), calls=%async_computation.7 | async-start | bytes 1081344 | tf_op jit(solution)/shard_map/all_to_all | solution.py:46
  151.9 11.1 %all-to-all-done.7 = f32[6,2,88,128]{3,2,1,0:T(8,128)S(1)} async-done(((f32[6,2,88,128]{3,2,1,0:T(8,128)}), f32[6,2,88,128]{3,2,1,0:T(8,128)S(1)}, u32[]{:S(2)}, u32[]{:S(2)}) %all-to-all-start.7) | async-done | bytes 540704 | tf_op jit(solution)/shard_map/all_to_all | solution.py:46
  163.1 32.9 %all-gather = bf16[24,88,128]{2,1,0:T(8,128)(2,1)S(1)} all-gather(bf16[2,88,128]{2,1,0:T(8,128)(2,1)S(1)} %reduce_sum.57), channel_id=2, replica_groups=mesh['z1'=3,'z0'=2,'core'=2,'zh'=2,'y'=8,'x'=4] {'zh','z1','z0'}, dimensions={0}, use_global_device_ids=true | all-gather | bytes 585728 | tf_op jit(solution)/shard_map/all_gather | solution.py:105
  196.6 7.9 %all_gather.15 = f32[2,2,64,352]{3,2,1,0:T(8,128)S(1)} all-gather(f32[1,2,64,352]{3,2,1,0:T(8,128)S(1)} %bitcast.140), channel_id=1, replica_groups=mesh['z1'=3,'z0'=2,'core'=2,'zh'=2,'y'=8,'x'=4] {'core'}, dimensions={0}, use_global_device_ids=true | all-gather | bytes 540672 | tf_op jit(solution)/shard_map/all_gather | solution.py:110
  204.6 17.4 %all_to_all.53 = bf16[8,64,352]{2,1,0:T(8,128)(2,1)S(1)} all-to-all(bf16[8,64,352]{2,1,0:T(8,128)(2,1)S(1)} %broadcast_in_dim.16), channel_id=1, replica_groups=mesh['z1'=3,'z0'=2,'core'=2,'zh'=2,'y'=8,'x'=4] {'y'}, dimensions={0} | all-to-all | bytes 720896 | tf_op jit(solution)/shard_map/all_to_all | solution.py:46
  222.3 20.0 %all_to_all.54 = bf16[4,512,352]{1,2,0:T(8,128)(2,1)S(1)} all-to-all(bf16[4,512,352]{1,2,0:T(8,128)(2,1)S(1)} %broadcast_in_dim.17), channel_id=1, replica_groups=mesh['z1'=3,'z0'=2,'core'=2,'zh'=2,'y'=8,'x'=4] {'x'}, dimensions={0} | all-to-all | bytes 2883584 | tf_op jit(solution)/shard_map/all_to_all | solution.py:46
  243.7 4.5 %all_gather.16 = f32[2,2,64,352]{3,2,1,0:T(8,128)S(1)} all-gather(f32[1,2,64,352]{3,2,1,0:T(8,128)S(1)} %bitcast.139), channel_id=1, replica_groups=mesh['z1'=3,'z0'=2,'core'=2,'zh'=2,'y'=8,'x'=4] {'core'}, dimensions={0}, use_global_device_ids=true | all-gather | bytes 540672 | tf_op jit(solution)/shard_map/all_gather | solution.py:110
  248.3 3.6 %collective-permute-start.5 = (f32[64,352]{1,0:T(8,128)S(1)}, f32[64,352]{1,0:T(8,128)S(1)}, u32[]{:S(2)}, u32[]{:S(2)}) collective-permute-start(f32[64,352]{1,0:T(8,128)S(1)} %multiply_add_fusion), channel_id=1, source_target_pairs={{0,0},{32,384},{64,32},{96,416},{128,64},{160,448},{192,96},{224,4... | collective-permute-start | bytes 270344 | tf_op jit(solution)/shard_map/ppermute | solution.py:120
  (72 shorter events, 20.1 us)
Async XLA Ops:
  2.1 22.5 %all-to-all-start = ((bf16[8,66,256]{2,1,0:T(8,128)(2,1)}), bf16[8,66,256]{2,1,0:T(8,128)(2,1)S(1)}, u32[]{:S(2)}, u32[]{:S(2)}) async-start(bf16[8,66,256]{2,1,0:T(8,128)(2,1)} %broadcast_in_dim.12), calls=%async_computation | async-start | bytes 589824 | tf_op jit(solution)/shard_map/all_to_all | solution.py:46
  9.8 16.4 %collective-permute-start = (bf16[64,256]{1,0:T(8,128)(2,1)}, bf16[64,256]{1,0:T(8,128)(2,1)S(1)}, u32[]{:S(2)}, u32[]{:S(2)}) collective-permute-start(bf16[64,256]{1,0:T(8,128)(2,1)} %bitcast.144), channel_id=1, source_target_pairs={{0,32},{32,0},{1,33},{33,1},{2,34},{34,2},{3,35},{35,3},{4,36},{36... | collective-permute-start | bytes 98312 | tf_op jit(solution)/shard_map/ppermute | solution.py:70
  27.2 4.2 %copy-start.8 = (f32[352,64]{0,1:T(8,128)S(1)}, f32[352,64]{0,1:T(8,128)}, u32[]{:S(2)}) copy-start(f32[352,64]{0,1:T(8,128)} %param.8) | copy-start | bytes 270340
  27.2 9.2 %copy-start.7 = (bf16[256,64]{0,1:T(8,128)(2,1)S(1)}, bf16[256,64]{0,1:T(8,128)(2,1)}, u32[]{:S(2)}) copy-start(bf16[256,64]{0,1:T(8,128)(2,1)} %param.7) | copy-start | bytes 98308
  27.2 18.7 %all-to-all-start.1 = ((bf16[4,528,256]{2,1,0:T(8,128)(2,1)}), bf16[4,528,256]{2,1,0:T(8,128)(2,1)S(1)}, u32[]{:S(2)}, u32[]{:S(2)}) async-start(bf16[4,528,256]{2,1,0:T(8,128)(2,1)} %broadcast_in_dim.13), calls=%async_computation.1 | async-start | bytes 2162688 | tf_op jit(solution)/shard_map/all_to_all | solution.py:46
  31.3 14.6 %collective-permute-start.1 = (f32[64,352]{1,0:T(8,128)S(1)}, f32[64,352]{1,0:T(8,128)S(1)}, u32[]{:S(2)}, u32[]{:S(2)}) collective-permute-start(f32[64,352]{1,0:T(8,128)S(1)} %bitcast.145), channel_id=1, source_target_pairs={{0,0},{384,32},{32,64},{416,96},{64,128},{448,160},{96,192},{480,2... | collective-permute-start | bytes 270344 | tf_op jit(solution)/shard_map/ppermute | solution.py:71
  66.8 19.7 %all-to-all-start.4 = ((f32[3,64,352]{2,1,0:T(8,128)}), f32[3,64,352]{2,1,0:T(8,128)S(1)}, u32[]{:S(2)}, u32[]{:S(2)}) async-start(f32[3,64,352]{2,1,0:T(8,128)} %reduce_sum.55), calls=%async_computation.4 | async-start | bytes 589824 | tf_op jit(solution)/shard_map/all_to_all | solution.py:46
  86.6 38.2 %copy-start = (bf16[64,352]{1,0:T(8,128)(2,1)}, bf16[64,352]{1,0:T(8,128)(2,1)S(1)}, u32[]{:S(2)}) copy-start(bf16[64,352]{1,0:T(8,128)(2,1)S(1)} %get-tuple-element.14) | copy-start | bytes 135172
  108.0 20.5 %all-to-all-start.6 = ((bf16[4,512,352]{1,2,0:T(8,128)(2,1)}), bf16[4,512,352]{1,2,0:T(8,128)(2,1)S(1)}, u32[]{:S(2)}, u32[]{:S(2)}) async-start(bf16[4,512,352]{1,2,0:T(8,128)(2,1)} %broadcast_in_dim.15), calls=%async_computation.6 | async-start | bytes 2883584 | tf_op jit(solution)/shard_map/all_to_all | solution.py:46
  111.6 17.8 %collective-permute-start.2 = (f32[64,352]{1,0:T(8,128)S(1)}, f32[64,352]{1,0:T(8,128)S(1)}, u32[]{:S(2)}, u32[]{:S(2)}) collective-permute-start(f32[64,352]{1,0:T(8,128)S(1)} %get-tuple-element.15), channel_id=1, source_target_pairs={{0,0},{32,384},{64,32},{96,416},{128,64},{160,448},{192,96},{224,4... | collective-permute-start | bytes 270344 | tf_op jit(solution)/shard_map/ppermute | solution.py:89
  129.4 0.6 copy-start.4
  130.1 9.5 %collective-permute-start.3 = (f32[528,128]{1,0:T(8,128)S(1)}, f32[528,128]{1,0:T(8,128)S(1)}, u32[]{:S(2)}, u32[]{:S(2)}) collective-permute-start(f32[528,128]{1,0:T(8,128)S(1)} %get-tuple-element.16), channel_id=1, source_target_pairs={{0,128},{128,0},{256,384},{384,256},{512,640},{640,512},{32,160},{... | collective-permute-start | bytes 811016 | tf_op jit(solution)/shard_map/ppermute | solution.py:101
  132.1 11.5 %collective-permute-start.4 = (f32[528,128]{1,0:T(8,128)S(1)}, f32[528,128]{1,0:T(8,128)}, u32[]{:S(2)}, u32[]{:S(2)}) collective-permute-start(f32[528,128]{1,0:T(8,128)S(1)} %get-tuple-element.17), channel_id=1, source_target_pairs={{0,672},{128,256},{256,128},{384,512},{512,384},{640,32},{32,640},... | collective-permute-start | bytes 811016 | tf_op jit(solution)/shard_map/ppermute | solution.py:101
  145.4 17.7 %all-to-all-start.7 = ((f32[6,2,88,128]{3,2,1,0:T(8,128)}), f32[6,2,88,128]{3,2,1,0:T(8,128)S(1)}, u32[]{:S(2)}, u32[]{:S(2)}) async-start(f32[6,2,88,128]{3,2,1,0:T(8,128)} %copy.39), calls=%async_computation.7 | async-start | bytes 1081344 | tf_op jit(solution)/shard_map/all_to_all | solution.py:46
  204.5 17.7 %copy-start.2 = (bf16[64,352]{1,0:T(8,128)(2,1)}, bf16[64,352]{1,0:T(8,128)(2,1)S(1)}, u32[]{:S(2)}) copy-start(bf16[64,352]{1,0:T(8,128)(2,1)S(1)} %dynamic-slice_reduce_fusion.1) | copy-start | bytes 135172
  243.2 5.1 %copy-start.1 = (bf16[64,352]{1,0:T(8,128)(2,1)S(1)}, bf16[64,352]{1,0:T(8,128)(2,1)}, u32[]{:S(2)}) copy-start(bf16[64,352]{1,0:T(8,128)(2,1)} %copy-done) | copy-start | bytes 135172
  243.2 5.1 %copy-start.3 = (bf16[64,352]{1,0:T(8,128)(2,1)S(1)}, bf16[64,352]{1,0:T(8,128)(2,1)}, u32[]{:S(2)}) copy-start(bf16[64,352]{1,0:T(8,128)(2,1)} %copy-done.2) | copy-start | bytes 135172
  243.2 11.0 %copy-start.6 = (f32[352,64]{0,1:T(8,128)S(1)}, f32[352,64]{0,1:T(8,128)}, u32[]{:S(2)}) copy-start(f32[352,64]{0,1:T(8,128)} %param.9) | copy-start | bytes 270340
  243.7 11.2 %copy-start.5 = (f32[64,352]{1,0:T(8,128)S(1)}, f32[64,352]{1,0:T(8,128)}, u32[]{:S(2)}) copy-start(f32[64,352]{1,0:T(8,128)} %copy-done.4) | copy-start | bytes 270340
  248.3 5.9 %collective-permute-start.5 = (f32[64,352]{1,0:T(8,128)S(1)}, f32[64,352]{1,0:T(8,128)S(1)}, u32[]{:S(2)}, u32[]{:S(2)}) collective-permute-start(f32[64,352]{1,0:T(8,128)S(1)} %multiply_add_fusion), channel_id=1, source_target_pairs={{0,0},{32,384},{64,32},{96,416},{128,64},{160,448},{192,96},{224,4... | collective-permute-start | bytes 270344 | tf_op jit(solution)/shard_map/ppermute | solution.py:120

commit v4 on v3

--- a/solution.py
+++ b/solution.py
@@ -1,3 +1,4 @@
+import itertools
 import math
 
 import jax
@@ -21,13 +22,26 @@
     return (zl * CORES + core) * ZH + zh
 
 
+def working_z(tile):
+    return (tile // 2 + 3 + 6 * (tile % 2)) % Z
+
+
 TO_WORK = [
-    (place(3 * zh + zl // 2, zl % 2, core), place(zl, core, zh))
-    for zl in range(ZL)
-    for core in range(CORES)
-    for zh in range(ZH)
+    (place(tile // 2, tile % 2, half), place(working_z(tile) % ZL, half, working_z(tile) // ZL))
+    for tile in range(Z)
+    for half in range(CORES)
 ]
 TO_HOME = [(work, home) for home, work in TO_WORK]
+
+
+def dealt(turn):
+    pairs = []
+    for zl, core, zh, y, x in itertools.product(*map(range, (ZL, CORES, ZH, Y, X))):
+        tile, unit = divmod(3 * ((zh * Y + y) * X + x) + (turn - zl) % 3, 16)
+        to_zh, to_zl = divmod(working_z(tile), ZL)
+        target = (place(to_zl, core, to_zh) * Y + unit % Y) * X + zl // 3 * 2 + unit // Y
+        pairs.append(((place(zl, core, zh) * Y + y) * X + x, target))
+    return pairs
 
 
 def ring(z):
@@ -64,25 +78,35 @@
 
 
 def per_device(activations, out_grad, momentum, weight, norm_scale, step_size):
-    core, high, odd = (lax.axis_index(name) for name in ("core", "zh", "z0"))
-    act, grad_out = activations.T, out_grad.T
-    features, tokens = act.shape
-    peer_out = lax.ppermute(grad_out, "zh", [(0, 1), (1, 0)])
+    core, high, odd, y, x = (lax.axis_index(name) for name in ("core", "zh", "z0", "y", "x"))
+    row_group = lax.axis_index("z1") * Z0 + odd
+    act = activations.T.reshape(3, -1, activations.shape[0])
     kept = lax.ppermute(momentum.T, COLUMN, TO_WORK)
 
-    act, peer_out, kept = over_plane(act, (peer_out,), (kept,))
-    act = act.reshape(X, Y, features, tokens)
-    act = act.transpose(1, 0, 2, 3).reshape(ZL, -1, tokens)
-    low_half = jnp.where(high == 0, grad_out, peer_out)
-    high_half = jnp.where(high == 0, peer_out, grad_out)
-    part = jnp.stack(
-        [contract(half, act[k], ((1,), (1,))) for half in (low_half, high_half) for k in range(ZL)]
+    hands = [
+        lax.ppermute(lax.dynamic_index_in_dim(act, (turn + 2 * row_group) % 3, 0, False), AXES, dealt(turn))
+        for turn in range(3)
+    ]
+    shift = (high * ZL + row_group + Z - 3) % Z
+    tile = shift % 6 * 2 + shift // 6
+    first = (tile + x % 2 * Y + y) % 3
+    hands = lax.dynamic_slice_in_dim(jnp.stack(hands + hands[:2]), first, 3, 0)
+    act = jnp.concatenate(list(hands), axis=1)
+    grad_out = lax.all_gather(out_grad.T, RING, axis=0, tiled=False)
+    act, grad_out, kept = over_plane(act, (grad_out,), (kept,))
+    tokens = act.shape[1]
+    act = act.reshape(2, -1, tokens)
+    width, height = out_grad.shape[1], act.shape[1]
+    grad_out = grad_out.reshape(ZH, ZL, width, -1).transpose(0, 2, 1, 3).reshape(ZH * width, -1)
+
+    def own_columns(both):
+        both = lax.all_gather(both.reshape(CORES, width, height), "core", axis=0, tiled=False)
+        return lax.dynamic_index_in_dim(both, core, 1, False).sum(axis=0)
+
+    gradient = own_columns(
+        contract(grad_out[:, :tokens], act[0], ((1,), (1,)))
+        + contract(grad_out[:, tokens:], act[1], ((1,), (1,)))
     )
-    width, height = part.shape[1:]
-    part = exchanged(part.reshape(CORES, ZL, width, height), "core").sum(axis=0)
-    part = part.reshape(Z1, Z0, width, height).transpose(1, 0, 2, 3)
-    part = exchanged(part, "z0").sum(axis=0)
-    gradient = exchanged(part, "z1").sum(axis=0)
 
     new_momentum = 0.95 * kept + gradient
     scaled = (new_momentum / norm_scale).astype(jnp.bfloat16)
@@ -106,9 +130,7 @@
     gram = gram.transpose(2, 1, 0, 3, 4).reshape(-1, CORES * width)[:depth]
 
     def times_gram(rows):
-        both = contract(gram, rows, ((0,), (0,))).reshape(CORES, width, height)
-        both = lax.all_gather(both, "core", axis=0, tiled=False)
-        return lax.dynamic_index_in_dim(both, core, 1, False).sum(axis=0)
+        return own_columns(contract(gram, rows, ((0,), (0,))))
 
     first_power = times_gram(panel).astype(jnp.bfloat16)
     second_power = times_gram(over_plane(first_power)[0])

time: 257 us -> 263 us (1.023)
  blocking collectives: 121 us -> 144 us
  waiting for transfers between devices: 41.7 us -> 30.2 us
    all_gather x2 -> x4, blocking collectives: 12.5 us -> 34.9 us  [the longest x3 18.1 us: own_columns(): lax.all_gather(both.reshape(CORES, width, height), 'core', axis=0, tiled=...]
    all_to_all x5 -> x3, waiting for transfers between devices: 25.3 us -> 11.8 us  [exchanged(): return lax.all_to_all(pieces, axes, split_axis=0, concat_axis=0, tiled=True)]
    ppermute x1 -> x3, starting transfers between devices: 14.8 us -> 26.6 us  [per_device(): lax.ppermute(lax.dynamic_index_in_dim(act, (turn + 2 * row_group) % 3, 0,...]
    ppermute x1, starting transfers between devices: 13.2 us -> 3.89 us  [per_device(): momentum_home = lax.ppermute(new_momentum, COLUMN, TO_HOME)]
    ppermute x1, waiting for transfers between devices: 9.45 us -> 1.62 us  [per_device(): kept = lax.ppermute(momentum.T, COLUMN, TO_WORK)]
    ppermute x1, starting transfers between devices: 5.08 us -> 12.1 us  [per_device(): kept = lax.ppermute(momentum.T, COLUMN, TO_WORK)]
    all_to_all x5 -> x4, blocking collectives: 74.2 us -> 79.9 us  [exchanged(): return lax.all_to_all(pieces, axes, split_axis=0, concat_axis=0, tiled=True)]
    ppermute x1, starting transfers between devices: 7.55 us -> 1.92 us  [per_device(): lax.ppermute(leaving[1], NEAR, ODD_PAIRS)]
  transfers between devices with their start and end apart: 11 -> 11, of which waited for: 7 -> 6; matrix products, arithmetic and copies ran while one was open for 0% -> 0% of each run, Pallas kernels for 0% -> 0%
where the time goes in v4:
time: 263 us; the launch traced here: 262 us
  blocking collectives  144 us (55%)
  starting transfers between devices  73.6 us (28%)
  waiting for transfers between devices  30.2 us (11%)
  local copies, waits for them, and re-layouts  7.53 us (3%)
    all_to_all x4, blocking collectives, exchanged(): return lax.all_to_all(pieces, axes, split_axis=0, concat_axis=0, tiled=True)  79.9 us
    all_gather x1, blocking collectives, per_device(): lax.all_gather(gram, RING, axis=0, tiled=False)  27.4 us
    ppermute x3, starting transfers between devices, per_device(): lax.ppermute(lax.dynamic_index_in_dim(act, (turn + 2 * row_group) % 3, 0,...  26.6 us
    all_to_all x3, starting transfers between devices, exchanged(): return lax.all_to_all(pieces, axes, split_axis=0, concat_axis=0, tiled=True)  23.9 us
    all_gather x3, blocking collectives, own_columns(): lax.all_gather(both.reshape(CORES, width, height), 'core', axis=0, tiled=...  18.1 us
    all_gather x1, blocking collectives, per_device(): grad_out = lax.all_gather(out_grad.T, RING, axis=0, tiled=False)  16.8 us
    ppermute x1, starting transfers between devices, per_device(): kept = lax.ppermute(momentum.T, COLUMN, TO_WORK)  12.1 us
    all_to_all x3, waiting for transfers between devices, exchanged(): return lax.all_to_all(pieces, axes, split_axis=0, concat_axis=0, tiled=True)  11.8 us
  transfers between devices with their start and end apart: 11, of which 6 were waited for; matrix products, arithmetic and copies ran while one was open for 0% of the time, Pallas kernels for 0%

profile of v4, /device:TPU:1, one launch (start us, length us, event | category | flops | bytes accessed | tf_op | source)
XLA Modules:
  0.0 261.8 jit_solution(10787483956037336849)
XLA Ops:
  1.5 8.4 %collective-permute-start = (bf16[22,256]{1,0:T(8,128)(2,1)S(1)}, bf16[22,256]{1,0:T(8,128)(2,1)S(1)}, u32[]{:S(2)}, u32[]{:S(2)}) collective-permute-start(bf16[22,256]{1,0:T(8,128)(2,1)S(1)} %get-tuple-element.23), channel_id=1, source_target_pairs={{0,384},{1,396},{2,408},{3,389},{4,401},{5,413},{6,424},{7,436},{8... | collective-permute-start | bytes 33800 | tf_op jit(solution)/shard_map/ppermute | solution.py:87
  10.0 9.6 %collective-permute-start.1 = (bf16[22,256]{1,0:T(8,128)(2,1)S(1)}, bf16[22,256]{1,0:T(8,128)(2,1)S(1)}, u32[]{:S(2)}, u32[]{:S(2)}) collective-permute-start(bf16[22,256]{1,0:T(8,128)(2,1)S(1)} %get-tuple-element.22), channel_id=1, source_target_pairs={{0,388},{1,400},{2,412},{3,393},{4,405},{5,416},{6,428},{7,440},{8... | collective-permute-start | bytes 33800 | tf_op jit(solution)/shard_map/ppermute | solution.py:87
  19.6 8.5 %collective-permute-start.2 = (bf16[22,256]{1,0:T(8,128)(2,1)S(1)}, bf16[22,256]{1,0:T(8,128)(2,1)S(1)}, u32[]{:S(2)}, u32[]{:S(2)}) collective-permute-start(bf16[22,256]{1,0:T(8,128)(2,1)S(1)} %get-tuple-element.21), channel_id=1, source_target_pairs={{0,392},{1,404},{2,385},{3,397},{4,409},{5,420},{6,432},{7,444},{8... | collective-permute-start | bytes 33800 | tf_op jit(solution)/shard_map/ppermute | solution.py:87
  28.3 3.6 %collective-permute-done.2 = bf16[22,256]{1,0:T(8,128)(2,1)S(1)} collective-permute-done((bf16[22,256]{1,0:T(8,128)(2,1)S(1)}, bf16[22,256]{1,0:T(8,128)(2,1)S(1)}, u32[]{:S(2)}, u32[]{:S(2)}) %collective-permute-start.2) | collective-permute-done | bytes 11296 | tf_op jit(solution)/shard_map/ppermute | solution.py:87
  32.7 16.8 %all-to-all-start = ((bf16[8,22,768]{2,1,0:T(8,128)(2,1)}), bf16[8,22,768]{2,1,0:T(8,128)(2,1)S(1)}, u32[]{:S(2)}, u32[]{:S(2)}) async-start(bf16[8,22,768]{2,1,0:T(8,128)(2,1)} %broadcast_in_dim.12), calls=%async_computation | async-start | bytes 589824 | tf_op jit(solution)/shard_map/all_to_all | solution.py:60
  49.5 16.8 %all-gather = bf16[768,256]{1,0:T(8,128)(2,1)S(1)} all-gather(bf16[64,256]{1,0:T(8,128)(2,1)S(1)} %bitcast.84), channel_id=2, replica_groups=mesh['z1'=3,'z0'=2,'core'=2,'zh'=2,'y'=8,'x'=4] {'zh','z1','z0'}, dimensions={0}, use_global_device_ids=true | all-gather | bytes 425984 | tf_op jit(solution)/shard_map/all_gather | solution.py:95
  67.4 3.5 %all-to-all-start.1 = ((bf16[4,176,768]{2,1,0:T(8,128)(2,1)}), bf16[4,176,768]{2,1,0:T(8,128)(2,1)S(1)}, u32[]{:S(2)}, u32[]{:S(2)}) async-start(bf16[4,176,768]{2,1,0:T(8,128)(2,1)} %broadcast_in_dim.13), calls=%async_computation.1 | async-start | bytes 2162688 | tf_op jit(solution)/shard_map/all_to_all | solution.py:60
  71.0 12.1 %collective-permute-start.3 = (f32[64,352]{1,0:T(8,128)S(1)}, f32[64,352]{1,0:T(8,128)S(1)}, u32[]{:S(2)}, u32[]{:S(2)}) collective-permute-start(f32[64,352]{1,0:T(8,128)S(1)} %bitcast.85), channel_id=1, source_target_pairs={{0,384},{32,448},{64,416},{96,480},{128,512},{160,576},{192,544},{... | collective-permute-start | bytes 270344 | tf_op jit(solution)/shard_map/ppermute | solution.py:84
  86.4 6.2 %all_gather.24 = f32[2,2,64,352]{3,2,1,0:T(8,128)S(1)} all-gather(f32[1,2,64,352]{3,2,1,0:T(8,128)S(1)} %bitcast.80), channel_id=1, replica_groups=mesh['z1'=3,'z0'=2,'core'=2,'zh'=2,'y'=8,'x'=4] {'core'}, dimensions={0}, use_global_device_ids=true | all-gather | bytes 540672 | tf_op jit(solution)/shard_map/all_gather | solution.py:103
  92.8 20.8 %all_to_all.35 = bf16[8,64,352]{2,1,0:T(8,128)(2,1)S(1)} all-to-all(bf16[8,64,352]{2,1,0:T(8,128)(2,1)S(1)} %broadcast_in_dim.14), channel_id=1, replica_groups=mesh['z1'=3,'z0'=2,'core'=2,'zh'=2,'y'=8,'x'=4] {'y'}, dimensions={0} | all-to-all | bytes 720896 | tf_op jit(solution)/shard_map/all_to_all | solution.py:60
  115.0 3.5 %all-to-all-start.3 = ((bf16[4,512,352]{1,2,0:T(8,128)(2,1)}), bf16[4,512,352]{1,2,0:T(8,128)(2,1)S(1)}, u32[]{:S(2)}, u32[]{:S(2)}) async-start(bf16[4,512,352]{1,2,0:T(8,128)(2,1)} %broadcast_in_dim.15), calls=%async_computation.3 | async-start | bytes 2883584 | tf_op jit(solution)/shard_map/all_to_all | solution.py:60
  118.5 3.9 %collective-permute-start.4 = (f32[64,352]{1,0:T(8,128)S(1)}, f32[64,352]{1,0:T(8,128)S(1)}, u32[]{:S(2)}, u32[]{:S(2)}) collective-permute-start(f32[64,352]{1,0:T(8,128)S(1)} %get-tuple-element.15), channel_id=1, source_target_pairs={{384,0},{448,32},{416,64},{480,96},{512,128},{576,160},{544,192},{... | collective-permute-start | bytes 270344 | tf_op jit(solution)/shard_map/ppermute | solution.py:113
  124.3 11.8 %all-to-all-done.3 = bf16[4,512,352]{1,2,0:T(8,128)(2,1)S(1)} async-done(((bf16[4,512,352]{1,2,0:T(8,128)(2,1)}), bf16[4,512,352]{1,2,0:T(8,128)(2,1)S(1)}, u32[]{:S(2)}, u32[]{:S(2)}) %all-to-all-start.3) | async-done | bytes 1441824 | tf_op jit(solution)/shard_map/all_to_all | solution.py:60
  137.7 2.8 %collective-permute-start.5 = (f32[528,128]{1,0:T(8,128)S(1)}, f32[528,128]{1,0:T(8,128)S(1)}, u32[]{:S(2)}, u32[]{:S(2)}) collective-permute-start(f32[528,128]{1,0:T(8,128)S(1)} %get-tuple-element.16), channel_id=1, source_target_pairs={{0,128},{128,0},{256,384},{384,256},{512,640},{640,512},{32,160},{... | collective-permute-start | bytes 811016 | tf_op jit(solution)/shard_map/ppermute | solution.py:125
  142.5 2.4 collective-permute-done.5
  144.9 4.2 %collective-permute-done.6 = f32[528,128]{1,0:T(8,128)} collective-permute-done((f32[528,128]{1,0:T(8,128)S(1)}, f32[528,128]{1,0:T(8,128)}, u32[]{:S(2)}, u32[]{:S(2)}) %collective-permute-start.6) | collective-permute-done | bytes 270368 | tf_op jit(solution)/shard_map/ppermute | solution.py:125
  150.1 20.1 %all_to_all.36 = f32[6,2,88,128]{3,2,1,0:T(8,128)S(1)} all-to-all(f32[6,2,88,128]{3,2,1,0:T(8,128)S(1)} %copy.30), channel_id=1, replica_groups=mesh['z1'=3,'z0'=2,'core'=2,'zh'=2,'y'=8,'x'=4] {'zh','z1'}, dimensions={0} | all-to-all | bytes 1081344 | tf_op jit(solution)/shard_map/all_to_all | solution.py:60
  170.3 27.4 %all-gather.1 = bf16[24,88,128]{2,1,0:T(8,128)(2,1)S(1)} all-gather(bf16[2,88,128]{2,1,0:T(8,128)(2,1)S(1)} %reduce_sum.37), channel_id=3, replica_groups=mesh['z1'=3,'z0'=2,'core'=2,'zh'=2,'y'=8,'x'=4] {'zh','z1','z0'}, dimensions={0}, use_global_device_ids=true | all-gather | bytes 585728 | tf_op jit(solution)/shard_map/all_gather | solution.py:129
  198.2 8.9 %all_gather.27 = f32[2,2,64,352]{3,2,1,0:T(8,128)S(1)} all-gather(f32[1,2,64,352]{3,2,1,0:T(8,128)S(1)} %bitcast.79), channel_id=1, replica_groups=mesh['z1'=3,'z0'=2,'core'=2,'zh'=2,'y'=8,'x'=4] {'core'}, dimensions={0}, use_global_device_ids=true | all-gather | bytes 540672 | tf_op jit(solution)/shard_map/all_gather | solution.py:103
  207.1 17.5 %all_to_all.37 = bf16[8,64,352]{2,1,0:T(8,128)(2,1)S(1)} all-to-all(bf16[8,64,352]{2,1,0:T(8,128)(2,1)S(1)} %broadcast_in_dim.16), channel_id=1, replica_groups=mesh['z1'=3,'z0'=2,'core'=2,'zh'=2,'y'=8,'x'=4] {'y'}, dimensions={0} | all-to-all | bytes 720896 | tf_op jit(solution)/shard_map/all_to_all | solution.py:60
  225.0 21.4 %all_to_all.38 = bf16[4,512,352]{1,2,0:T(8,128)(2,1)S(1)} all-to-all(bf16[4,512,352]{1,2,0:T(8,128)(2,1)S(1)} %broadcast_in_dim.17), channel_id=1, replica_groups=mesh['z1'=3,'z0'=2,'core'=2,'zh'=2,'y'=8,'x'=4] {'x'}, dimensions={0} | all-to-all | bytes 2883584 | tf_op jit(solution)/shard_map/all_to_all | solution.py:60
  247.8 3.0 %all_gather.28 = f32[2,2,64,352]{3,2,1,0:T(8,128)S(1)} all-gather(f32[1,2,64,352]{3,2,1,0:T(8,128)S(1)} %bitcast.78), channel_id=1, replica_groups=mesh['z1'=3,'z0'=2,'core'=2,'zh'=2,'y'=8,'x'=4] {'core'}, dimensions={0}, use_global_device_ids=true | all-gather | bytes 540672 | tf_op jit(solution)/shard_map/all_gather | solution.py:103
  250.9 2.3 collective-permute-start.7
  253.8 6.6 %collective-permute-done.7 = f32[64,352]{1,0:T(8,128)S(1)} collective-permute-done((f32[64,352]{1,0:T(8,128)S(1)}, f32[64,352]{1,0:T(8,128)S(1)}, u32[]{:S(2)}, u32[]{:S(2)}) %collective-permute-start.7) | collective-permute-done | bytes 90144 | tf_op jit(solution)/shard_map/ppermute | solution.py:142
  (68 shorter events, 16.9 us)
Async XLA Ops:
  0.6 48.9 %copy-start.7 = (bf16[256,64]{0,1:T(8,128)(2,1)S(1)}, bf16[256,64]{0,1:T(8,128)(2,1)}, u32[]{:S(2)}) copy-start(bf16[256,64]{0,1:T(8,128)(2,1)} %param.7) | copy-start | bytes 98308
  1.5 26.7 %collective-permute-start = (bf16[22,256]{1,0:T(8,128)(2,1)S(1)}, bf16[22,256]{1,0:T(8,128)(2,1)S(1)}, u32[]{:S(2)}, u32[]{:S(2)}) collective-permute-start(bf16[22,256]{1,0:T(8,128)(2,1)S(1)} %get-tuple-element.23), channel_id=1, source_target_pairs={{0,384},{1,396},{2,408},{3,389},{4,401},{5,413},{6,424},{7,436},{8... | collective-permute-start | bytes 33800 | tf_op jit(solution)/shard_map/ppermute | solution.py:87
  10.0 18.3 %collective-permute-start.1 = (bf16[22,256]{1,0:T(8,128)(2,1)S(1)}, bf16[22,256]{1,0:T(8,128)(2,1)S(1)}, u32[]{:S(2)}, u32[]{:S(2)}) collective-permute-start(bf16[22,256]{1,0:T(8,128)(2,1)S(1)} %get-tuple-element.22), channel_id=1, source_target_pairs={{0,388},{1,400},{2,412},{3,393},{4,405},{5,416},{6,428},{7,440},{8... | collective-permute-start | bytes 33800 | tf_op jit(solution)/shard_map/ppermute | solution.py:87
  19.6 12.3 %collective-permute-start.2 = (bf16[22,256]{1,0:T(8,128)(2,1)S(1)}, bf16[22,256]{1,0:T(8,128)(2,1)S(1)}, u32[]{:S(2)}, u32[]{:S(2)}) collective-permute-start(bf16[22,256]{1,0:T(8,128)(2,1)S(1)} %get-tuple-element.21), channel_id=1, source_target_pairs={{0,392},{1,404},{2,385},{3,397},{4,409},{5,420},{6,432},{7,444},{8... | collective-permute-start | bytes 33800 | tf_op jit(solution)/shard_map/ppermute | solution.py:87
  32.7 33.6 %all-to-all-start = ((bf16[8,22,768]{2,1,0:T(8,128)(2,1)}), bf16[8,22,768]{2,1,0:T(8,128)(2,1)S(1)}, u32[]{:S(2)}, u32[]{:S(2)}) async-start(bf16[8,22,768]{2,1,0:T(8,128)(2,1)} %broadcast_in_dim.12), calls=%async_computation | async-start | bytes 589824 | tf_op jit(solution)/shard_map/all_to_all | solution.py:60
  66.4 4.6 %copy-start.8 = (f32[352,64]{0,1:T(8,128)S(1)}, f32[352,64]{0,1:T(8,128)}, u32[]{:S(2)}) copy-start(f32[352,64]{0,1:T(8,128)} %param.8) | copy-start | bytes 270340
  67.4 18.3 %all-to-all-start.1 = ((bf16[4,176,768]{2,1,0:T(8,128)(2,1)}), bf16[4,176,768]{2,1,0:T(8,128)(2,1)S(1)}, u32[]{:S(2)}, u32[]{:S(2)}) async-start(bf16[4,176,768]{2,1,0:T(8,128)(2,1)} %broadcast_in_dim.13), calls=%async_computation.1 | async-start | bytes 2162688 | tf_op jit(solution)/shard_map/all_to_all | solution.py:60
  71.0 14.7 %collective-permute-start.3 = (f32[64,352]{1,0:T(8,128)S(1)}, f32[64,352]{1,0:T(8,128)S(1)}, u32[]{:S(2)}, u32[]{:S(2)}) collective-permute-start(f32[64,352]{1,0:T(8,128)S(1)} %bitcast.85), channel_id=1, source_target_pairs={{0,384},{32,448},{64,416},{96,480},{128,512},{160,576},{192,544},{... | collective-permute-start | bytes 270344 | tf_op jit(solution)/shard_map/ppermute | solution.py:84
  92.7 29.7 %copy-start = (bf16[64,352]{1,0:T(8,128)(2,1)}, bf16[64,352]{1,0:T(8,128)(2,1)S(1)}, u32[]{:S(2)}) copy-start(bf16[64,352]{1,0:T(8,128)(2,1)S(1)} %get-tuple-element.14) | copy-start | bytes 135172
  115.0 21.1 %all-to-all-start.3 = ((bf16[4,512,352]{1,2,0:T(8,128)(2,1)}), bf16[4,512,352]{1,2,0:T(8,128)(2,1)S(1)}, u32[]{:S(2)}, u32[]{:S(2)}) async-start(bf16[4,512,352]{1,2,0:T(8,128)(2,1)} %broadcast_in_dim.15), calls=%async_computation.3 | async-start | bytes 2883584 | tf_op jit(solution)/shard_map/all_to_all | solution.py:60
  118.5 18.4 %collective-permute-start.4 = (f32[64,352]{1,0:T(8,128)S(1)}, f32[64,352]{1,0:T(8,128)S(1)}, u32[]{:S(2)}, u32[]{:S(2)}) collective-permute-start(f32[64,352]{1,0:T(8,128)S(1)} %get-tuple-element.15), channel_id=1, source_target_pairs={{384,0},{448,32},{416,64},{480,96},{512,128},{576,160},{544,192},{... | collective-permute-start | bytes 270344 | tf_op jit(solution)/shard_map/ppermute | solution.py:113
  137.0 0.7 copy-start.4
  137.7 7.2 %collective-permute-start.5 = (f32[528,128]{1,0:T(8,128)S(1)}, f32[528,128]{1,0:T(8,128)S(1)}, u32[]{:S(2)}, u32[]{:S(2)}) collective-permute-start(f32[528,128]{1,0:T(8,128)S(1)} %get-tuple-element.16), channel_id=1, source_target_pairs={{0,128},{128,0},{256,384},{384,256},{512,640},{640,512},{32,160},{... | collective-permute-start | bytes 811016 | tf_op jit(solution)/shard_map/ppermute | solution.py:125
  140.5 8.5 %collective-permute-start.6 = (f32[528,128]{1,0:T(8,128)S(1)}, f32[528,128]{1,0:T(8,128)}, u32[]{:S(2)}, u32[]{:S(2)}) collective-permute-start(f32[528,128]{1,0:T(8,128)S(1)} %get-tuple-element.17), channel_id=1, source_target_pairs={{0,672},{128,256},{256,128},{384,512},{512,384},{640,32},{32,640},... | collective-permute-start | bytes 811016 | tf_op jit(solution)/shard_map/ppermute | solution.py:125
  207.1 17.9 %copy-start.2 = (bf16[64,352]{1,0:T(8,128)(2,1)}, bf16[64,352]{1,0:T(8,128)(2,1)S(1)}, u32[]{:S(2)}) copy-start(bf16[64,352]{1,0:T(8,128)(2,1)S(1)} %dynamic-slice_reduce_fusion.1) | copy-start | bytes 135172
  247.2 3.6 %copy-start.1 = (bf16[64,352]{1,0:T(8,128)(2,1)S(1)}, bf16[64,352]{1,0:T(8,128)(2,1)}, u32[]{:S(2)}) copy-start(bf16[64,352]{1,0:T(8,128)(2,1)} %copy-done) | copy-start | bytes 135172
  247.3 3.6 %copy-start.3 = (bf16[64,352]{1,0:T(8,128)(2,1)S(1)}, bf16[64,352]{1,0:T(8,128)(2,1)}, u32[]{:S(2)}) copy-start(bf16[64,352]{1,0:T(8,128)(2,1)} %copy-done.2) | copy-start | bytes 135172
  247.3 13.2 %copy-start.6 = (f32[352,64]{0,1:T(8,128)S(1)}, f32[352,64]{0,1:T(8,128)}, u32[]{:S(2)}) copy-start(f32[352,64]{0,1:T(8,128)} %param.9) | copy-start | bytes 270340
  247.3 13.9 %copy-start.5 = (f32[64,352]{1,0:T(8,128)S(1)}, f32[64,352]{1,0:T(8,128)}, u32[]{:S(2)}) copy-start(f32[64,352]{1,0:T(8,128)} %copy-done.4) | copy-start | bytes 270340
  250.9 9.6 %collective-permute-start.7 = (f32[64,352]{1,0:T(8,128)S(1)}, f32[64,352]{1,0:T(8,128)S(1)}, u32[]{:S(2)}, u32[]{:S(2)}) collective-permute-start(f32[64,352]{1,0:T(8,128)S(1)} %multiply_add_fusion), channel_id=1, source_target_pairs={{384,0},{448,32},{416,64},{480,96},{512,128},{576,160},{544,192},{... | collective-permute-start | bytes 270344 | tf_op jit(solution)/shard_map/ppermute | solution.py:142

commit v5 on v3

--- a/solution.py
+++ b/solution.py
@@ -54,29 +54,29 @@
     return with_layout_constraint(array, Layout(tuple(range(array.ndim))))
 
 
-def over_plane(tile, beside_y=(), beside_x=()):
-    rows, width = tile.shape
-    by_y = from_all(tile, "y", Y).reshape(Y * rows, width)
-    by_y, *beside_y = lax.optimization_barrier((row_major(by_y), *beside_y))
-    panel = from_all(by_y, "x", X).reshape(X * Y * rows, width)
-    panel, *beside_x = lax.optimization_barrier((row_major(panel), *beside_x))
-    return panel, *beside_y, *beside_x
+def over_y(tile, *beside):
+    by_y = from_all(tile, "y", Y).reshape(-1, tile.shape[1])
+    return lax.optimization_barrier((row_major(by_y), *beside))
+
+
+def over_x(rows, *beside):
+    panel = from_all(rows, "x", X).reshape(-1, rows.shape[1])
+    return lax.optimization_barrier((row_major(panel), *beside))
 
 
 def per_device(activations, out_grad, momentum, weight, norm_scale, step_size):
-    core, high, odd = (lax.axis_index(name) for name in ("core", "zh", "z0"))
+    odd = lax.axis_index("z0")
     act, grad_out = activations.T, out_grad.T
     features, tokens = act.shape
-    peer_out = lax.ppermute(grad_out, "zh", [(0, 1), (1, 0)])
+    halves = lax.all_gather(grad_out, "zh", axis=0, tiled=False)
     kept = lax.ppermute(momentum.T, COLUMN, TO_WORK)
 
-    act, peer_out, kept = over_plane(act, (peer_out,), (kept,))
+    act, halves = over_y(act, halves)
+    act, kept = over_x(act, kept)
     act = act.reshape(X, Y, features, tokens)
     act = act.transpose(1, 0, 2, 3).reshape(ZL, -1, tokens)
-    low_half = jnp.where(high == 0, grad_out, peer_out)
-    high_half = jnp.where(high == 0, peer_out, grad_out)
     part = jnp.stack(
-        [contract(half, act[k], ((1,), (1,))) for half in (low_half, high_half) for k in range(ZL)]
+        [contract(half, act[k], ((1,), (1,))) for half in halves for k in range(ZL)]
     )
     width, height = part.shape[1:]
     part = exchanged(part.reshape(CORES, ZL, width, height), "core").sum(axis=0)
@@ -88,10 +88,12 @@
     scaled = (new_momentum / norm_scale).astype(jnp.bfloat16)
     momentum_home = lax.ppermute(new_momentum, COLUMN, TO_HOME)
 
-    pair = lax.all_gather(scaled, "core", axis=0, tiled=True)
-    panel, momentum_home = over_plane(scaled, (), (momentum_home,))
-    depth = panel.shape[0]
-    part = contract(panel, pair, ((1,), (1,)))
+    across = lax.all_gather(scaled, "core", axis=0, tiled=True)
+    across = lax.all_gather(across, "x", axis=0, tiled=False)
+    panel, across = over_y(scaled, across)
+    part = jnp.einsum("br,kqr->kbq", panel, across, preferred_element_type=jnp.float32)
+    part = part.reshape(-1, CORES * width)
+    depth = part.shape[0]
     piece = -(-depth // (2 * Z * 8)) * 8
     part = jnp.pad(part, ((0, 2 * Z * piece - depth), (0, 0)))
     part = part.reshape(2, Z0, Z // Z0 * piece, CORES * width)
@@ -105,13 +107,15 @@
     gram = lax.all_gather(gram, RING, axis=0, tiled=False).reshape(Z // Z0, Z0, 2, piece, CORES * width)
     gram = gram.transpose(2, 1, 0, 3, 4).reshape(-1, CORES * width)[:depth]
 
+    gram = gram.reshape(X, -1, CORES * width)
+
     def times_gram(rows):
-        both = contract(gram, rows, ((0,), (0,))).reshape(CORES, width, height)
-        both = lax.all_gather(both, "core", axis=0, tiled=False)
-        return lax.dynamic_index_in_dim(both, core, 1, False).sum(axis=0)
+        parts = jnp.einsum("kbq,br->kqr", gram, rows, preferred_element_type=jnp.float32)
+        return exchanged(parts.reshape(-1, width, height), ("x", "core")).sum(axis=0)
 
     first_power = times_gram(panel).astype(jnp.bfloat16)
-    second_power = times_gram(over_plane(first_power)[0])
+    panel, momentum_home = over_y(first_power, momentum_home)
+    second_power = times_gram(panel)
     direction = (
         3.4445 * scaled.astype(jnp.float32)
         - 4.775 * first_power.astype(jnp.float32)

time: 257 us -> 241 us (0.938)
  starting transfers between devices: 74.8 us -> 54.7 us
  blocking collectives: 121 us -> 133 us
  waiting for transfers between devices: 41.7 us -> 38.1 us
    all_gather x1, blocking collectives: 32.9 us -> 17.6 us  [per_device(): lax.all_gather(gram, RING, axis=0, tiled=False)]
    ppermute x1 -> x0, starting transfers between devices: 14.8 us -> none  [per_device(): peer_out = lax.ppermute(grad_out, 'zh', [(0, 1), (1, 0)])]
    all_gather x3, blocking collectives: 14.3 us -> 27.9 us  [the longest x1 15.2 us: per_device(): halves = lax.all_gather(grad_out, 'zh', axis=0, tiled=False)]
    all_to_all x5, blocking collectives: 74.2 us -> 87.4 us  [exchanged(): return lax.all_to_all(pieces, axes, split_axis=0, concat_axis=0, tiled=True)]
    ppermute x1, starting transfers between devices: 13.2 us -> 5.64 us  [per_device(): momentum_home = lax.ppermute(new_momentum, COLUMN, TO_HOME)]
    all_to_all x5, waiting for transfers between devices: 25.3 us -> 19.7 us  [exchanged(): return lax.all_to_all(pieces, axes, split_axis=0, concat_axis=0, tiled=True)]
  transfers between devices with their start and end apart: 11 -> 10, of which waited for: 7 -> 7; matrix products, arithmetic and copies ran while one was open for 0% -> 0% of each run, Pallas kernels for 0% -> 0%
where the time goes in v5:
time: 241 us; the launch traced here: 240 us
  blocking collectives  133 us (55%)
  starting transfers between devices  54.7 us (23%)
  waiting for transfers between devices  38.1 us (16%)
  local copies, waits for them, and re-layouts  6.41 us (3%)
  matrix products  3.64 us (2%)
    all_to_all x5, blocking collectives, exchanged(): return lax.all_to_all(pieces, axes, split_axis=0, concat_axis=0, tiled=True)  87.4 us
    all_to_all x5, starting transfers between devices, exchanged(): return lax.all_to_all(pieces, axes, split_axis=0, concat_axis=0, tiled=True)  29.2 us
    all_to_all x5, waiting for transfers between devices, exchanged(): return lax.all_to_all(pieces, axes, split_axis=0, concat_axis=0, tiled=True)  19.7 us
    all_gather x1, blocking collectives, per_device(): lax.all_gather(gram, RING, axis=0, tiled=False)  17.6 us
    all_gather x1, blocking collectives, per_device(): halves = lax.all_gather(grad_out, 'zh', axis=0, tiled=False)  15.2 us
    ppermute x1, waiting for transfers between devices, per_device(): kept = lax.ppermute(momentum.T, COLUMN, TO_WORK)  10.6 us
    all_gather x1, blocking collectives, per_device(): across = lax.all_gather(across, 'x', axis=0, tiled=False)  10.2 us
    ppermute x1, starting transfers between devices, per_device(): lax.ppermute(leaving[1], NEAR, ODD_PAIRS)  7.3 us
  transfers between devices with their start and end apart: 10, of which 7 were waited for; matrix products, arithmetic and copies ran while one was open for 0% of the time, Pallas kernels for 0%

profile of v5, /device:TPU:1, one launch (start us, length us, event | category | flops | bytes accessed | tf_op | source)
XLA Modules:
  0.0 239.7 jit_solution(2240217809746070120)
XLA Ops:
  2.1 7.7 %all-to-all-start = ((bf16[8,66,256]{2,1,0:T(8,128)(2,1)}), bf16[8,66,256]{2,1,0:T(8,128)(2,1)S(1)}, u32[]{:S(2)}, u32[]{:S(2)}) async-start(bf16[8,66,256]{2,1,0:T(8,128)(2,1)} %broadcast_in_dim.8), calls=%async_computation | async-start | bytes 589824 | tf_op jit(solution)/shard_map/all_to_all | solution.py:46
  9.8 15.2 %all-gather = bf16[128,256]{1,0:T(8,128)(2,1)S(1)} all-gather(bf16[64,256]{1,0:T(8,128)(2,1)} %bitcast.182), channel_id=2, replica_groups=mesh['z1'=3,'z0'=2,'core'=2,'zh'=2,'y'=8,'x'=4] {'zh'}, dimensions={0}, use_global_device_ids=true | all-gather | bytes 98304 | tf_op jit(solution)/shard_map/all_gather | solution.py:71
  26.1 4.1 %all-to-all-start.1 = ((bf16[4,528,256]{2,1,0:T(8,128)(2,1)}), bf16[4,528,256]{2,1,0:T(8,128)(2,1)S(1)}, u32[]{:S(2)}, u32[]{:S(2)}) async-start(bf16[4,528,256]{2,1,0:T(8,128)(2,1)} %broadcast_in_dim.9), calls=%async_computation.1 | async-start | bytes 2162688 | tf_op jit(solution)/shard_map/all_to_all | solution.py:46
  30.2 5.1 %collective-permute-start = (f32[64,352]{1,0:T(8,128)S(1)}, f32[64,352]{1,0:T(8,128)S(1)}, u32[]{:S(2)}, u32[]{:S(2)}) collective-permute-start(f32[64,352]{1,0:T(8,128)S(1)} %bitcast.183), channel_id=1, source_target_pairs={{0,0},{384,32},{32,64},{416,96},{64,128},{448,160},{96,192},{480,2... | collective-permute-start | bytes 270344 | tf_op jit(solution)/shard_map/ppermute | solution.py:72
  35.3 10.6 %collective-permute-done = f32[64,352]{1,0:T(8,128)S(1)} collective-permute-done((f32[64,352]{1,0:T(8,128)S(1)}, f32[64,352]{1,0:T(8,128)S(1)}, u32[]{:S(2)}, u32[]{:S(2)}) %collective-permute-start) | collective-permute-done | bytes 90144 | tf_op jit(solution)/shard_map/ppermute | solution.py:72
  49.0 5.0 %all_to_all.50 = f32[2,6,64,352]{3,2,1,0:T(8,128)S(1)} all-to-all(f32[2,6,64,352]{3,2,1,0:T(8,128)S(1)} %bitcast.177), channel_id=1, replica_groups=mesh['z1'=3,'z0'=2,'core'=2,'zh'=2,'y'=8,'x'=4] {'core'}, dimensions={0} | all-to-all | bytes 2162688 | tf_op jit(solution)/shard_map/all_to_all | solution.py:46
  54.3 10.7 %all_to_all.51 = f32[2,3,64,352]{3,2,1,0:T(8,128)S(1)} all-to-all(f32[2,3,64,352]{3,2,1,0:T(8,128)S(1)} %copy.47), channel_id=1, replica_groups=mesh['z1'=3,'z0'=2,'core'=2,'zh'=2,'y'=8,'x'=4] {'z0'}, dimensions={0} | all-to-all | bytes 1081344 | tf_op jit(solution)/shard_map/all_to_all | solution.py:46
  65.7 6.8 %all-to-all-start.4 = ((f32[3,64,352]{2,1,0:T(8,128)}), f32[3,64,352]{2,1,0:T(8,128)S(1)}, u32[]{:S(2)}, u32[]{:S(2)}) async-start(f32[3,64,352]{2,1,0:T(8,128)} %reduce_sum.55), calls=%async_computation.4 | async-start | bytes 589824 | tf_op jit(solution)/shard_map/all_to_all | solution.py:46
  73.2 12.3 %all-to-all-done.4 = f32[3,64,352]{2,1,0:T(8,128)S(1)} async-done(((f32[3,64,352]{2,1,0:T(8,128)}), f32[3,64,352]{2,1,0:T(8,128)S(1)}, u32[]{:S(2)}, u32[]{:S(2)}) %all-to-all-start.4) | async-done | bytes 270368 | tf_op jit(solution)/shard_map/all_to_all | solution.py:46
  86.4 6.5 %all-to-all-start.5 = ((bf16[8,64,352]{2,1,0:T(8,128)(2,1)}), bf16[8,64,352]{2,1,0:T(8,128)(2,1)S(1)}, u32[]{:S(2)}, u32[]{:S(2)}) async-start(bf16[8,64,352]{2,1,0:T(8,128)(2,1)} %broadcast_in_dim.10), calls=%async_computation.5 | async-start | bytes 786432 | tf_op jit(solution)/shard_map/all_to_all | solution.py:46
  92.9 2.5 %all_gather.21 = bf16[128,352]{1,0:T(8,128)(2,1)S(1)} all-gather(bf16[64,352]{1,0:T(8,128)(2,1)S(1)} %get-tuple-element.18), channel_id=1, replica_groups=mesh['z1'=3,'z0'=2,'core'=2,'zh'=2,'y'=8,'x'=4] {'core'}, dimensions={0}, use_global_device_ids=true | all-gather | bytes 135168 | tf_op jit(solution)/shard_map/all_gather | solution.py:91
  95.4 10.2 %all-gather.1 = bf16[512,352]{1,0:T(8,128)(2,1)S(1)} all-gather(bf16[128,352]{1,0:T(8,128)(2,1)S(1)} %all_gather.21), channel_id=3, replica_groups=mesh['z1'=3,'z0'=2,'core'=2,'zh'=2,'y'=8,'x'=4] {'x'}, dimensions={0}, use_global_device_ids=true | all-gather | bytes 450560 | tf_op jit(solution)/shard_map/all_gather | solution.py:92
  108.0 1.9 collective-permute-start.1
  109.9 7.3 %collective-permute-start.2 = (f32[528,128]{1,0:T(8,128)S(1)}, f32[528,128]{1,0:T(8,128)S(1)}, u32[]{:S(2)}, u32[]{:S(2)}) collective-permute-start(f32[528,128]{1,0:T(8,128)S(1)} %get-tuple-element.21), channel_id=1, source_target_pairs={{0,672},{128,256},{256,128},{384,512},{512,384},{640,32},{32,640},... | collective-permute-start | bytes 811016 | tf_op jit(solution)/shard_map/ppermute | solution.py:103
  117.3 5.3 %collective-permute-done.2 = f32[528,128]{1,0:T(8,128)S(1)} collective-permute-done((f32[528,128]{1,0:T(8,128)S(1)}, f32[528,128]{1,0:T(8,128)S(1)}, u32[]{:S(2)}, u32[]{:S(2)}) %collective-permute-start.2) | collective-permute-done | bytes 270368 | tf_op jit(solution)/shard_map/ppermute | solution.py:103
  122.6 27.1 %all_to_all.52 = f32[6,2,88,128]{3,2,1,0:T(8,128)S(1)} all-to-all(f32[6,2,88,128]{3,2,1,0:T(8,128)S(1)} %copy.52), channel_id=1, replica_groups=mesh['z1'=3,'z0'=2,'core'=2,'zh'=2,'y'=8,'x'=4] {'zh','z1'}, dimensions={0} | all-to-all | bytes 1081344 | tf_op jit(solution)/shard_map/all_to_all | solution.py:46
  149.8 17.6 %all-gather.2 = bf16[24,88,128]{2,1,0:T(8,128)(2,1)S(1)} all-gather(bf16[2,88,128]{2,1,0:T(8,128)(2,1)S(1)} %reduce_sum.57), channel_id=4, replica_groups=mesh['z1'=3,'z0'=2,'core'=2,'zh'=2,'y'=8,'x'=4] {'zh','z1','z0'}, dimensions={0}, use_global_device_ids=true | all-gather | bytes 585728 | tf_op jit(solution)/shard_map/all_gather | solution.py:107
  168.1 27.3 %all_to_all.53 = f32[8,64,352]{2,1,0:T(8,128)S(1)} all-to-all(f32[8,64,352]{2,1,0:T(8,128)S(1)} %fusion.15), channel_id=1, replica_groups=mesh['z1'=3,'z0'=2,'core'=2,'zh'=2,'y'=8,'x'=4] {'x','core'}, dimensions={0} | all-to-all | bytes 1441792 | tf_op jit(solution)/shard_map/all_to_all | solution.py:46
  196.3 4.1 %all-to-all-start.8 = ((bf16[8,64,352]{2,1,0:T(8,128)(2,1)}), bf16[8,64,352]{2,1,0:T(8,128)(2,1)S(1)}, u32[]{:S(2)}, u32[]{:S(2)}) async-start(bf16[8,64,352]{2,1,0:T(8,128)(2,1)} %broadcast_in_dim.11), calls=%async_computation.8 | async-start | bytes 786432 | tf_op jit(solution)/shard_map/all_to_all | solution.py:46
  200.3 5.6 %collective-permute-start.3 = (f32[64,352]{1,0:T(8,128)S(1)}, f32[64,352]{1,0:T(8,128)S(1)}, u32[]{:S(2)}, u32[]{:S(2)}) collective-permute-start(f32[64,352]{1,0:T(8,128)S(1)} %get-tuple-element.19), channel_id=1, source_target_pairs={{0,0},{32,384},{64,32},{96,416},{128,64},{160,448},{192,96},{224,4... | collective-permute-start | bytes 270344 | tf_op jit(solution)/shard_map/ppermute | solution.py:89
  206.0 1.6 collective-permute-done.3
  207.6 5.9 %all-to-all-done.8 = bf16[8,64,352]{2,1,0:T(8,128)(2,1)S(1)} async-done(((bf16[8,64,352]{2,1,0:T(8,128)(2,1)}), bf16[8,64,352]{2,1,0:T(8,128)(2,1)S(1)}, u32[]{:S(2)}, u32[]{:S(2)}) %all-to-all-start.8) | async-done | bytes 360480 | tf_op jit(solution)/shard_map/all_to_all | solution.py:46
  214.0 17.2 %all_to_all.54 = f32[8,64,352]{2,1,0:T(8,128)S(1)} all-to-all(f32[8,64,352]{2,1,0:T(8,128)S(1)} %fusion.13), channel_id=1, replica_groups=mesh['z1'=3,'z0'=2,'core'=2,'zh'=2,'y'=8,'x'=4] {'x','core'}, dimensions={0} | all-to-all | bytes 1441792 | tf_op jit(solution)/shard_map/all_to_all | solution.py:46
  231.3 5.5 %collective-permute-start.4 = (f32[64,352]{1,0:T(8,128)S(1)}, f32[64,352]{1,0:T(8,128)S(1)}, u32[]{:S(2)}, u32[]{:S(2)}) collective-permute-start(f32[64,352]{1,0:T(8,128)S(1)} %multiply_add_fusion), channel_id=1, source_target_pairs={{0,0},{32,384},{64,32},{96,416},{128,64},{160,448},{192,96},{224,4... | collective-permute-start | bytes 270344 | tf_op jit(solution)/shard_map/ppermute | solution.py:124
  (52 shorter events, 14.2 us)
Async XLA Ops:
  2.1 22.8 %all-to-all-start = ((bf16[8,66,256]{2,1,0:T(8,128)(2,1)}), bf16[8,66,256]{2,1,0:T(8,128)(2,1)S(1)}, u32[]{:S(2)}, u32[]{:S(2)}) async-start(bf16[8,66,256]{2,1,0:T(8,128)(2,1)} %broadcast_in_dim.8), calls=%async_computation | async-start | bytes 589824 | tf_op jit(solution)/shard_map/all_to_all | solution.py:46
  26.1 4.1 %copy-start.1 = (f32[352,64]{0,1:T(8,128)S(1)}, f32[352,64]{0,1:T(8,128)}, u32[]{:S(2)}) copy-start(f32[352,64]{0,1:T(8,128)} %param.8) | copy-start | bytes 270340
  26.1 19.8 %all-to-all-start.1 = ((bf16[4,528,256]{2,1,0:T(8,128)(2,1)}), bf16[4,528,256]{2,1,0:T(8,128)(2,1)S(1)}, u32[]{:S(2)}, u32[]{:S(2)}) async-start(bf16[4,528,256]{2,1,0:T(8,128)(2,1)} %broadcast_in_dim.9), calls=%async_computation.1 | async-start | bytes 2162688 | tf_op jit(solution)/shard_map/all_to_all | solution.py:46
  30.2 15.7 %collective-permute-start = (f32[64,352]{1,0:T(8,128)S(1)}, f32[64,352]{1,0:T(8,128)S(1)}, u32[]{:S(2)}, u32[]{:S(2)}) collective-permute-start(f32[64,352]{1,0:T(8,128)S(1)} %bitcast.183), channel_id=1, source_target_pairs={{0,0},{384,32},{32,64},{416,96},{64,128},{448,160},{96,192},{480,2... | collective-permute-start | bytes 270344 | tf_op jit(solution)/shard_map/ppermute | solution.py:72
  65.7 19.8 %all-to-all-start.4 = ((f32[3,64,352]{2,1,0:T(8,128)}), f32[3,64,352]{2,1,0:T(8,128)S(1)}, u32[]{:S(2)}, u32[]{:S(2)}) async-start(f32[3,64,352]{2,1,0:T(8,128)} %reduce_sum.55), calls=%async_computation.4 | async-start | bytes 589824 | tf_op jit(solution)/shard_map/all_to_all | solution.py:46
  86.4 20.7 %all-to-all-start.5 = ((bf16[8,64,352]{2,1,0:T(8,128)(2,1)}), bf16[8,64,352]{2,1,0:T(8,128)(2,1)S(1)}, u32[]{:S(2)}, u32[]{:S(2)}) async-start(bf16[8,64,352]{2,1,0:T(8,128)(2,1)} %broadcast_in_dim.10), calls=%async_computation.5 | async-start | bytes 786432 | tf_op jit(solution)/shard_map/all_to_all | solution.py:46
  108.0 9.3 %collective-permute-start.1 = (f32[528,128]{1,0:T(8,128)S(1)}, f32[528,128]{1,0:T(8,128)S(1)}, u32[]{:S(2)}, u32[]{:S(2)}) collective-permute-start(f32[528,128]{1,0:T(8,128)S(1)} %get-tuple-element.20), channel_id=1, source_target_pairs={{0,128},{128,0},{256,384},{384,256},{512,640},{640,512},{32,160},{... | collective-permute-start | bytes 811016 | tf_op jit(solution)/shard_map/ppermute | solution.py:103
  109.9 12.6 %collective-permute-start.2 = (f32[528,128]{1,0:T(8,128)S(1)}, f32[528,128]{1,0:T(8,128)S(1)}, u32[]{:S(2)}, u32[]{:S(2)}) collective-permute-start(f32[528,128]{1,0:T(8,128)S(1)} %get-tuple-element.21), channel_id=1, source_target_pairs={{0,672},{128,256},{256,128},{384,512},{512,384},{640,32},{32,640},... | collective-permute-start | bytes 811016 | tf_op jit(solution)/shard_map/ppermute | solution.py:103
  196.3 17.2 %all-to-all-start.8 = ((bf16[8,64,352]{2,1,0:T(8,128)(2,1)}), bf16[8,64,352]{2,1,0:T(8,128)(2,1)S(1)}, u32[]{:S(2)}, u32[]{:S(2)}) async-start(bf16[8,64,352]{2,1,0:T(8,128)(2,1)} %broadcast_in_dim.11), calls=%async_computation.8 | async-start | bytes 786432 | tf_op jit(solution)/shard_map/all_to_all | solution.py:46
  200.3 7.3 %collective-permute-start.3 = (f32[64,352]{1,0:T(8,128)S(1)}, f32[64,352]{1,0:T(8,128)S(1)}, u32[]{:S(2)}, u32[]{:S(2)}) collective-permute-start(f32[64,352]{1,0:T(8,128)S(1)} %get-tuple-element.19), channel_id=1, source_target_pairs={{0,0},{32,384},{64,32},{96,416},{128,64},{160,448},{192,96},{224,4... | collective-permute-start | bytes 270344 | tf_op jit(solution)/shard_map/ppermute | solution.py:89
  213.9 24.5 %copy-start = (f32[352,64]{0,1:T(8,128)S(1)}, f32[352,64]{0,1:T(8,128)}, u32[]{:S(2)}) copy-start(f32[352,64]{0,1:T(8,128)} %param.9) | copy-start | bytes 270340
  231.3 7.2 %collective-permute-start.4 = (f32[64,352]{1,0:T(8,128)S(1)}, f32[64,352]{1,0:T(8,128)S(1)}, u32[]{:S(2)}, u32[]{:S(2)}) collective-permute-start(f32[64,352]{1,0:T(8,128)S(1)} %multiply_add_fusion), channel_id=1, source_target_pairs={{0,0},{32,384},{64,32},{96,416},{128,64},{160,448},{192,96},{224,4... | collective-permute-start | bytes 270344 | tf_op jit(solution)/shard_map/ppermute | solution.py:124

commit v6 on v5

--- a/solution.py
+++ b/solution.py
@@ -71,8 +71,7 @@
     halves = lax.all_gather(grad_out, "zh", axis=0, tiled=False)
     kept = lax.ppermute(momentum.T, COLUMN, TO_WORK)
 
-    act, halves = over_y(act, halves)
-    act, kept = over_x(act, kept)
+    act, kept, halves = over_x(over_y(act)[0], kept, halves)
     act = act.reshape(X, Y, features, tokens)
     act = act.transpose(1, 0, 2, 3).reshape(ZL, -1, tokens)
     part = jnp.stack(
@@ -88,34 +87,35 @@
     scaled = (new_momentum / norm_scale).astype(jnp.bfloat16)
     momentum_home = lax.ppermute(new_momentum, COLUMN, TO_HOME)
 
-    across = lax.all_gather(scaled, "core", axis=0, tiled=True)
-    across = lax.all_gather(across, "x", axis=0, tiled=False)
+    across = lax.all_gather(scaled, "x", axis=0, tiled=True)
     panel, across = over_y(scaled, across)
+    panel = lax.all_gather(panel, "core", axis=0, tiled=True)
+    across = across.reshape(X // 2, 2 * width, height)
     part = jnp.einsum("br,kqr->kbq", panel, across, preferred_element_type=jnp.float32)
-    part = part.reshape(-1, CORES * width)
+    part = part.reshape(-1, 2 * width)
     depth = part.shape[0]
     piece = -(-depth // (2 * Z * 8)) * 8
     part = jnp.pad(part, ((0, 2 * Z * piece - depth), (0, 0)))
-    part = part.reshape(2, Z0, Z // Z0 * piece, CORES * width)
+    part = part.reshape(2, Z0, Z // Z0 * piece, 2 * width)
     leaving = lax.dynamic_index_in_dim(part, 1 - odd, 1, False)
     staying = lax.dynamic_index_in_dim(part, odd, 1, False)
     came = jnp.stack(
         [lax.ppermute(leaving[0], NEAR, EVEN_PAIRS), lax.ppermute(leaving[1], NEAR, ODD_PAIRS)]
     )
-    part = (staying + came).reshape(2, Z // Z0, piece, CORES * width).transpose(1, 0, 2, 3)
+    part = (staying + came).reshape(2, Z // Z0, piece, 2 * width).transpose(1, 0, 2, 3)
     gram = exchanged(part, ("zh", "z1")).sum(axis=0).astype(jnp.bfloat16)
-    gram = lax.all_gather(gram, RING, axis=0, tiled=False).reshape(Z // Z0, Z0, 2, piece, CORES * width)
-    gram = gram.transpose(2, 1, 0, 3, 4).reshape(-1, CORES * width)[:depth]
+    gram = lax.all_gather(gram, RING, axis=0, tiled=False).reshape(Z // Z0, Z0, 2, piece, 2 * width)
+    gram = gram.transpose(2, 1, 0, 3, 4).reshape(-1, 2 * width)[:depth]
 
-    gram = gram.reshape(X, -1, CORES * width)
+    gram = gram.reshape(X // 2, -1, 2 * width)
 
     def times_gram(rows):
         parts = jnp.einsum("kbq,br->kqr", gram, rows, preferred_element_type=jnp.float32)
-        return exchanged(parts.reshape(-1, width, height), ("x", "core")).sum(axis=0)
+        return exchanged(parts.reshape(X, width, height), "x").sum(axis=0)
 
     first_power = times_gram(panel).astype(jnp.bfloat16)
     panel, momentum_home = over_y(first_power, momentum_home)
-    second_power = times_gram(panel)
+    second_power = times_gram(lax.all_gather(panel, "core", axis=0, tiled=True))
     direction = (
         3.4445 * scaled.astype(jnp.float32)
         - 4.775 * first_power.astype(jnp.float32)

time: 241 us -> 233 us (0.967)
  waiting for transfers between devices: 38.1 us -> 29.9 us
  blocking collectives: 133 us -> 137 us
  starting transfers between devices: 54.7 us -> 51.6 us
    all_gather x1, blocking collectives: 17.6 us -> 28.1 us  [per_device(): lax.all_gather(gram, RING, axis=0, tiled=False)]
    all_to_all x5 -> x6, blocking collectives: 87.4 us -> 77.9 us  [exchanged(): return lax.all_to_all(pieces, axes, split_axis=0, concat_axis=0, tiled=True)]
    all_gather x2 -> x3, blocking collectives: 12.7 us -> 21.2 us  [the longest x1 10.4 us: per_device(): across = lax.all_gather(scaled, 'x', axis=0, tiled=True)]
    ppermute x1, waiting for transfers between devices: 10.6 us -> 3.17 us  [per_device(): kept = lax.ppermute(momentum.T, COLUMN, TO_WORK)]
    all_to_all x5 -> x4, starting transfers between devices: 29.2 us -> 22.6 us  [exchanged(): return lax.all_to_all(pieces, axes, split_axis=0, concat_axis=0, tiled=True)]
    ppermute x1, starting transfers between devices: 5.64 us -> 11.1 us  [per_device(): momentum_home = lax.ppermute(new_momentum, COLUMN, TO_HOME)]
    all_gather x1, blocking collectives: 15.2 us -> 9.97 us  [per_device(): halves = lax.all_gather(grad_out, 'zh', axis=0, tiled=False)]
    ppermute x1, waiting for transfers between devices: 0.01 us -> 4.01 us  [per_device(): lax.ppermute(leaving[0], NEAR, EVEN_PAIRS)]
  transfers between devices with their start and end apart: 10 -> 9, of which waited for: 7 -> 7; matrix products, arithmetic and copies ran while one was open for 0% -> 0% of each run, Pallas kernels for 0% -> 0%
where the time goes in v6:
time: 233 us; the launch traced here: 232 us
  blocking collectives  137 us (59%)
  starting transfers between devices  51.6 us (22%)
  waiting for transfers between devices  29.9 us (13%)
  local copies, waits for them, and re-layouts  5.71 us (2%)
  matrix products  3.64 us (2%)
    all_to_all x6, blocking collectives, exchanged(): return lax.all_to_all(pieces, axes, split_axis=0, concat_axis=0, tiled=True)  77.9 us
    all_gather x1, blocking collectives, per_device(): lax.all_gather(gram, RING, axis=0, tiled=False)  28.1 us
    all_to_all x4, starting transfers between devices, exchanged(): return lax.all_to_all(pieces, axes, split_axis=0, concat_axis=0, tiled=True)  22.6 us
    all_to_all x4, waiting for transfers between devices, exchanged(): return lax.all_to_all(pieces, axes, split_axis=0, concat_axis=0, tiled=True)  17 us
    ppermute x1, starting transfers between devices, per_device(): momentum_home = lax.ppermute(new_momentum, COLUMN, TO_HOME)  11.1 us
    all_gather x1, blocking collectives, per_device(): across = lax.all_gather(scaled, 'x', axis=0, tiled=True)  10.4 us
    all_gather x1, blocking collectives, per_device(): halves = lax.all_gather(grad_out, 'zh', axis=0, tiled=False)  9.97 us
    all_gather x1, blocking collectives, per_device(): second_power = times_gram(lax.all_gather(panel, 'core', axis=0, tiled=True))  8.28 us
  transfers between devices with their start and end apart: 9, of which 7 were waited for; matrix products, arithmetic and copies ran while one was open for 0% of the time, Pallas kernels for 0%

profile of v6, /device:TPU:1, one launch (start us, length us, event | category | flops | bytes accessed | tf_op | source)
XLA Modules:
  0.0 232.0 jit_solution(3246990788308374947)
XLA Ops:
  1.4 17.1 %all_to_all.50 = bf16[8,66,256]{2,1,0:T(8,128)(2,1)S(1)} all-to-all(bf16[8,66,256]{2,1,0:T(8,128)(2,1)S(1)} %broadcast_in_dim.8), channel_id=1, replica_groups=mesh['z1'=3,'z0'=2,'core'=2,'zh'=2,'y'=8,'x'=4] {'y'}, dimensions={0} | all-to-all | bytes 540672 | tf_op jit(solution)/shard_map/all_to_all | solution.py:46
  19.7 5.3 %all-to-all-start.1 = ((bf16[4,528,256]{2,1,0:T(8,128)(2,1)}), bf16[4,528,256]{2,1,0:T(8,128)(2,1)S(1)}, u32[]{:S(2)}, u32[]{:S(2)}) async-start(bf16[4,528,256]{2,1,0:T(8,128)(2,1)} %broadcast_in_dim.9), calls=%async_computation.1 | async-start | bytes 2162688 | tf_op jit(solution)/shard_map/all_to_all | solution.py:46
  25.0 6.8 %collective-permute-start = (f32[64,352]{1,0:T(8,128)S(1)}, f32[64,352]{1,0:T(8,128)S(1)}, u32[]{:S(2)}, u32[]{:S(2)}) collective-permute-start(f32[64,352]{1,0:T(8,128)S(1)} %bitcast.182), channel_id=1, source_target_pairs={{0,0},{384,32},{32,64},{416,96},{64,128},{448,160},{96,192},{480,2... | collective-permute-start | bytes 270344 | tf_op jit(solution)/shard_map/ppermute | solution.py:72
  31.9 10.0 %all-gather = bf16[128,256]{1,0:T(8,128)(2,1)S(1)} all-gather(bf16[64,256]{1,0:T(8,128)(2,1)S(1)} %bitcast.181), channel_id=2, replica_groups=mesh['z1'=3,'z0'=2,'core'=2,'zh'=2,'y'=8,'x'=4] {'zh'}, dimensions={0}, use_global_device_ids=true | all-gather | bytes 98304 | tf_op jit(solution)/shard_map/all_gather | solution.py:71
  41.8 3.2 %collective-permute-done = f32[64,352]{1,0:T(8,128)S(1)} collective-permute-done((f32[64,352]{1,0:T(8,128)S(1)}, f32[64,352]{1,0:T(8,128)S(1)}, u32[]{:S(2)}, u32[]{:S(2)}) %collective-permute-start) | collective-permute-done | bytes 90144 | tf_op jit(solution)/shard_map/ppermute | solution.py:72
  48.1 5.4 %all_to_all.51 = f32[2,6,64,352]{3,2,1,0:T(8,128)S(1)} all-to-all(f32[2,6,64,352]{3,2,1,0:T(8,128)S(1)} %bitcast.175), channel_id=1, replica_groups=mesh['z1'=3,'z0'=2,'core'=2,'zh'=2,'y'=8,'x'=4] {'core'}, dimensions={0} | all-to-all | bytes 2162688 | tf_op jit(solution)/shard_map/all_to_all | solution.py:46
  53.7 12.9 %all_to_all.52 = f32[2,3,64,352]{3,2,1,0:T(8,128)S(1)} all-to-all(f32[2,3,64,352]{3,2,1,0:T(8,128)S(1)} %copy.47), channel_id=1, replica_groups=mesh['z1'=3,'z0'=2,'core'=2,'zh'=2,'y'=8,'x'=4] {'z0'}, dimensions={0} | all-to-all | bytes 1081344 | tf_op jit(solution)/shard_map/all_to_all | solution.py:46
  67.3 10.0 %all-to-all-start.4 = ((f32[3,64,352]{2,1,0:T(8,128)}), f32[3,64,352]{2,1,0:T(8,128)S(1)}, u32[]{:S(2)}, u32[]{:S(2)}) async-start(f32[3,64,352]{2,1,0:T(8,128)} %reduce_sum.55), calls=%async_computation.4 | async-start | bytes 589824 | tf_op jit(solution)/shard_map/all_to_all | solution.py:46
  78.0 12.3 %all-to-all-done.4 = f32[3,64,352]{2,1,0:T(8,128)S(1)} async-done(((f32[3,64,352]{2,1,0:T(8,128)}), f32[3,64,352]{2,1,0:T(8,128)S(1)}, u32[]{:S(2)}, u32[]{:S(2)}) %all-to-all-start.4) | async-done | bytes 270368 | tf_op jit(solution)/shard_map/all_to_all | solution.py:46
  91.2 3.5 %all-to-all-start.5 = ((bf16[8,64,352]{2,1,0:T(8,128)(2,1)}), bf16[8,64,352]{2,1,0:T(8,128)(2,1)S(1)}, u32[]{:S(2)}, u32[]{:S(2)}) async-start(bf16[8,64,352]{2,1,0:T(8,128)(2,1)} %broadcast_in_dim.10), calls=%async_computation.5 | async-start | bytes 786432 | tf_op jit(solution)/shard_map/all_to_all | solution.py:46
  94.6 10.4 %all_gather.21 = bf16[256,352]{1,0:T(8,128)(2,1)S(1)} all-gather(bf16[64,352]{1,0:T(8,128)(2,1)S(1)} %get-tuple-element.16), channel_id=1, replica_groups=mesh['z1'=3,'z0'=2,'core'=2,'zh'=2,'y'=8,'x'=4] {'x'}, dimensions={0}, use_global_device_ids=true | all-gather | bytes 225280 | tf_op jit(solution)/shard_map/all_gather | solution.py:90
  105.1 4.6 %all-to-all-done.5 = bf16[8,64,352]{2,1,0:T(8,128)(2,1)S(1)} async-done(((bf16[8,64,352]{2,1,0:T(8,128)(2,1)}), bf16[8,64,352]{2,1,0:T(8,128)(2,1)S(1)}, u32[]{:S(2)}, u32[]{:S(2)}) %all-to-all-start.5) | async-done | bytes 360480 | tf_op jit(solution)/shard_map/all_to_all | solution.py:46
  109.7 2.5 %all_gather.22 = bf16[1024,352]{1,0:T(8,128)(2,1)S(1)} all-gather(bf16[512,352]{1,0:T(8,128)(2,1)S(1)} %bitcast.173), channel_id=1, replica_groups=mesh['z1'=3,'z0'=2,'core'=2,'zh'=2,'y'=8,'x'=4] {'core'}, dimensions={0}, use_global_device_ids=true | all-gather | bytes 1081344 | tf_op jit(solution)/shard_map/all_gather | solution.py:92
  115.0 3.6 %collective-permute-start.2 = (f32[528,128]{1,0:T(8,128)S(1)}, f32[528,128]{1,0:T(8,128)S(1)}, u32[]{:S(2)}, u32[]{:S(2)}) collective-permute-start(f32[528,128]{1,0:T(8,128)S(1)} %get-tuple-element.19), channel_id=1, source_target_pairs={{0,672},{128,256},{256,128},{384,512},{512,384},{640,32},{32,640},... | collective-permute-start | bytes 811016 | tf_op jit(solution)/shard_map/ppermute | solution.py:103
  118.7 4.0 %collective-permute-done.1 = f32[528,128]{1,0:T(8,128)S(1)} collective-permute-done((f32[528,128]{1,0:T(8,128)S(1)}, f32[528,128]{1,0:T(8,128)S(1)}, u32[]{:S(2)}, u32[]{:S(2)}) %collective-permute-start.1) | collective-permute-done | bytes 270368 | tf_op jit(solution)/shard_map/ppermute | solution.py:103
  122.7 3.1 %collective-permute-done.2 = f32[528,128]{1,0:T(8,128)S(1)} collective-permute-done((f32[528,128]{1,0:T(8,128)S(1)}, f32[528,128]{1,0:T(8,128)S(1)}, u32[]{:S(2)}, u32[]{:S(2)}) %collective-permute-start.2) | collective-permute-done | bytes 270368 | tf_op jit(solution)/shard_map/ppermute | solution.py:103
  126.0 21.9 %all_to_all.53 = f32[6,2,88,128]{3,2,1,0:T(8,128)S(1)} all-to-all(f32[6,2,88,128]{3,2,1,0:T(8,128)S(1)} %copy.52), channel_id=1, replica_groups=mesh['z1'=3,'z0'=2,'core'=2,'zh'=2,'y'=8,'x'=4] {'zh','z1'}, dimensions={0} | all-to-all | bytes 1081344 | tf_op jit(solution)/shard_map/all_to_all | solution.py:46
  147.9 28.1 %all-gather.1 = bf16[24,88,128]{2,1,0:T(8,128)(2,1)S(1)} all-gather(bf16[2,88,128]{2,1,0:T(8,128)(2,1)S(1)} %reduce_sum.57), channel_id=3, replica_groups=mesh['z1'=3,'z0'=2,'core'=2,'zh'=2,'y'=8,'x'=4] {'zh','z1','z0'}, dimensions={0}, use_global_device_ids=true | all-gather | bytes 585728 | tf_op jit(solution)/shard_map/all_gather | solution.py:107
  176.7 10.3 %all_to_all.54 = f32[4,64,352]{2,1,0:T(8,128)S(1)} all-to-all(f32[4,64,352]{2,1,0:T(8,128)S(1)} %fusion.14), channel_id=1, replica_groups=mesh['z1'=3,'z0'=2,'core'=2,'zh'=2,'y'=8,'x'=4] {'x'}, dimensions={0} | all-to-all | bytes 720896 | tf_op jit(solution)/shard_map/all_to_all | solution.py:46
  187.8 3.9 %all-to-all-start.8 = ((bf16[8,64,352]{2,1,0:T(8,128)(2,1)}), bf16[8,64,352]{2,1,0:T(8,128)(2,1)S(1)}, u32[]{:S(2)}, u32[]{:S(2)}) async-start(bf16[8,64,352]{2,1,0:T(8,128)(2,1)} %broadcast_in_dim.11), calls=%async_computation.8 | async-start | bytes 786432 | tf_op jit(solution)/shard_map/all_to_all | solution.py:46
  191.6 11.1 %collective-permute-start.3 = (f32[64,352]{1,0:T(8,128)S(1)}, f32[64,352]{1,0:T(8,128)S(1)}, u32[]{:S(2)}, u32[]{:S(2)}) collective-permute-start(f32[64,352]{1,0:T(8,128)S(1)} %get-tuple-element.17), channel_id=1, source_target_pairs={{0,0},{32,384},{64,32},{96,416},{128,64},{160,448},{192,96},{224,4... | collective-permute-start | bytes 270344 | tf_op jit(solution)/shard_map/ppermute | solution.py:88
  204.4 8.3 %all_gather.24 = bf16[1024,352]{1,0:T(8,128)(2,1)S(1)} all-gather(bf16[512,352]{1,0:T(8,128)(2,1)S(1)} %bitcast.174), channel_id=1, replica_groups=mesh['z1'=3,'z0'=2,'core'=2,'zh'=2,'y'=8,'x'=4] {'core'}, dimensions={0}, use_global_device_ids=true | all-gather | bytes 1081344 | tf_op jit(solution)/shard_map/all_gather | solution.py:118
  213.1 10.4 %all_to_all.55 = f32[4,64,352]{2,1,0:T(8,128)S(1)} all-to-all(f32[4,64,352]{2,1,0:T(8,128)S(1)} %fusion.12), channel_id=1, replica_groups=mesh['z1'=3,'z0'=2,'core'=2,'zh'=2,'y'=8,'x'=4] {'x'}, dimensions={0} | all-to-all | bytes 720896 | tf_op jit(solution)/shard_map/all_to_all | solution.py:46
  223.5 5.5 %collective-permute-start.4 = (f32[64,352]{1,0:T(8,128)S(1)}, f32[64,352]{1,0:T(8,128)S(1)}, u32[]{:S(2)}, u32[]{:S(2)}) collective-permute-start(f32[64,352]{1,0:T(8,128)S(1)} %multiply_add_fusion), channel_id=1, source_target_pairs={{0,0},{32,384},{64,32},{96,416},{128,64},{160,448},{192,96},{224,4... | collective-permute-start | bytes 270344 | tf_op jit(solution)/shard_map/ppermute | solution.py:124
  (54 shorter events, 15.6 us)
Async XLA Ops:
  19.7 5.3 %copy-start.2 = (f32[352,64]{0,1:T(8,128)S(1)}, f32[352,64]{0,1:T(8,128)}, u32[]{:S(2)}) copy-start(f32[352,64]{0,1:T(8,128)} %param.8) | copy-start | bytes 270340
  19.7 12.2 %copy-start.1 = (bf16[256,64]{0,1:T(8,128)(2,1)S(1)}, bf16[256,64]{0,1:T(8,128)(2,1)}, u32[]{:S(2)}) copy-start(bf16[256,64]{0,1:T(8,128)(2,1)} %param.7) | copy-start | bytes 98308
  19.7 25.3 %all-to-all-start.1 = ((bf16[4,528,256]{2,1,0:T(8,128)(2,1)}), bf16[4,528,256]{2,1,0:T(8,128)(2,1)S(1)}, u32[]{:S(2)}, u32[]{:S(2)}) async-start(bf16[4,528,256]{2,1,0:T(8,128)(2,1)} %broadcast_in_dim.9), calls=%async_computation.1 | async-start | bytes 2162688 | tf_op jit(solution)/shard_map/all_to_all | solution.py:46
  25.0 20.0 %collective-permute-start = (f32[64,352]{1,0:T(8,128)S(1)}, f32[64,352]{1,0:T(8,128)S(1)}, u32[]{:S(2)}, u32[]{:S(2)}) collective-permute-start(f32[64,352]{1,0:T(8,128)S(1)} %bitcast.182), channel_id=1, source_target_pairs={{0,0},{384,32},{32,64},{416,96},{64,128},{448,160},{96,192},{480,2... | collective-permute-start | bytes 270344 | tf_op jit(solution)/shard_map/ppermute | solution.py:72
  67.3 23.0 %all-to-all-start.4 = ((f32[3,64,352]{2,1,0:T(8,128)}), f32[3,64,352]{2,1,0:T(8,128)S(1)}, u32[]{:S(2)}, u32[]{:S(2)}) async-start(f32[3,64,352]{2,1,0:T(8,128)} %reduce_sum.55), calls=%async_computation.4 | async-start | bytes 589824 | tf_op jit(solution)/shard_map/all_to_all | solution.py:46
  91.2 18.5 %all-to-all-start.5 = ((bf16[8,64,352]{2,1,0:T(8,128)(2,1)}), bf16[8,64,352]{2,1,0:T(8,128)(2,1)S(1)}, u32[]{:S(2)}, u32[]{:S(2)}) async-start(bf16[8,64,352]{2,1,0:T(8,128)(2,1)} %broadcast_in_dim.10), calls=%async_computation.5 | async-start | bytes 786432 | tf_op jit(solution)/shard_map/all_to_all | solution.py:46
  113.1 9.6 %collective-permute-start.1 = (f32[528,128]{1,0:T(8,128)S(1)}, f32[528,128]{1,0:T(8,128)S(1)}, u32[]{:S(2)}, u32[]{:S(2)}) collective-permute-start(f32[528,128]{1,0:T(8,128)S(1)} %get-tuple-element.18), channel_id=1, source_target_pairs={{0,128},{128,0},{256,384},{384,256},{512,640},{640,512},{32,160},{... | collective-permute-start | bytes 811016 | tf_op jit(solution)/shard_map/ppermute | solution.py:103
  115.0 10.8 %collective-permute-start.2 = (f32[528,128]{1,0:T(8,128)S(1)}, f32[528,128]{1,0:T(8,128)S(1)}, u32[]{:S(2)}, u32[]{:S(2)}) collective-permute-start(f32[528,128]{1,0:T(8,128)S(1)} %get-tuple-element.19), channel_id=1, source_target_pairs={{0,672},{128,256},{256,128},{384,512},{512,384},{640,32},{32,640},... | collective-permute-start | bytes 811016 | tf_op jit(solution)/shard_map/ppermute | solution.py:103
  187.8 16.6 %all-to-all-start.8 = ((bf16[8,64,352]{2,1,0:T(8,128)(2,1)}), bf16[8,64,352]{2,1,0:T(8,128)(2,1)S(1)}, u32[]{:S(2)}, u32[]{:S(2)}) async-start(bf16[8,64,352]{2,1,0:T(8,128)(2,1)} %broadcast_in_dim.11), calls=%async_computation.8 | async-start | bytes 786432 | tf_op jit(solution)/shard_map/all_to_all | solution.py:46
  191.6 12.7 %collective-permute-start.3 = (f32[64,352]{1,0:T(8,128)S(1)}, f32[64,352]{1,0:T(8,128)S(1)}, u32[]{:S(2)}, u32[]{:S(2)}) collective-permute-start(f32[64,352]{1,0:T(8,128)S(1)} %get-tuple-element.17), channel_id=1, source_target_pairs={{0,0},{32,384},{64,32},{96,416},{128,64},{160,448},{192,96},{224,4... | collective-permute-start | bytes 270344 | tf_op jit(solution)/shard_map/ppermute | solution.py:88
  213.1 17.6 %copy-start = (f32[352,64]{0,1:T(8,128)S(1)}, f32[352,64]{0,1:T(8,128)}, u32[]{:S(2)}) copy-start(f32[352,64]{0,1:T(8,128)} %param.9) | copy-start | bytes 270340
  223.5 7.2 %collective-permute-start.4 = (f32[64,352]{1,0:T(8,128)S(1)}, f32[64,352]{1,0:T(8,128)S(1)}, u32[]{:S(2)}, u32[]{:S(2)}) collective-permute-start(f32[64,352]{1,0:T(8,128)S(1)} %multiply_add_fusion), channel_id=1, source_target_pairs={{0,0},{32,384},{64,32},{96,416},{128,64},{160,448},{192,96},{224,4... | collective-permute-start | bytes 270344 | tf_op jit(solution)/shard_map/ppermute | solution.py:124

commit v7 on v6

--- a/solution.py
+++ b/solution.py
@@ -71,14 +71,12 @@
     halves = lax.all_gather(grad_out, "zh", axis=0, tiled=False)
     kept = lax.ppermute(momentum.T, COLUMN, TO_WORK)
 
-    act, kept, halves = over_x(over_y(act)[0], kept, halves)
+    act, halves = over_x(over_y(act)[0], halves)
     act = act.reshape(X, Y, features, tokens)
     act = act.transpose(1, 0, 2, 3).reshape(ZL, -1, tokens)
-    part = jnp.stack(
-        [contract(half, act[k], ((1,), (1,))) for half in halves for k in range(ZL)]
-    )
-    width, height = part.shape[1:]
-    part = exchanged(part.reshape(CORES, ZL, width, height), "core").sum(axis=0)
+    part = jnp.einsum("cqk,grk->cgqr", halves, act, preferred_element_type=jnp.float32)
+    width, height = part.shape[2:]
+    part = exchanged(part, "core").sum(axis=0)
     part = part.reshape(Z1, Z0, width, height).transpose(1, 0, 2, 3)
     part = exchanged(part, "z0").sum(axis=0)
     gradient = exchanged(part, "z1").sum(axis=0)
@@ -103,10 +101,9 @@
         [lax.ppermute(leaving[0], NEAR, EVEN_PAIRS), lax.ppermute(leaving[1], NEAR, ODD_PAIRS)]
     )
     part = (staying + came).reshape(2, Z // Z0, piece, 2 * width).transpose(1, 0, 2, 3)
-    gram = exchanged(part, ("zh", "z1")).sum(axis=0).astype(jnp.bfloat16)
-    gram = lax.all_gather(gram, RING, axis=0, tiled=False).reshape(Z // Z0, Z0, 2, piece, 2 * width)
-    gram = gram.transpose(2, 1, 0, 3, 4).reshape(-1, 2 * width)[:depth]
-
+    gram = exchanged(part, ("z1", "zh")).sum(axis=0).astype(jnp.bfloat16)
+    gram = lax.all_gather(gram, RING, axis=0, tiled=False).reshape(ZH, Z1, Z0, 2, piece, 2 * width)
+    gram = gram.transpose(3, 2, 1, 0, 4, 5).reshape(-1, 2 * width)[:depth]
     gram = gram.reshape(X // 2, -1, 2 * width)
 
     def times_gram(rows):

time: 233 us -> 230 us (0.987)
  waiting for transfers between devices: 29.9 us -> 25.9 us
  blocking collectives: 137 us -> 140 us
    all_gather x1, blocking collectives: 9.97 us -> 14.9 us  [per_device(): halves = lax.all_gather(grad_out, 'zh', axis=0, tiled=False)]
    ppermute x1, waiting for transfers between devices: 4.01 us -> 0.54 us  [per_device(): lax.ppermute(leaving[0], NEAR, EVEN_PAIRS)]
    ppermute x1, starting transfers between devices: 3.59 us -> 7.06 us  [per_device(): lax.ppermute(leaving[1], NEAR, ODD_PAIRS)]
    ppermute x1, starting transfers between devices: 6.85 us -> 3.59 us  [per_device(): kept = lax.ppermute(momentum.T, COLUMN, TO_WORK)]
    ppermute x1, waiting for transfers between devices: 3.17 us -> 0.01 us  [per_device(): kept = lax.ppermute(momentum.T, COLUMN, TO_WORK)]
    all_gather x1, blocking collectives: 28.1 us -> 25.6 us  [per_device(): lax.all_gather(gram, RING, axis=0, tiled=False)]
    ppermute x1, waiting for transfers between devices: 3.14 us -> 5.62 us  [per_device(): lax.ppermute(leaving[1], NEAR, ODD_PAIRS)]
  transfers between devices with their start and end apart: 9 -> 9, of which waited for: 7 -> 6; matrix products, arithmetic and copies ran while one was open for 0% -> 0% of each run, Pallas kernels for 0% -> 0%
where the time goes in v7:
time: 230 us; the launch traced here: 229 us
  blocking collectives  140 us (61%)
  starting transfers between devices  52 us (23%)
  waiting for transfers between devices  25.9 us (11%)
  local copies, waits for them, and re-layouts  5.79 us (3%)
    all_to_all x6, blocking collectives, exchanged(): return lax.all_to_all(pieces, axes, split_axis=0, concat_axis=0, tiled=True)  78.7 us
    all_gather x1, blocking collectives, per_device(): lax.all_gather(gram, RING, axis=0, tiled=False)  25.6 us
    all_to_all x4, starting transfers between devices, exchanged(): return lax.all_to_all(pieces, axes, split_axis=0, concat_axis=0, tiled=True)  20.7 us
    all_to_all x4, waiting for transfers between devices, exchanged(): return lax.all_to_all(pieces, axes, split_axis=0, concat_axis=0, tiled=True)  17.1 us
    all_gather x1, blocking collectives, per_device(): halves = lax.all_gather(grad_out, 'zh', axis=0, tiled=False)  14.9 us
    ppermute x1, starting transfers between devices, per_device(): momentum_home = lax.ppermute(new_momentum, COLUMN, TO_HOME)  13 us
    all_gather x1, blocking collectives, per_device(): across = lax.all_gather(scaled, 'x', axis=0, tiled=True)  9.83 us
    all_gather x1, blocking collectives, per_device(): second_power = times_gram(lax.all_gather(panel, 'core', axis=0, tiled=True))  8.03 us
  transfers between devices with their start and end apart: 9, of which 6 were waited for; matrix products, arithmetic and copies ran while one was open for 0% of the time, Pallas kernels for 0%

profile of v7, /device:TPU:1, one launch (start us, length us, event | category | flops | bytes accessed | tf_op | source)
XLA Modules:
  0.0 228.9 jit_solution(8223410684752313315)
XLA Ops:
  1.4 17.1 %all_to_all.50 = bf16[8,66,256]{2,1,0:T(8,128)(2,1)S(1)} all-to-all(bf16[8,66,256]{2,1,0:T(8,128)(2,1)S(1)} %broadcast_in_dim.8), channel_id=1, replica_groups=mesh['z1'=3,'z0'=2,'core'=2,'zh'=2,'y'=8,'x'=4] {'y'}, dimensions={0} | all-to-all | bytes 540672 | tf_op jit(solution)/shard_map/all_to_all | solution.py:46
  19.7 5.3 %all-to-all-start.1 = ((bf16[4,528,256]{2,1,0:T(8,128)(2,1)}), bf16[4,528,256]{2,1,0:T(8,128)(2,1)S(1)}, u32[]{:S(2)}, u32[]{:S(2)}) async-start(bf16[4,528,256]{2,1,0:T(8,128)(2,1)} %broadcast_in_dim.9), calls=%async_computation.1 | async-start | bytes 2162688 | tf_op jit(solution)/shard_map/all_to_all | solution.py:46
  25.0 14.9 %all-gather = bf16[128,256]{1,0:T(8,128)(2,1)S(1)} all-gather(bf16[64,256]{1,0:T(8,128)(2,1)S(1)} %bitcast.78), channel_id=2, replica_groups=mesh['z1'=3,'z0'=2,'core'=2,'zh'=2,'y'=8,'x'=4] {'zh'}, dimensions={0}, use_global_device_ids=true | all-gather | bytes 98304 | tf_op jit(solution)/shard_map/all_gather | solution.py:71
  41.3 8.2 %all_to_all.51 = f32[2,6,64,352]{3,2,1,0:T(8,128)S(1)} all-to-all(f32[2,6,64,352]{3,2,1,0:T(8,128)S(1)} %copy.50), channel_id=1, replica_groups=mesh['z1'=3,'z0'=2,'core'=2,'zh'=2,'y'=8,'x'=4] {'core'}, dimensions={0} | all-to-all | bytes 2162688 | tf_op jit(solution)/shard_map/all_to_all | solution.py:46
  49.6 10.8 %all_to_all.52 = f32[2,3,64,352]{3,2,1,0:T(8,128)S(1)} all-to-all(f32[2,3,64,352]{3,2,1,0:T(8,128)S(1)} %copy.51), channel_id=1, replica_groups=mesh['z1'=3,'z0'=2,'core'=2,'zh'=2,'y'=8,'x'=4] {'z0'}, dimensions={0} | all-to-all | bytes 1081344 | tf_op jit(solution)/shard_map/all_to_all | solution.py:46
  61.2 8.2 %all-to-all-start.4 = ((f32[3,64,352]{2,1,0:T(8,128)}), f32[3,64,352]{2,1,0:T(8,128)S(1)}, u32[]{:S(2)}, u32[]{:S(2)}) async-start(f32[3,64,352]{2,1,0:T(8,128)} %reduce_sum.55), calls=%async_computation.4 | async-start | bytes 589824 | tf_op jit(solution)/shard_map/all_to_all | solution.py:46
  69.4 3.6 %collective-permute-start = (f32[64,352]{1,0:T(8,128)S(1)}, f32[64,352]{1,0:T(8,128)S(1)}, u32[]{:S(2)}, u32[]{:S(2)}) collective-permute-start(f32[64,352]{1,0:T(8,128)S(1)} %bitcast.79), channel_id=1, source_target_pairs={{0,0},{384,32},{32,64},{416,96},{64,128},{448,160},{96,192},{480,2... | collective-permute-start | bytes 270344 | tf_op jit(solution)/shard_map/ppermute | solution.py:72
  73.7 11.9 %all-to-all-done.4 = f32[3,64,352]{2,1,0:T(8,128)S(1)} async-done(((f32[3,64,352]{2,1,0:T(8,128)}), f32[3,64,352]{2,1,0:T(8,128)S(1)}, u32[]{:S(2)}, u32[]{:S(2)}) %all-to-all-start.4) | async-done | bytes 270368 | tf_op jit(solution)/shard_map/all_to_all | solution.py:46
  86.4 3.5 %all-to-all-start.5 = ((bf16[8,64,352]{2,1,0:T(8,128)(2,1)}), bf16[8,64,352]{2,1,0:T(8,128)(2,1)S(1)}, u32[]{:S(2)}, u32[]{:S(2)}) async-start(bf16[8,64,352]{2,1,0:T(8,128)(2,1)} %broadcast_in_dim.10), calls=%async_computation.5 | async-start | bytes 786432 | tf_op jit(solution)/shard_map/all_to_all | solution.py:46
  89.9 9.8 %all_gather.21 = bf16[256,352]{1,0:T(8,128)(2,1)S(1)} all-gather(bf16[64,352]{1,0:T(8,128)(2,1)S(1)} %get-tuple-element.14), channel_id=1, replica_groups=mesh['z1'=3,'z0'=2,'core'=2,'zh'=2,'y'=8,'x'=4] {'x'}, dimensions={0}, use_global_device_ids=true | all-gather | bytes 225280 | tf_op jit(solution)/shard_map/all_gather | solution.py:88
  99.7 5.2 %all-to-all-done.5 = bf16[8,64,352]{2,1,0:T(8,128)(2,1)S(1)} async-done(((bf16[8,64,352]{2,1,0:T(8,128)(2,1)}), bf16[8,64,352]{2,1,0:T(8,128)(2,1)S(1)}, u32[]{:S(2)}, u32[]{:S(2)}) %all-to-all-start.5) | async-done | bytes 360480 | tf_op jit(solution)/shard_map/all_to_all | solution.py:46
  104.9 2.5 %all_gather.22 = bf16[1024,352]{1,0:T(8,128)(2,1)S(1)} all-gather(bf16[512,352]{1,0:T(8,128)(2,1)S(1)} %bitcast.70), channel_id=1, replica_groups=mesh['z1'=3,'z0'=2,'core'=2,'zh'=2,'y'=8,'x'=4] {'core'}, dimensions={0}, use_global_device_ids=true | all-gather | bytes 1081344 | tf_op jit(solution)/shard_map/all_gather | solution.py:90
  108.3 1.9 collective-permute-start.1
  110.3 7.1 %collective-permute-start.2 = (f32[528,128]{1,0:T(8,128)S(1)}, f32[528,128]{1,0:T(8,128)S(1)}, u32[]{:S(2)}, u32[]{:S(2)}) collective-permute-start(f32[528,128]{1,0:T(8,128)S(1)} %get-tuple-element.17), channel_id=1, source_target_pairs={{0,672},{128,256},{256,128},{384,512},{512,384},{640,32},{32,640},... | collective-permute-start | bytes 811016 | tf_op jit(solution)/shard_map/ppermute | solution.py:101
  117.9 5.6 %collective-permute-done.2 = f32[528,128]{1,0:T(8,128)S(1)} collective-permute-done((f32[528,128]{1,0:T(8,128)S(1)}, f32[528,128]{1,0:T(8,128)S(1)}, u32[]{:S(2)}, u32[]{:S(2)}) %collective-permute-start.2) | collective-permute-done | bytes 270368 | tf_op jit(solution)/shard_map/ppermute | solution.py:101
  123.7 23.4 %all_to_all.53 = f32[6,2,88,128]{3,2,1,0:T(8,128)S(1)} all-to-all(f32[6,2,88,128]{3,2,1,0:T(8,128)S(1)} %copy.56), channel_id=1, replica_groups=mesh['z1'=3,'z0'=2,'core'=2,'zh'=2,'y'=8,'x'=4] {'z1','zh'}, dimensions={0} | all-to-all | bytes 1081344 | tf_op jit(solution)/shard_map/all_to_all | solution.py:46
  147.1 25.6 %all-gather.1 = bf16[24,88,128]{2,1,0:T(8,128)(2,1)S(1)} all-gather(bf16[2,88,128]{2,1,0:T(8,128)(2,1)S(1)} %reduce_sum.57), channel_id=3, replica_groups=mesh['z1'=3,'z0'=2,'core'=2,'zh'=2,'y'=8,'x'=4] {'zh','z1','z0'}, dimensions={0}, use_global_device_ids=true | all-gather | bytes 585728 | tf_op jit(solution)/shard_map/all_gather | solution.py:105
  173.4 8.8 %all_to_all.54 = f32[4,64,352]{2,1,0:T(8,128)S(1)} all-to-all(f32[4,64,352]{2,1,0:T(8,128)S(1)} %fusion.3), channel_id=1, replica_groups=mesh['z1'=3,'z0'=2,'core'=2,'zh'=2,'y'=8,'x'=4] {'x'}, dimensions={0} | all-to-all | bytes 720896 | tf_op jit(solution)/shard_map/all_to_all | solution.py:46
  183.0 3.7 %all-to-all-start.8 = ((bf16[8,64,352]{2,1,0:T(8,128)(2,1)}), bf16[8,64,352]{2,1,0:T(8,128)(2,1)S(1)}, u32[]{:S(2)}, u32[]{:S(2)}) async-start(bf16[8,64,352]{2,1,0:T(8,128)(2,1)} %broadcast_in_dim.11), calls=%async_computation.8 | async-start | bytes 786432 | tf_op jit(solution)/shard_map/all_to_all | solution.py:46
  186.8 13.0 %collective-permute-start.3 = (f32[64,352]{1,0:T(8,128)S(1)}, f32[64,352]{1,0:T(8,128)S(1)}, u32[]{:S(2)}, u32[]{:S(2)}) collective-permute-start(f32[64,352]{1,0:T(8,128)S(1)} %get-tuple-element.15), channel_id=1, source_target_pairs={{0,0},{32,384},{64,32},{96,416},{128,64},{160,448},{192,96},{224,4... | collective-permute-start | bytes 270344 | tf_op jit(solution)/shard_map/ppermute | solution.py:86
  199.7 1.6 collective-permute-done.3
  201.3 8.0 %all_gather.24 = bf16[1024,352]{1,0:T(8,128)(2,1)S(1)} all-gather(bf16[512,352]{1,0:T(8,128)(2,1)S(1)} %bitcast.71), channel_id=1, replica_groups=mesh['z1'=3,'z0'=2,'core'=2,'zh'=2,'y'=8,'x'=4] {'core'}, dimensions={0}, use_global_device_ids=true | all-gather | bytes 1081344 | tf_op jit(solution)/shard_map/all_gather | solution.py:115
  209.8 10.4 %all_to_all.55 = f32[4,64,352]{2,1,0:T(8,128)S(1)} all-to-all(f32[4,64,352]{2,1,0:T(8,128)S(1)} %fusion.1), channel_id=1, replica_groups=mesh['z1'=3,'z0'=2,'core'=2,'zh'=2,'y'=8,'x'=4] {'x'}, dimensions={0} | all-to-all | bytes 720896 | tf_op jit(solution)/shard_map/all_to_all | solution.py:46
  220.2 5.8 %collective-permute-start.4 = (f32[64,352]{1,0:T(8,128)S(1)}, f32[64,352]{1,0:T(8,128)S(1)}, u32[]{:S(2)}, u32[]{:S(2)}) collective-permute-start(f32[64,352]{1,0:T(8,128)S(1)} %multiply_add_fusion), channel_id=1, source_target_pairs={{0,0},{32,384},{64,32},{96,416},{128,64},{160,448},{192,96},{224,4... | collective-permute-start | bytes 270344 | tf_op jit(solution)/shard_map/ppermute | solution.py:121
  (44 shorter events, 10.9 us)
Async XLA Ops:
  19.7 5.3 %copy-start.1 = (bf16[256,64]{0,1:T(8,128)(2,1)S(1)}, bf16[256,64]{0,1:T(8,128)(2,1)}, u32[]{:S(2)}) copy-start(bf16[256,64]{0,1:T(8,128)(2,1)} %param.7) | copy-start | bytes 98308
  19.7 20.2 %all-to-all-start.1 = ((bf16[4,528,256]{2,1,0:T(8,128)(2,1)}), bf16[4,528,256]{2,1,0:T(8,128)(2,1)S(1)}, u32[]{:S(2)}, u32[]{:S(2)}) async-start(bf16[4,528,256]{2,1,0:T(8,128)(2,1)} %broadcast_in_dim.9), calls=%async_computation.1 | async-start | bytes 2162688 | tf_op jit(solution)/shard_map/all_to_all | solution.py:46
  49.6 19.8 %copy-start.2 = (f32[352,64]{0,1:T(8,128)S(1)}, f32[352,64]{0,1:T(8,128)}, u32[]{:S(2)}) copy-start(f32[352,64]{0,1:T(8,128)} %param.8) | copy-start | bytes 270340
  61.2 24.4 %all-to-all-start.4 = ((f32[3,64,352]{2,1,0:T(8,128)}), f32[3,64,352]{2,1,0:T(8,128)S(1)}, u32[]{:S(2)}, u32[]{:S(2)}) async-start(f32[3,64,352]{2,1,0:T(8,128)} %reduce_sum.55), calls=%async_computation.4 | async-start | bytes 589824 | tf_op jit(solution)/shard_map/all_to_all | solution.py:46
  69.4 16.2 %collective-permute-start = (f32[64,352]{1,0:T(8,128)S(1)}, f32[64,352]{1,0:T(8,128)S(1)}, u32[]{:S(2)}, u32[]{:S(2)}) collective-permute-start(f32[64,352]{1,0:T(8,128)S(1)} %bitcast.79), channel_id=1, source_target_pairs={{0,0},{384,32},{32,64},{416,96},{64,128},{448,160},{96,192},{480,2... | collective-permute-start | bytes 270344 | tf_op jit(solution)/shard_map/ppermute | solution.py:72
  86.4 18.5 %all-to-all-start.5 = ((bf16[8,64,352]{2,1,0:T(8,128)(2,1)}), bf16[8,64,352]{2,1,0:T(8,128)(2,1)S(1)}, u32[]{:S(2)}, u32[]{:S(2)}) async-start(bf16[8,64,352]{2,1,0:T(8,128)(2,1)} %broadcast_in_dim.10), calls=%async_computation.5 | async-start | bytes 786432 | tf_op jit(solution)/shard_map/all_to_all | solution.py:46
  108.3 9.6 %collective-permute-start.1 = (f32[528,128]{1,0:T(8,128)S(1)}, f32[528,128]{1,0:T(8,128)S(1)}, u32[]{:S(2)}, u32[]{:S(2)}) collective-permute-start(f32[528,128]{1,0:T(8,128)S(1)} %get-tuple-element.16), channel_id=1, source_target_pairs={{0,128},{128,0},{256,384},{384,256},{512,640},{640,512},{32,160},{... | collective-permute-start | bytes 811016 | tf_op jit(solution)/shard_map/ppermute | solution.py:101
  110.3 13.3 %collective-permute-start.2 = (f32[528,128]{1,0:T(8,128)S(1)}, f32[528,128]{1,0:T(8,128)S(1)}, u32[]{:S(2)}, u32[]{:S(2)}) collective-permute-start(f32[528,128]{1,0:T(8,128)S(1)} %get-tuple-element.17), channel_id=1, source_target_pairs={{0,672},{128,256},{256,128},{384,512},{512,384},{640,32},{32,640},... | collective-permute-start | bytes 811016 | tf_op jit(solution)/shard_map/ppermute | solution.py:101
  183.0 18.3 %all-to-all-start.8 = ((bf16[8,64,352]{2,1,0:T(8,128)(2,1)}), bf16[8,64,352]{2,1,0:T(8,128)(2,1)S(1)}, u32[]{:S(2)}, u32[]{:S(2)}) async-start(bf16[8,64,352]{2,1,0:T(8,128)(2,1)} %broadcast_in_dim.11), calls=%async_computation.8 | async-start | bytes 786432 | tf_op jit(solution)/shard_map/all_to_all | solution.py:46
  186.8 14.6 %collective-permute-start.3 = (f32[64,352]{1,0:T(8,128)S(1)}, f32[64,352]{1,0:T(8,128)S(1)}, u32[]{:S(2)}, u32[]{:S(2)}) collective-permute-start(f32[64,352]{1,0:T(8,128)S(1)} %get-tuple-element.15), channel_id=1, source_target_pairs={{0,0},{32,384},{64,32},{96,416},{128,64},{160,448},{192,96},{224,4... | collective-permute-start | bytes 270344 | tf_op jit(solution)/shard_map/ppermute | solution.py:86
  209.8 17.8 %copy-start = (f32[352,64]{0,1:T(8,128)S(1)}, f32[352,64]{0,1:T(8,128)}, u32[]{:S(2)}) copy-start(f32[352,64]{0,1:T(8,128)} %param.9) | copy-start | bytes 270340
  220.2 7.4 %collective-permute-start.4 = (f32[64,352]{1,0:T(8,128)S(1)}, f32[64,352]{1,0:T(8,128)S(1)}, u32[]{:S(2)}, u32[]{:S(2)}) collective-permute-start(f32[64,352]{1,0:T(8,128)S(1)} %multiply_add_fusion), channel_id=1, source_target_pairs={{0,0},{32,384},{64,32},{96,416},{128,64},{160,448},{192,96},{224,4... | collective-permute-start | bytes 270344 | tf_op jit(solution)/shard_map/ppermute | solution.py:121

commit v8 on v7

--- a/solution.py
+++ b/solution.py
@@ -78,8 +78,14 @@
     width, height = part.shape[2:]
     part = exchanged(part, "core").sum(axis=0)
     part = part.reshape(Z1, Z0, width, height).transpose(1, 0, 2, 3)
-    part = exchanged(part, "z0").sum(axis=0)
-    gradient = exchanged(part, "z1").sum(axis=0)
+    leaving = lax.dynamic_index_in_dim(part, 1 - odd, 0, False)
+    part = lax.dynamic_index_in_dim(part, odd, 0, False)
+    part += lax.ppermute(leaving, "z0", [(0, 1), (1, 0)])
+    third = lax.axis_index("z1")
+    gradient = lax.dynamic_index_in_dim(part, third, 0, False)
+    for ahead in range(1, Z1):
+        leaving = lax.dynamic_index_in_dim(part, (third + ahead) % Z1, 0, False)
+        gradient += lax.ppermute(leaving, "z1", [(k, (k + ahead) % Z1) for k in range(Z1)])
 
     new_momentum = 0.95 * kept + gradient
     scaled = (new_momentum / norm_scale).astype(jnp.bfloat16)

time: 230 us -> 225 us (0.978)
  starting transfers between devices: 52 us -> 59.9 us
  blocking collectives: 140 us -> 133 us
  waiting for transfers between devices: 25.9 us -> 19.6 us
    all_to_all x4 -> x3, waiting for transfers between devices: 17.1 us -> 1.37 us  [exchanged(): return lax.all_to_all(pieces, axes, split_axis=0, concat_axis=0, tiled=True)]
    ppermute x0 -> x3, starting transfers between devices: none -> 15.3 us  [the longest x2 12.2 us: per_device(): lax.ppermute(leaving, 'z1', [(k, (k + ahead) % Z1) for k in range(Z1)])]
    all_to_all x6 -> x5, blocking collectives: 78.7 us -> 68.3 us  [exchanged(): return lax.all_to_all(pieces, axes, split_axis=0, concat_axis=0, tiled=True)]
    all_to_all x4 -> x3, starting transfers between devices: 20.7 us -> 12.8 us  [exchanged(): return lax.all_to_all(pieces, axes, split_axis=0, concat_axis=0, tiled=True)]
    ppermute x0 -> x3, waiting for transfers between devices: none -> 5.7 us  [the longest x1 4.22 us: per_device(): part += lax.ppermute(leaving, 'z0', [(0, 1), (1, 0)])]
    all_gather x1, blocking collectives: 2.49 us -> 7.29 us  [per_device(): panel = lax.all_gather(panel, 'core', axis=0, tiled=True)]
    ppermute x1, waiting for transfers between devices: 0.01 us -> 3.81 us  [per_device(): kept = lax.ppermute(momentum.T, COLUMN, TO_WORK)]
    ppermute x1, starting transfers between devices: 1.92 us -> 4.41 us  [per_device(): lax.ppermute(leaving[0], NEAR, EVEN_PAIRS)]
  transfers between devices with their start and end apart: 9 -> 11, of which waited for: 6 -> 8; matrix products, arithmetic and copies ran while one was open for 0% -> 0% of each run, Pallas kernels for 0% -> 0%
where the time goes in v8:
time: 225 us; the launch traced here: 224 us
  blocking collectives  133 us (59%)
  starting transfers between devices  59.9 us (27%)
  waiting for transfers between devices  19.6 us (9%)
  local copies, waits for them, and re-layouts  5.82 us (3%)
    all_to_all x5, blocking collectives, exchanged(): return lax.all_to_all(pieces, axes, split_axis=0, concat_axis=0, tiled=True)  68.3 us
    all_gather x1, blocking collectives, per_device(): lax.all_gather(gram, RING, axis=0, tiled=False)  25.6 us
    all_gather x1, blocking collectives, per_device(): halves = lax.all_gather(grad_out, 'zh', axis=0, tiled=False)  14.9 us
    ppermute x1, starting transfers between devices, per_device(): momentum_home = lax.ppermute(new_momentum, COLUMN, TO_HOME)  12.9 us
    all_to_all x3, starting transfers between devices, exchanged(): return lax.all_to_all(pieces, axes, split_axis=0, concat_axis=0, tiled=True)  12.8 us
    ppermute x2, starting transfers between devices, per_device(): lax.ppermute(leaving, 'z1', [(k, (k + ahead) % Z1) for k in range(Z1)])  12.2 us
    all_gather x1, blocking collectives, per_device(): across = lax.all_gather(scaled, 'x', axis=0, tiled=True)  9.24 us
    all_gather x1, blocking collectives, per_device(): second_power = times_gram(lax.all_gather(panel, 'core', axis=0, tiled=True))  8.09 us
  transfers between devices with their start and end apart: 11, of which 8 were waited for; matrix products, arithmetic and copies ran while one was open for 0% of the time, Pallas kernels for 0%

profile of v8, /device:TPU:1, one launch (start us, length us, event | category | flops | bytes accessed | tf_op | source)
XLA Modules:
  0.0 223.8 jit_solution(454613736205092637)
XLA Ops:
  1.4 17.1 %all_to_all.40 = bf16[8,66,256]{2,1,0:T(8,128)(2,1)S(1)} all-to-all(bf16[8,66,256]{2,1,0:T(8,128)(2,1)S(1)} %broadcast_in_dim.8), channel_id=1, replica_groups=mesh['z1'=3,'z0'=2,'core'=2,'zh'=2,'y'=8,'x'=4] {'y'}, dimensions={0} | all-to-all | bytes 540672 | tf_op jit(solution)/shard_map/all_to_all | solution.py:46
  19.7 5.3 %all-to-all-start.1 = ((bf16[4,528,256]{2,1,0:T(8,128)(2,1)}), bf16[4,528,256]{2,1,0:T(8,128)(2,1)S(1)}, u32[]{:S(2)}, u32[]{:S(2)}) async-start(bf16[4,528,256]{2,1,0:T(8,128)(2,1)} %broadcast_in_dim.9), calls=%async_computation.1 | async-start | bytes 2162688 | tf_op jit(solution)/shard_map/all_to_all | solution.py:46
  25.0 14.9 %all-gather = bf16[128,256]{1,0:T(8,128)(2,1)S(1)} all-gather(bf16[64,256]{1,0:T(8,128)(2,1)S(1)} %bitcast.92), channel_id=2, replica_groups=mesh['z1'=3,'z0'=2,'core'=2,'zh'=2,'y'=8,'x'=4] {'zh'}, dimensions={0}, use_global_device_ids=true | all-gather | bytes 98304 | tf_op jit(solution)/shard_map/all_gather | solution.py:71
  41.3 8.1 %all_to_all.41 = f32[2,6,64,352]{3,2,1,0:T(8,128)S(1)} all-to-all(f32[2,6,64,352]{3,2,1,0:T(8,128)S(1)} %copy.38), channel_id=1, replica_groups=mesh['z1'=3,'z0'=2,'core'=2,'zh'=2,'y'=8,'x'=4] {'core'}, dimensions={0} | all-to-all | bytes 2162688 | tf_op jit(solution)/shard_map/all_to_all | solution.py:46
  49.6 3.1 %collective-permute-start.1 = (f32[3,64,352]{2,1,0:T(8,128)S(1)}, f32[3,64,352]{2,1,0:T(8,128)S(1)}, u32[]{:S(2)}, u32[]{:S(2)}) collective-permute-start(f32[3,64,352]{2,1,0:T(8,128)S(1)} %dynamic-slice_bitcast_fusion), channel_id=1, source_target_pairs={{0,128},{128,0},{1,129},{129,1},{2,130},{130,2},{3,131},{131,3},{4... | collective-permute-start | bytes 811016 | tf_op jit(solution)/shard_map/ppermute | solution.py:83
  52.7 2.7 %collective-permute-start = (f32[64,352]{1,0:T(8,128)S(1)}, f32[64,352]{1,0:T(8,128)S(1)}, u32[]{:S(2)}, u32[]{:S(2)}) collective-permute-start(f32[64,352]{1,0:T(8,128)S(1)} %bitcast.93), channel_id=1, source_target_pairs={{0,0},{384,32},{32,64},{416,96},{64,128},{448,160},{96,192},{480,2... | collective-permute-start | bytes 270344 | tf_op jit(solution)/shard_map/ppermute | solution.py:72
  55.5 4.2 %collective-permute-done.1 = f32[3,64,352]{2,1,0:T(8,128)S(1)} collective-permute-done((f32[3,64,352]{2,1,0:T(8,128)S(1)}, f32[3,64,352]{2,1,0:T(8,128)S(1)}, u32[]{:S(2)}, u32[]{:S(2)}) %collective-permute-start.1) | collective-permute-done | bytes 270368 | tf_op jit(solution)/shard_map/ppermute | solution.py:83
  59.8 4.5 %collective-permute-start.2 = (f32[64,352]{1,0:T(8,128)S(1)}, f32[64,352]{1,0:T(8,128)S(1)}, u32[]{:S(2)}, u32[]{:S(2)}) collective-permute-start(f32[64,352]{1,0:T(8,128)S(1)} %get-tuple-element.18), channel_id=1, source_target_pairs={{0,256},{256,512},{512,0},{1,257},{257,513},{513,1},{2,258},{258,5... | collective-permute-start | bytes 270344 | tf_op jit(solution)/shard_map/ppermute | solution.py:88
  64.2 7.8 %collective-permute-start.3 = (f32[64,352]{1,0:T(8,128)S(1)}, f32[64,352]{1,0:T(8,128)S(1)}, u32[]{:S(2)}, u32[]{:S(2)}) collective-permute-start(f32[64,352]{1,0:T(8,128)S(1)} %get-tuple-element.19), channel_id=1, source_target_pairs={{0,512},{256,0},{512,256},{1,513},{257,1},{513,257},{2,514},{258,2... | collective-permute-start | bytes 270344 | tf_op jit(solution)/shard_map/ppermute | solution.py:88
  72.7 3.8 %collective-permute-done = f32[64,352]{1,0:T(8,128)S(1)} collective-permute-done((f32[64,352]{1,0:T(8,128)S(1)}, f32[64,352]{1,0:T(8,128)S(1)}, u32[]{:S(2)}, u32[]{:S(2)}) %collective-permute-start) | collective-permute-done | bytes 90144 | tf_op jit(solution)/shard_map/ppermute | solution.py:72
  78.8 3.5 %all-to-all-start.3 = ((bf16[8,64,352]{2,1,0:T(8,128)(2,1)}), bf16[8,64,352]{2,1,0:T(8,128)(2,1)S(1)}, u32[]{:S(2)}, u32[]{:S(2)}) async-start(bf16[8,64,352]{2,1,0:T(8,128)(2,1)} %broadcast_in_dim.10), calls=%async_computation.3 | async-start | bytes 786432 | tf_op jit(solution)/shard_map/all_to_all | solution.py:46
  82.2 9.2 %all_gather.21 = bf16[256,352]{1,0:T(8,128)(2,1)S(1)} all-gather(bf16[64,352]{1,0:T(8,128)(2,1)S(1)} %get-tuple-element.14), channel_id=1, replica_groups=mesh['z1'=3,'z0'=2,'core'=2,'zh'=2,'y'=8,'x'=4] {'x'}, dimensions={0}, use_global_device_ids=true | all-gather | bytes 225280 | tf_op jit(solution)/shard_map/all_gather | solution.py:94
  92.8 7.3 %all_gather.22 = bf16[1024,352]{1,0:T(8,128)(2,1)S(1)} all-gather(bf16[512,352]{1,0:T(8,128)(2,1)S(1)} %bitcast.85), channel_id=1, replica_groups=mesh['z1'=3,'z0'=2,'core'=2,'zh'=2,'y'=8,'x'=4] {'core'}, dimensions={0}, use_global_device_ids=true | all-gather | bytes 1081344 | tf_op jit(solution)/shard_map/all_gather | solution.py:96
  101.1 4.4 %collective-permute-start.4 = (f32[528,128]{1,0:T(8,128)S(1)}, f32[528,128]{1,0:T(8,128)S(1)}, u32[]{:S(2)}, u32[]{:S(2)}) collective-permute-start(f32[528,128]{1,0:T(8,128)S(1)} %get-tuple-element.16), channel_id=1, source_target_pairs={{0,128},{128,0},{256,384},{384,256},{512,640},{640,512},{32,160},{... | collective-permute-start | bytes 811016 | tf_op jit(solution)/shard_map/ppermute | solution.py:107
  105.5 6.0 %collective-permute-start.5 = (f32[528,128]{1,0:T(8,128)S(1)}, f32[528,128]{1,0:T(8,128)S(1)}, u32[]{:S(2)}, u32[]{:S(2)}) collective-permute-start(f32[528,128]{1,0:T(8,128)S(1)} %get-tuple-element.17), channel_id=1, source_target_pairs={{0,672},{128,256},{256,128},{384,512},{512,384},{640,32},{32,640},... | collective-permute-start | bytes 811016 | tf_op jit(solution)/shard_map/ppermute | solution.py:107
  112.0 5.7 %collective-permute-done.5 = f32[528,128]{1,0:T(8,128)S(1)} collective-permute-done((f32[528,128]{1,0:T(8,128)S(1)}, f32[528,128]{1,0:T(8,128)S(1)}, u32[]{:S(2)}, u32[]{:S(2)}) %collective-permute-start.5) | collective-permute-done | bytes 270368 | tf_op jit(solution)/shard_map/ppermute | solution.py:107
  117.8 24.0 %all_to_all.42 = f32[6,2,88,128]{3,2,1,0:T(8,128)S(1)} all-to-all(f32[6,2,88,128]{3,2,1,0:T(8,128)S(1)} %copy.43), channel_id=1, replica_groups=mesh['z1'=3,'z0'=2,'core'=2,'zh'=2,'y'=8,'x'=4] {'z1','zh'}, dimensions={0} | all-to-all | bytes 1081344 | tf_op jit(solution)/shard_map/all_to_all | solution.py:46
  141.9 25.6 %all-gather.1 = bf16[24,88,128]{2,1,0:T(8,128)(2,1)S(1)} all-gather(bf16[2,88,128]{2,1,0:T(8,128)(2,1)S(1)} %reduce_sum.37), channel_id=3, replica_groups=mesh['z1'=3,'z0'=2,'core'=2,'zh'=2,'y'=8,'x'=4] {'zh','z1','z0'}, dimensions={0}, use_global_device_ids=true | all-gather | bytes 585728 | tf_op jit(solution)/shard_map/all_gather | solution.py:111
  168.2 8.6 %all_to_all.43 = f32[4,64,352]{2,1,0:T(8,128)S(1)} all-to-all(f32[4,64,352]{2,1,0:T(8,128)S(1)} %fusion.3), channel_id=1, replica_groups=mesh['z1'=3,'z0'=2,'core'=2,'zh'=2,'y'=8,'x'=4] {'x'}, dimensions={0} | all-to-all | bytes 720896 | tf_op jit(solution)/shard_map/all_to_all | solution.py:46
  177.6 4.0 %all-to-all-start.6 = ((bf16[8,64,352]{2,1,0:T(8,128)(2,1)}), bf16[8,64,352]{2,1,0:T(8,128)(2,1)S(1)}, u32[]{:S(2)}, u32[]{:S(2)}) async-start(bf16[8,64,352]{2,1,0:T(8,128)(2,1)} %broadcast_in_dim.11), calls=%async_computation.6 | async-start | bytes 786432 | tf_op jit(solution)/shard_map/all_to_all | solution.py:46
  181.7 12.9 %collective-permute-start.6 = (f32[64,352]{1,0:T(8,128)S(1)}, f32[64,352]{1,0:T(8,128)S(1)}, u32[]{:S(2)}, u32[]{:S(2)}) collective-permute-start(f32[64,352]{1,0:T(8,128)S(1)} %get-tuple-element.15), channel_id=1, source_target_pairs={{0,0},{32,384},{64,32},{96,416},{128,64},{160,448},{192,96},{224,4... | collective-permute-start | bytes 270344 | tf_op jit(solution)/shard_map/ppermute | solution.py:92
  196.2 8.1 %all_gather.24 = bf16[1024,352]{1,0:T(8,128)(2,1)S(1)} all-gather(bf16[512,352]{1,0:T(8,128)(2,1)S(1)} %bitcast.84), channel_id=1, replica_groups=mesh['z1'=3,'z0'=2,'core'=2,'zh'=2,'y'=8,'x'=4] {'core'}, dimensions={0}, use_global_device_ids=true | all-gather | bytes 1081344 | tf_op jit(solution)/shard_map/all_gather | solution.py:121
  204.8 10.3 %all_to_all.44 = f32[4,64,352]{2,1,0:T(8,128)S(1)} all-to-all(f32[4,64,352]{2,1,0:T(8,128)S(1)} %fusion.1), channel_id=1, replica_groups=mesh['z1'=3,'z0'=2,'core'=2,'zh'=2,'y'=8,'x'=4] {'x'}, dimensions={0} | all-to-all | bytes 720896 | tf_op jit(solution)/shard_map/all_to_all | solution.py:46
  215.2 5.7 %collective-permute-start.7 = (f32[64,352]{1,0:T(8,128)S(1)}, f32[64,352]{1,0:T(8,128)S(1)}, u32[]{:S(2)}, u32[]{:S(2)}) collective-permute-start(f32[64,352]{1,0:T(8,128)S(1)} %multiply_add_fusion), channel_id=1, source_target_pairs={{0,0},{32,384},{64,32},{96,416},{128,64},{160,448},{192,96},{224,4... | collective-permute-start | bytes 270344 | tf_op jit(solution)/shard_map/ppermute | solution.py:127
  (47 shorter events, 14.6 us)
Async XLA Ops:
  19.7 5.3 %copy-start.1 = (bf16[256,64]{0,1:T(8,128)(2,1)S(1)}, bf16[256,64]{0,1:T(8,128)(2,1)}, u32[]{:S(2)}) copy-start(bf16[256,64]{0,1:T(8,128)(2,1)} %param.7) | copy-start | bytes 98308
  19.7 20.2 %all-to-all-start.1 = ((bf16[4,528,256]{2,1,0:T(8,128)(2,1)}), bf16[4,528,256]{2,1,0:T(8,128)(2,1)S(1)}, u32[]{:S(2)}, u32[]{:S(2)}) async-start(bf16[4,528,256]{2,1,0:T(8,128)(2,1)} %broadcast_in_dim.9), calls=%async_computation.1 | async-start | bytes 2162688 | tf_op jit(solution)/shard_map/all_to_all | solution.py:46
  49.4 3.3 %copy-start.2 = (f32[352,64]{0,1:T(8,128)S(1)}, f32[352,64]{0,1:T(8,128)}, u32[]{:S(2)}) copy-start(f32[352,64]{0,1:T(8,128)} %param.8) | copy-start | bytes 270340
  49.6 10.1 %collective-permute-start.1 = (f32[3,64,352]{2,1,0:T(8,128)S(1)}, f32[3,64,352]{2,1,0:T(8,128)S(1)}, u32[]{:S(2)}, u32[]{:S(2)}) collective-permute-start(f32[3,64,352]{2,1,0:T(8,128)S(1)} %dynamic-slice_bitcast_fusion), channel_id=1, source_target_pairs={{0,128},{128,0},{1,129},{129,1},{2,130},{130,2},{3,131},{131,3},{4... | collective-permute-start | bytes 811016 | tf_op jit(solution)/shard_map/ppermute | solution.py:83
  52.7 23.8 %collective-permute-start = (f32[64,352]{1,0:T(8,128)S(1)}, f32[64,352]{1,0:T(8,128)S(1)}, u32[]{:S(2)}, u32[]{:S(2)}) collective-permute-start(f32[64,352]{1,0:T(8,128)S(1)} %bitcast.93), channel_id=1, source_target_pairs={{0,0},{384,32},{32,64},{416,96},{64,128},{448,160},{96,192},{480,2... | collective-permute-start | bytes 270344 | tf_op jit(solution)/shard_map/ppermute | solution.py:72
  59.8 18.2 %collective-permute-start.2 = (f32[64,352]{1,0:T(8,128)S(1)}, f32[64,352]{1,0:T(8,128)S(1)}, u32[]{:S(2)}, u32[]{:S(2)}) collective-permute-start(f32[64,352]{1,0:T(8,128)S(1)} %get-tuple-element.18), channel_id=1, source_target_pairs={{0,256},{256,512},{512,0},{1,257},{257,513},{513,1},{2,258},{258,5... | collective-permute-start | bytes 270344 | tf_op jit(solution)/shard_map/ppermute | solution.py:88
  64.2 13.7 %collective-permute-start.3 = (f32[64,352]{1,0:T(8,128)S(1)}, f32[64,352]{1,0:T(8,128)S(1)}, u32[]{:S(2)}, u32[]{:S(2)}) collective-permute-start(f32[64,352]{1,0:T(8,128)S(1)} %get-tuple-element.19), channel_id=1, source_target_pairs={{0,512},{256,0},{512,256},{1,513},{257,1},{513,257},{2,514},{258,2... | collective-permute-start | bytes 270344 | tf_op jit(solution)/shard_map/ppermute | solution.py:88
  78.8 14.1 %all-to-all-start.3 = ((bf16[8,64,352]{2,1,0:T(8,128)(2,1)}), bf16[8,64,352]{2,1,0:T(8,128)(2,1)S(1)}, u32[]{:S(2)}, u32[]{:S(2)}) async-start(bf16[8,64,352]{2,1,0:T(8,128)(2,1)} %broadcast_in_dim.10), calls=%async_computation.3 | async-start | bytes 786432 | tf_op jit(solution)/shard_map/all_to_all | solution.py:46
  101.1 11.0 %collective-permute-start.4 = (f32[528,128]{1,0:T(8,128)S(1)}, f32[528,128]{1,0:T(8,128)S(1)}, u32[]{:S(2)}, u32[]{:S(2)}) collective-permute-start(f32[528,128]{1,0:T(8,128)S(1)} %get-tuple-element.16), channel_id=1, source_target_pairs={{0,128},{128,0},{256,384},{384,256},{512,640},{640,512},{32,160},{... | collective-permute-start | bytes 811016 | tf_op jit(solution)/shard_map/ppermute | solution.py:107
  105.5 12.2 %collective-permute-start.5 = (f32[528,128]{1,0:T(8,128)S(1)}, f32[528,128]{1,0:T(8,128)S(1)}, u32[]{:S(2)}, u32[]{:S(2)}) collective-permute-start(f32[528,128]{1,0:T(8,128)S(1)} %get-tuple-element.17), channel_id=1, source_target_pairs={{0,672},{128,256},{256,128},{384,512},{512,384},{640,32},{32,640},... | collective-permute-start | bytes 811016 | tf_op jit(solution)/shard_map/ppermute | solution.py:107
  177.6 18.6 %all-to-all-start.6 = ((bf16[8,64,352]{2,1,0:T(8,128)(2,1)}), bf16[8,64,352]{2,1,0:T(8,128)(2,1)S(1)}, u32[]{:S(2)}, u32[]{:S(2)}) async-start(bf16[8,64,352]{2,1,0:T(8,128)(2,1)} %broadcast_in_dim.11), calls=%async_computation.6 | async-start | bytes 786432 | tf_op jit(solution)/shard_map/all_to_all | solution.py:46
  181.7 14.5 %collective-permute-start.6 = (f32[64,352]{1,0:T(8,128)S(1)}, f32[64,352]{1,0:T(8,128)S(1)}, u32[]{:S(2)}, u32[]{:S(2)}) collective-permute-start(f32[64,352]{1,0:T(8,128)S(1)} %get-tuple-element.15), channel_id=1, source_target_pairs={{0,0},{32,384},{64,32},{96,416},{128,64},{160,448},{192,96},{224,4... | collective-permute-start | bytes 270344 | tf_op jit(solution)/shard_map/ppermute | solution.py:92
  204.8 17.8 %copy-start = (f32[352,64]{0,1:T(8,128)S(1)}, f32[352,64]{0,1:T(8,128)}, u32[]{:S(2)}) copy-start(f32[352,64]{0,1:T(8,128)} %param.9) | copy-start | bytes 270340
  215.2 7.3 %collective-permute-start.7 = (f32[64,352]{1,0:T(8,128)S(1)}, f32[64,352]{1,0:T(8,128)S(1)}, u32[]{:S(2)}, u32[]{:S(2)}) collective-permute-start(f32[64,352]{1,0:T(8,128)S(1)} %multiply_add_fusion), channel_id=1, source_target_pairs={{0,0},{32,384},{64,32},{96,416},{128,64},{160,448},{192,96},{224,4... | collective-permute-start | bytes 270344 | tf_op jit(solution)/shard_map/ppermute | solution.py:127

commit v9 on v8

--- a/solution.py
+++ b/solution.py
@@ -103,10 +103,9 @@
     part = part.reshape(2, Z0, Z // Z0 * piece, 2 * width)
     leaving = lax.dynamic_index_in_dim(part, 1 - odd, 1, False)
     staying = lax.dynamic_index_in_dim(part, odd, 1, False)
-    came = jnp.stack(
-        [lax.ppermute(leaving[0], NEAR, EVEN_PAIRS), lax.ppermute(leaving[1], NEAR, ODD_PAIRS)]
-    )
-    part = (staying + came).reshape(2, Z // Z0, piece, 2 * width).transpose(1, 0, 2, 3)
+    came = (lax.ppermute(leaving[0], NEAR, EVEN_PAIRS), lax.ppermute(leaving[1], NEAR, ODD_PAIRS))
+    shape = (Z // Z0, 1, piece, 2 * width)
+    part = jnp.concatenate([(staying[k] + came[k]).reshape(shape) for k in range(2)], axis=1)
     gram = exchanged(part, ("z1", "zh")).sum(axis=0).astype(jnp.bfloat16)
     gram = lax.all_gather(gram, RING, axis=0, tiled=False).reshape(ZH, Z1, Z0, 2, piece, 2 * width)
     gram = gram.transpose(3, 2, 1, 0, 4, 5).reshape(-1, 2 * width)[:depth]

time: 225 us -> 225 us (level)
  no operation moved by 1% of the time
where the time goes in v9:
time: 225 us; the launch traced here: 224 us
  blocking collectives  133 us (59%)
  starting transfers between devices  59.9 us (27%)
  waiting for transfers between devices  19.7 us (9%)
  local copies, waits for them, and re-layouts  5.72 us (3%)
    all_to_all x5, blocking collectives, exchanged(): return lax.all_to_all(pieces, axes, split_axis=0, concat_axis=0, tiled=True)  68.3 us
    all_gather x1, blocking collectives, per_device(): lax.all_gather(gram, RING, axis=0, tiled=False)  25.6 us
    all_gather x1, blocking collectives, per_device(): halves = lax.all_gather(grad_out, 'zh', axis=0, tiled=False)  14.9 us
    ppermute x1, starting transfers between devices, per_device(): momentum_home = lax.ppermute(new_momentum, COLUMN, TO_HOME)  12.9 us
    all_to_all x3, starting transfers between devices, exchanged(): return lax.all_to_all(pieces, axes, split_axis=0, concat_axis=0, tiled=True)  12.8 us
    ppermute x2, starting transfers between devices, per_device(): lax.ppermute(leaving, 'z1', [(k, (k + ahead) % Z1) for k in range(Z1)])  12.2 us
    all_gather x1, blocking collectives, per_device(): across = lax.all_gather(scaled, 'x', axis=0, tiled=True)  9.24 us
    all_gather x1, blocking collectives, per_device(): second_power = times_gram(lax.all_gather(panel, 'core', axis=0, tiled=True))  8.09 us
  transfers between devices with their start and end apart: 11, of which 8 were waited for; matrix products, arithmetic and copies ran while one was open for 0% of the time, Pallas kernels for 0%

profile of v9, /device:TPU:1, one launch (start us, length us, event | category | flops | bytes accessed | tf_op | source)
XLA Modules:
  0.0 223.8 jit_solution(3302178562422667549)
XLA Ops:
  1.4 17.1 %all_to_all.40 = bf16[8,66,256]{2,1,0:T(8,128)(2,1)S(1)} all-to-all(bf16[8,66,256]{2,1,0:T(8,128)(2,1)S(1)} %broadcast_in_dim.8), channel_id=1, replica_groups=mesh['z1'=3,'z0'=2,'core'=2,'zh'=2,'y'=8,'x'=4] {'y'}, dimensions={0} | all-to-all | bytes 540672 | tf_op jit(solution)/shard_map/all_to_all | solution.py:46
  19.7 5.3 %all-to-all-start.1 = ((bf16[4,528,256]{2,1,0:T(8,128)(2,1)}), bf16[4,528,256]{2,1,0:T(8,128)(2,1)S(1)}, u32[]{:S(2)}, u32[]{:S(2)}) async-start(bf16[4,528,256]{2,1,0:T(8,128)(2,1)} %broadcast_in_dim.9), calls=%async_computation.1 | async-start | bytes 2162688 | tf_op jit(solution)/shard_map/all_to_all | solution.py:46
  25.0 14.9 %all-gather = bf16[128,256]{1,0:T(8,128)(2,1)S(1)} all-gather(bf16[64,256]{1,0:T(8,128)(2,1)S(1)} %bitcast.94), channel_id=2, replica_groups=mesh['z1'=3,'z0'=2,'core'=2,'zh'=2,'y'=8,'x'=4] {'zh'}, dimensions={0}, use_global_device_ids=true | all-gather | bytes 98304 | tf_op jit(solution)/shard_map/all_gather | solution.py:71
  41.3 8.1 %all_to_all.41 = f32[2,6,64,352]{3,2,1,0:T(8,128)S(1)} all-to-all(f32[2,6,64,352]{3,2,1,0:T(8,128)S(1)} %copy.29), channel_id=1, replica_groups=mesh['z1'=3,'z0'=2,'core'=2,'zh'=2,'y'=8,'x'=4] {'core'}, dimensions={0} | all-to-all | bytes 2162688 | tf_op jit(solution)/shard_map/all_to_all | solution.py:46
  49.6 3.1 %collective-permute-start.1 = (f32[3,64,352]{2,1,0:T(8,128)S(1)}, f32[3,64,352]{2,1,0:T(8,128)S(1)}, u32[]{:S(2)}, u32[]{:S(2)}) collective-permute-start(f32[3,64,352]{2,1,0:T(8,128)S(1)} %dynamic-slice_bitcast_fusion), channel_id=1, source_target_pairs={{0,128},{128,0},{1,129},{129,1},{2,130},{130,2},{3,131},{131,3},{4... | collective-permute-start | bytes 811016 | tf_op jit(solution)/shard_map/ppermute | solution.py:83
  52.7 2.7 %collective-permute-start = (f32[64,352]{1,0:T(8,128)S(1)}, f32[64,352]{1,0:T(8,128)S(1)}, u32[]{:S(2)}, u32[]{:S(2)}) collective-permute-start(f32[64,352]{1,0:T(8,128)S(1)} %bitcast.95), channel_id=1, source_target_pairs={{0,0},{384,32},{32,64},{416,96},{64,128},{448,160},{96,192},{480,2... | collective-permute-start | bytes 270344 | tf_op jit(solution)/shard_map/ppermute | solution.py:72
  55.5 4.2 %collective-permute-done.1 = f32[3,64,352]{2,1,0:T(8,128)S(1)} collective-permute-done((f32[3,64,352]{2,1,0:T(8,128)S(1)}, f32[3,64,352]{2,1,0:T(8,128)S(1)}, u32[]{:S(2)}, u32[]{:S(2)}) %collective-permute-start.1) | collective-permute-done | bytes 270368 | tf_op jit(solution)/shard_map/ppermute | solution.py:83
  59.8 4.5 %collective-permute-start.2 = (f32[64,352]{1,0:T(8,128)S(1)}, f32[64,352]{1,0:T(8,128)S(1)}, u32[]{:S(2)}, u32[]{:S(2)}) collective-permute-start(f32[64,352]{1,0:T(8,128)S(1)} %get-tuple-element.20), channel_id=1, source_target_pairs={{0,256},{256,512},{512,0},{1,257},{257,513},{513,1},{2,258},{258,5... | collective-permute-start | bytes 270344 | tf_op jit(solution)/shard_map/ppermute | solution.py:88
  64.2 7.8 %collective-permute-start.3 = (f32[64,352]{1,0:T(8,128)S(1)}, f32[64,352]{1,0:T(8,128)S(1)}, u32[]{:S(2)}, u32[]{:S(2)}) collective-permute-start(f32[64,352]{1,0:T(8,128)S(1)} %get-tuple-element.21), channel_id=1, source_target_pairs={{0,512},{256,0},{512,256},{1,513},{257,1},{513,257},{2,514},{258,2... | collective-permute-start | bytes 270344 | tf_op jit(solution)/shard_map/ppermute | solution.py:88
  72.7 3.8 %collective-permute-done = f32[64,352]{1,0:T(8,128)S(1)} collective-permute-done((f32[64,352]{1,0:T(8,128)S(1)}, f32[64,352]{1,0:T(8,128)S(1)}, u32[]{:S(2)}, u32[]{:S(2)}) %collective-permute-start) | collective-permute-done | bytes 90144 | tf_op jit(solution)/shard_map/ppermute | solution.py:72
  78.7 3.5 %all-to-all-start.3 = ((bf16[8,64,352]{2,1,0:T(8,128)(2,1)}), bf16[8,64,352]{2,1,0:T(8,128)(2,1)S(1)}, u32[]{:S(2)}, u32[]{:S(2)}) async-start(bf16[8,64,352]{2,1,0:T(8,128)(2,1)} %broadcast_in_dim.10), calls=%async_computation.3 | async-start | bytes 786432 | tf_op jit(solution)/shard_map/all_to_all | solution.py:46
  82.2 9.2 %all_gather.21 = bf16[256,352]{1,0:T(8,128)(2,1)S(1)} all-gather(bf16[64,352]{1,0:T(8,128)(2,1)S(1)} %get-tuple-element.14), channel_id=1, replica_groups=mesh['z1'=3,'z0'=2,'core'=2,'zh'=2,'y'=8,'x'=4] {'x'}, dimensions={0}, use_global_device_ids=true | all-gather | bytes 225280 | tf_op jit(solution)/shard_map/all_gather | solution.py:94
  92.8 7.3 %all_gather.22 = bf16[1024,352]{1,0:T(8,128)(2,1)S(1)} all-gather(bf16[512,352]{1,0:T(8,128)(2,1)S(1)} %bitcast.87), channel_id=1, replica_groups=mesh['z1'=3,'z0'=2,'core'=2,'zh'=2,'y'=8,'x'=4] {'core'}, dimensions={0}, use_global_device_ids=true | all-gather | bytes 1081344 | tf_op jit(solution)/shard_map/all_gather | solution.py:96
  101.0 4.4 %collective-permute-start.4 = (f32[528,128]{1,0:T(8,128)S(1)}, f32[528,128]{1,0:T(8,128)S(1)}, u32[]{:S(2)}, u32[]{:S(2)}) collective-permute-start(f32[528,128]{1,0:T(8,128)S(1)} %get-tuple-element.18), channel_id=1, source_target_pairs={{0,128},{128,0},{256,384},{384,256},{512,640},{640,512},{32,160},{... | collective-permute-start | bytes 811016 | tf_op jit(solution)/shard_map/ppermute | solution.py:106
  105.5 6.0 %collective-permute-start.5 = (f32[528,128]{1,0:T(8,128)S(1)}, f32[528,128]{1,0:T(8,128)S(1)}, u32[]{:S(2)}, u32[]{:S(2)}) collective-permute-start(f32[528,128]{1,0:T(8,128)S(1)} %get-tuple-element.19), channel_id=1, source_target_pairs={{0,672},{128,256},{256,128},{384,512},{512,384},{640,32},{32,640},... | collective-permute-start | bytes 811016 | tf_op jit(solution)/shard_map/ppermute | solution.py:106
  112.0 5.7 %collective-permute-done.5 = f32[528,128]{1,0:T(8,128)S(1)} collective-permute-done((f32[528,128]{1,0:T(8,128)S(1)}, f32[528,128]{1,0:T(8,128)S(1)}, u32[]{:S(2)}, u32[]{:S(2)}) %collective-permute-start.5) | collective-permute-done | bytes 270368 | tf_op jit(solution)/shard_map/ppermute | solution.py:106
  117.8 24.0 %all_to_all.42 = f32[6,2,88,128]{3,2,1,0:T(8,128)S(1)} all-to-all(f32[6,2,88,128]{3,2,1,0:T(8,128)S(1)} %pad_maximum_fusion), channel_id=1, replica_groups=mesh['z1'=3,'z0'=2,'core'=2,'zh'=2,'y'=8,'x'=4] {'z1','zh'}, dimensions={0} | all-to-all | bytes 1081344 | tf_op jit(solution)/shard_map/all_to_all | solution.py:46
  141.9 25.6 %all-gather.1 = bf16[24,88,128]{2,1,0:T(8,128)(2,1)S(1)} all-gather(bf16[2,88,128]{2,1,0:T(8,128)(2,1)S(1)} %reduce_sum.37), channel_id=3, replica_groups=mesh['z1'=3,'z0'=2,'core'=2,'zh'=2,'y'=8,'x'=4] {'zh','z1','z0'}, dimensions={0}, use_global_device_ids=true | all-gather | bytes 585728 | tf_op jit(solution)/shard_map/all_gather | solution.py:110
  168.2 8.6 %all_to_all.43 = f32[4,64,352]{2,1,0:T(8,128)S(1)} all-to-all(f32[4,64,352]{2,1,0:T(8,128)S(1)} %fusion.3), channel_id=1, replica_groups=mesh['z1'=3,'z0'=2,'core'=2,'zh'=2,'y'=8,'x'=4] {'x'}, dimensions={0} | all-to-all | bytes 720896 | tf_op jit(solution)/shard_map/all_to_all | solution.py:46
  177.6 4.0 %all-to-all-start.6 = ((bf16[8,64,352]{2,1,0:T(8,128)(2,1)}), bf16[8,64,352]{2,1,0:T(8,128)(2,1)S(1)}, u32[]{:S(2)}, u32[]{:S(2)}) async-start(bf16[8,64,352]{2,1,0:T(8,128)(2,1)} %broadcast_in_dim.11), calls=%async_computation.6 | async-start | bytes 786432 | tf_op jit(solution)/shard_map/all_to_all | solution.py:46
  181.7 12.9 %collective-permute-start.6 = (f32[64,352]{1,0:T(8,128)S(1)}, f32[64,352]{1,0:T(8,128)S(1)}, u32[]{:S(2)}, u32[]{:S(2)}) collective-permute-start(f32[64,352]{1,0:T(8,128)S(1)} %get-tuple-element.15), channel_id=1, source_target_pairs={{0,0},{32,384},{64,32},{96,416},{128,64},{160,448},{192,96},{224,4... | collective-permute-start | bytes 270344 | tf_op jit(solution)/shard_map/ppermute | solution.py:92
  196.2 8.1 %all_gather.24 = bf16[1024,352]{1,0:T(8,128)(2,1)S(1)} all-gather(bf16[512,352]{1,0:T(8,128)(2,1)S(1)} %bitcast.86), channel_id=1, replica_groups=mesh['z1'=3,'z0'=2,'core'=2,'zh'=2,'y'=8,'x'=4] {'core'}, dimensions={0}, use_global_device_ids=true | all-gather | bytes 1081344 | tf_op jit(solution)/shard_map/all_gather | solution.py:120
  204.8 10.3 %all_to_all.44 = f32[4,64,352]{2,1,0:T(8,128)S(1)} all-to-all(f32[4,64,352]{2,1,0:T(8,128)S(1)} %fusion.1), channel_id=1, replica_groups=mesh['z1'=3,'z0'=2,'core'=2,'zh'=2,'y'=8,'x'=4] {'x'}, dimensions={0} | all-to-all | bytes 720896 | tf_op jit(solution)/shard_map/all_to_all | solution.py:46
  215.2 5.7 %collective-permute-start.7 = (f32[64,352]{1,0:T(8,128)S(1)}, f32[64,352]{1,0:T(8,128)S(1)}, u32[]{:S(2)}, u32[]{:S(2)}) collective-permute-start(f32[64,352]{1,0:T(8,128)S(1)} %multiply_add_fusion), channel_id=1, source_target_pairs={{0,0},{32,384},{64,32},{96,416},{128,64},{160,448},{192,96},{224,4... | collective-permute-start | bytes 270344 | tf_op jit(solution)/shard_map/ppermute | solution.py:126
  (46 shorter events, 14.6 us)
Async XLA Ops:
  19.7 5.3 %copy-start.1 = (bf16[256,64]{0,1:T(8,128)(2,1)S(1)}, bf16[256,64]{0,1:T(8,128)(2,1)}, u32[]{:S(2)}) copy-start(bf16[256,64]{0,1:T(8,128)(2,1)} %param.7) | copy-start | bytes 98308
  19.7 20.2 %all-to-all-start.1 = ((bf16[4,528,256]{2,1,0:T(8,128)(2,1)}), bf16[4,528,256]{2,1,0:T(8,128)(2,1)S(1)}, u32[]{:S(2)}, u32[]{:S(2)}) async-start(bf16[4,528,256]{2,1,0:T(8,128)(2,1)} %broadcast_in_dim.9), calls=%async_computation.1 | async-start | bytes 2162688 | tf_op jit(solution)/shard_map/all_to_all | solution.py:46
  49.4 3.3 %copy-start.2 = (f32[352,64]{0,1:T(8,128)S(1)}, f32[352,64]{0,1:T(8,128)}, u32[]{:S(2)}) copy-start(f32[352,64]{0,1:T(8,128)} %param.8) | copy-start | bytes 270340
  49.6 10.1 %collective-permute-start.1 = (f32[3,64,352]{2,1,0:T(8,128)S(1)}, f32[3,64,352]{2,1,0:T(8,128)S(1)}, u32[]{:S(2)}, u32[]{:S(2)}) collective-permute-start(f32[3,64,352]{2,1,0:T(8,128)S(1)} %dynamic-slice_bitcast_fusion), channel_id=1, source_target_pairs={{0,128},{128,0},{1,129},{129,1},{2,130},{130,2},{3,131},{131,3},{4... | collective-permute-start | bytes 811016 | tf_op jit(solution)/shard_map/ppermute | solution.py:83
  52.7 23.8 %collective-permute-start = (f32[64,352]{1,0:T(8,128)S(1)}, f32[64,352]{1,0:T(8,128)S(1)}, u32[]{:S(2)}, u32[]{:S(2)}) collective-permute-start(f32[64,352]{1,0:T(8,128)S(1)} %bitcast.95), channel_id=1, source_target_pairs={{0,0},{384,32},{32,64},{416,96},{64,128},{448,160},{96,192},{480,2... | collective-permute-start | bytes 270344 | tf_op jit(solution)/shard_map/ppermute | solution.py:72
  59.8 18.2 %collective-permute-start.2 = (f32[64,352]{1,0:T(8,128)S(1)}, f32[64,352]{1,0:T(8,128)S(1)}, u32[]{:S(2)}, u32[]{:S(2)}) collective-permute-start(f32[64,352]{1,0:T(8,128)S(1)} %get-tuple-element.20), channel_id=1, source_target_pairs={{0,256},{256,512},{512,0},{1,257},{257,513},{513,1},{2,258},{258,5... | collective-permute-start | bytes 270344 | tf_op jit(solution)/shard_map/ppermute | solution.py:88
  64.2 13.7 %collective-permute-start.3 = (f32[64,352]{1,0:T(8,128)S(1)}, f32[64,352]{1,0:T(8,128)S(1)}, u32[]{:S(2)}, u32[]{:S(2)}) collective-permute-start(f32[64,352]{1,0:T(8,128)S(1)} %get-tuple-element.21), channel_id=1, source_target_pairs={{0,512},{256,0},{512,256},{1,513},{257,1},{513,257},{2,514},{258,2... | collective-permute-start | bytes 270344 | tf_op jit(solution)/shard_map/ppermute | solution.py:88
  78.7 14.1 %all-to-all-start.3 = ((bf16[8,64,352]{2,1,0:T(8,128)(2,1)}), bf16[8,64,352]{2,1,0:T(8,128)(2,1)S(1)}, u32[]{:S(2)}, u32[]{:S(2)}) async-start(bf16[8,64,352]{2,1,0:T(8,128)(2,1)} %broadcast_in_dim.10), calls=%async_computation.3 | async-start | bytes 786432 | tf_op jit(solution)/shard_map/all_to_all | solution.py:46
  101.0 11.0 %collective-permute-start.4 = (f32[528,128]{1,0:T(8,128)S(1)}, f32[528,128]{1,0:T(8,128)S(1)}, u32[]{:S(2)}, u32[]{:S(2)}) collective-permute-start(f32[528,128]{1,0:T(8,128)S(1)} %get-tuple-element.18), channel_id=1, source_target_pairs={{0,128},{128,0},{256,384},{384,256},{512,640},{640,512},{32,160},{... | collective-permute-start | bytes 811016 | tf_op jit(solution)/shard_map/ppermute | solution.py:106
  105.5 12.2 %collective-permute-start.5 = (f32[528,128]{1,0:T(8,128)S(1)}, f32[528,128]{1,0:T(8,128)S(1)}, u32[]{:S(2)}, u32[]{:S(2)}) collective-permute-start(f32[528,128]{1,0:T(8,128)S(1)} %get-tuple-element.19), channel_id=1, source_target_pairs={{0,672},{128,256},{256,128},{384,512},{512,384},{640,32},{32,640},... | collective-permute-start | bytes 811016 | tf_op jit(solution)/shard_map/ppermute | solution.py:106
  177.6 18.6 %all-to-all-start.6 = ((bf16[8,64,352]{2,1,0:T(8,128)(2,1)}), bf16[8,64,352]{2,1,0:T(8,128)(2,1)S(1)}, u32[]{:S(2)}, u32[]{:S(2)}) async-start(bf16[8,64,352]{2,1,0:T(8,128)(2,1)} %broadcast_in_dim.11), calls=%async_computation.6 | async-start | bytes 786432 | tf_op jit(solution)/shard_map/all_to_all | solution.py:46
  181.7 14.5 %collective-permute-start.6 = (f32[64,352]{1,0:T(8,128)S(1)}, f32[64,352]{1,0:T(8,128)S(1)}, u32[]{:S(2)}, u32[]{:S(2)}) collective-permute-start(f32[64,352]{1,0:T(8,128)S(1)} %get-tuple-element.15), channel_id=1, source_target_pairs={{0,0},{32,384},{64,32},{96,416},{128,64},{160,448},{192,96},{224,4... | collective-permute-start | bytes 270344 | tf_op jit(solution)/shard_map/ppermute | solution.py:92
  204.7 17.8 %copy-start = (f32[352,64]{0,1:T(8,128)S(1)}, f32[352,64]{0,1:T(8,128)}, u32[]{:S(2)}) copy-start(f32[352,64]{0,1:T(8,128)} %param.9) | copy-start | bytes 270340
  215.2 7.3 %collective-permute-start.7 = (f32[64,352]{1,0:T(8,128)S(1)}, f32[64,352]{1,0:T(8,128)S(1)}, u32[]{:S(2)}, u32[]{:S(2)}) collective-permute-start(f32[64,352]{1,0:T(8,128)S(1)} %multiply_add_fusion), channel_id=1, source_target_pairs={{0,0},{32,384},{64,32},{96,416},{128,64},{160,448},{192,96},{224,4... | collective-permute-start | bytes 270344 | tf_op jit(solution)/shard_map/ppermute | solution.py:126
